TPU v7x, 256 devices: a whole 4x4x8 slice. The times are simulated.
256 devices in a mesh: tok: 4 (over x), vocab: 64 (over y, z, core).
Axes of the slice: x: 4, y: 4, z: 8, core: 2. Of those that a mesh axis runs over, the one named last changes fastest.
Arguments:
- hidden: bfloat16 [512, 4608], P('tok', 'vocab'), may hold values from -6 to 6
- weight: bfloat16 [131072, 4608], P(('tok', 'vocab')), may hold values from -0.75 to 0.75
- targets: int32 [512], P('tok'), may hold values from 0 to 131071
Outputs:
- loss: float32 [512], P('tok')
- grad_hidden: bfloat16 [512, 4608], P('tok', 'vocab')
- grad_weight: bfloat16 [131072, 4608], P(('tok', 'vocab'))
All inputs are finite; a program needn't handle non-finite values.
Results may differ from a plain program's by a relative error of at most 0.0038.
Values may be sent and summed in bfloat16 or wider, within the bound.
No kernel may reach another device: no remote copies, remote signals or barrier semaphores. Data moves between devices by JAX's collectives and lax.ppermute only.
A program may use at most 64 MiB of HBM per device.

v0:
```python
import jax
import jax.numpy as jnp
from jax import lax
from jax.sharding import PartitionSpec as P

CAP = 30


def per_device(hidden, weight, targets):
    tok_rows = hidden.shape[0]
    voc_rows = weight.shape[0]
    gathered, all_targets = (
        lax.all_gather(hidden, "tok", axis=0, tiled=True),
        lax.all_gather(targets, "tok", axis=0, tiled=True),
    )
    full = lax.all_gather(gathered, "vocab", axis=1, tiled=True)
    offset = (lax.axis_index("tok") * lax.axis_size("vocab") + lax.axis_index("vocab")) * voc_rows
    logits = lax.dot_general(
        full, weight, (((1,), (1,)), ((), ())), preferred_element_type=jnp.float32
    )
    capped = CAP * jnp.tanh(logits / CAP)
    columns = offset + jnp.arange(voc_rows, dtype=jnp.int32)
    hit = columns[None, :] == all_targets[:, None]
    picked_part = jnp.sum(jnp.where(hit, capped, 0.0), axis=1)
    total, picked = lax.psum(
        (jnp.sum(jnp.exp(capped - CAP), axis=1), picked_part), ("tok", "vocab")
    )
    lse = CAP + jnp.log(total)
    loss_all = lse - picked
    loss = lax.dynamic_slice_in_dim(loss_all, lax.axis_index("tok") * tok_rows, tok_rows, 0)
    probs = jnp.exp(capped - lse[:, None])
    dlogits = ((probs - hit.astype(jnp.float32)) * (1.0 - (capped / CAP) ** 2)).astype(jnp.bfloat16)
    grad_weight = lax.dot_general(
        dlogits, full, (((0,), (0,)), ((), ())), preferred_element_type=jnp.float32
    ).astype(jnp.bfloat16)
    partial_grad = jnp.dot(dlogits, weight, preferred_element_type=jnp.float32)
    shared = lax.psum_scatter(partial_grad, "vocab", scatter_dimension=1, tiled=True)
    shared = lax.psum_scatter(shared, "tok", scatter_dimension=0, tiled=True)
    return (loss, shared.astype(jnp.bfloat16), grad_weight)


def solution(mesh):
    in_specs = (P("tok", "vocab"), P(("tok", "vocab"), None), P("tok"))
    out_specs = (P("tok"), P("tok", "vocab"), P(("tok", "vocab"), None))
    return jax.shard_map(
        per_device, mesh=mesh, in_specs=in_specs, out_specs=out_specs, check_vma=False
    )
```

profile of v0, /device:TPU:8, one launch (start us, length us, event | category | flops | bytes accessed | tf_op | source)
XLA Modules:
  0.0 376.8 jit_solution(16852351269151932645)
XLA Ops:
  7.2 0.0 all-gather.3.cloned.1.call-start
  7.2 12.1 %all_gather.9 = bf16[512,72]{0,1:T(8,128)(2,1)} all-gather(bf16[128,72]{0,1:T(8,128)(2,1)} %param.3), channel_id=1, replica_groups=mesh['tok'=4,'vocab'=64] {'tok'}, dimensions={0}, use_global_device_ids=true | all-gather | bytes 92160 | tf_op jit(solution)/shard_map/all_gather | solution.py:13
  19.3 0.0 all-gather.3.cloned.1.call-update
  19.4 0.0 reduce-scatter.3.cloned.1.call-start
  19.4 8.9 %all-gather = s32[4,1,128]{2,1,0:T(1,128)S(1)} all-gather(s32[1,1,128]{2,1,0:T(1,128)} %bitcast.9), channel_id=1, replica_groups=mesh['tok'=4,'vocab'=64] {'tok'}, dimensions={0}, use_global_device_ids=true | all-gather | bytes 2560 | tf_op jit(solution)/shard_map/all_gather | solution.py:14
  28.3 71.8 %all-gather.3.cloned.1.call-done = bf16[512,4608]{0,1:T(8,128)(2,1)} async-done(((bf16[512,72]{0,1:T(8,128)(2,1)}), bf16[512,4608]{0,1:T(8,128)(2,1)}) %all-gather.3.cloned.1.call-update) | async-done | bytes 4718608 | tf_op jit(solution)/shard_map/all_gather | solution.py:16
  100.1 8.1 %exponential_reduce_fusion = (f32[512]{0:T(512)S(1)}, f32[512]{0:T(512)S(1)}, f32[512,512]{0,1:T(8,128)S(1)}) fusion(s32[512]{0:T(512)S(1)} %bitcast.6, s32[512]{0:T(512)S(1)} %iota_add_fusion, bf16[512,4608]{1,0:T(8,128)(2,1)} %param.4, bf16[512,4608]{0,1:T(8,128)(2,1)} %all-gather.3.cloned.1.call-done), kind=kOutput, calls=%fused_computation.9 | convolution fusion | flops 2417753088 | bytes 10493952 | tf_op jit(solution)/shard_map/dot_general | solution.py:18
  108.2 76.0 %all-reduce = (f32[512]{0:T(512)S(1)}, f32[512]{0:T(512)S(1)}) all-reduce(f32[512]{0:T(512)S(1)} %get-tuple-element.4, f32[512]{0:T(512)S(1)} %get-tuple-element.3), channel_id=1, replica_groups=mesh['tok'=4,'vocab'=64] {'tok','vocab'}, use_global_device_ids=true, to_apply=%region_3.4 | all-reduce | flops 1024 | bytes 8192 | tf_op jit(solution)/shard_map/psum | solution.py:25
  184.1 8.9 %fusion.7 = f32[512,4608]{0,1:T(8,128)} fusion(bf16[512,4608]{1,0:T(8,128)(2,1)} %param.4, f32[512,512]{0,1:T(8,128)S(1)} %get-tuple-element.9, f32[512]{0:T(512)S(1)} %get-tuple-element.7, s32[512]{0:T(512)S(1)} %bitcast.7, s32[512]{0:T(512)S(1)} %iota_add_fusion), kind=kOutput, calls=%fused_computation.13 | convolution fusion | flops 2418278400 | bytes 15210496 | tf_op jit(solution)/shard_map/dot_general | solution.py:36
  193.0 0.0 reduce-scatter.3.cloned.1.call-update
  193.1 0.0 reduce-scatter.5.cloned.1.call-start
  193.1 151.2 %reduce-scatter.3.cloned.1.call-done = f32[512,72]{0,1:T(8,128)} async-done(((f32[512,4608]{0,1:T(8,128)}), f32[512,72]{0,1:T(8,128)}) %reduce-scatter.3.cloned.1.call-update) | async-done | bytes 147472 | tf_op jit(solution)/shard_map/reduce_scatter | solution.py:37
  344.3 0.0 reduce-scatter.5.cloned.1.call-update
  344.3 6.9 %convolution_convert_fusion = bf16[512,4608]{1,0:T(8,128)(2,1)} fusion(bf16[512,4608]{0,1:T(8,128)(2,1)} %all-gather.3.cloned.1.call-done, f32[512,512]{0,1:T(8,128)S(1)} %get-tuple-element.9, f32[512]{0:T(512)S(1)} %get-tuple-element.7, s32[512]{0:T(512)S(1)} %bitcast.8, s32[512]{0:T(512)S(1)} %iota_add_fusion), kind=kOutput, calls=%fused_computation | convolution fusion | flops 2420637696 | bytes 10491904 | tf_op jit(solution)/shard_map/dot_general | solution.py:33
  351.2 0.6 dynamic_slice.3
  351.8 17.1 %reduce-scatter.5.cloned.1.call-done = f32[128,72]{0,1:T(8,128)} async-done(((f32[512,72]{0,1:T(8,128)}), f32[128,72]{0,1:T(8,128)}) %reduce-scatter.5.cloned.1.call-update) | async-done | bytes 36880 | tf_op jit(solution)/shard_map/reduce_scatter | solution.py:38
  368.9 1.4 convert_element_type.14
  (2 shorter events, 0.0 us)
Async XLA Ops:
  7.2 92.9 %all-gather.3.cloned.1.call-start = ((), (), s32[]{:S(2)}) async-start(), calls=%async_computation.2 | async-start | bytes 4792320 | tf_op jit(solution)/shard_map/all_gather | solution.py:16
  19.4 325.0 %reduce-scatter.3.cloned.1.call-start = ((), (), s32[]{:S(2)}) async-start(), calls=%async_computation.3 | async-start | bytes 9584640 | tf_op jit(solution)/shard_map/reduce_scatter | solution.py:37
  193.1 175.9 %reduce-scatter.5.cloned.1.call-start = ((), (), s32[]{:S(2)}) async-start(), calls=%async_computation.4 | async-start | bytes 184320 | tf_op jit(solution)/shard_map/reduce_scatter | solution.py:38
Sparse Core Ops, SparseCore 0:
  19.5 80.5 all-gather.2
  193.2 151.0 reduce-scatter.2
  346.8 22.0 reduce-scatter.4
where the time goes:
time: 377 us
  waiting for transfers between devices  240 us (64%)
  blocking collectives  96.9 us (26%)
  matrix products  23.9 us (6%)
  between operations  13.8 us (4%)
    reduce_scatter x1, waiting for transfers between devices, per_device(): lax.psum_scatter(partial_grad, 'vocab', scatter_dimension=1, tiled=True)  151 us
    psum x1, blocking collectives, per_device(): lax.psum((jnp.sum(jnp.exp(capped - CAP), axis=1), picked_part), ('tok', '...  76 us
    all_gather x1, waiting for transfers between devices, per_device(): full = lax.all_gather(gathered, 'vocab', axis=1, tiled=True)  71.8 us
    reduce_scatter x1, waiting for transfers between devices, per_device(): shared = lax.psum_scatter(shared, 'tok', scatter_dimension=0, tiled=True)  17.1 us
    all_gather x1, blocking collectives, per_device(): lax.all_gather(hidden, 'tok', axis=0, tiled=True)  12.1 us
    dot_general x1, matrix products, per_device(): partial_grad = jnp.dot(dlogits, weight, preferred_element_type=jnp.float32)  8.89 us
    all_gather x1, blocking collectives, per_device(): lax.all_gather(targets, 'tok', axis=0, tiled=True)  8.88 us
    dot_general x1, matrix products, per_device(): lax.dot_general(full, weight, (((1,), (1,)), ((), ())), preferred_element...  8.1 us
  transfers between devices with their start and end apart: 3, of which 3 were waited for; matrix products, arithmetic and copies ran while one was open for 2% of the time, Pallas kernels for 0%

commit v1 on v0

v1 whole, which is shorter than its diff:
```python
import jax
import jax.numpy as jnp
from jax import lax
from jax.sharding import Mesh, PartitionSpec as P

CAP = 30
F32, BF16 = jnp.float32, jnp.bfloat16
X, Y, Z, C = 4, 4, 8, 2


def pull(array, axis, size, step):
    return lax.ppermute(array, axis, [((i + step) % size, i) for i in range(size)])


def push(array, axis, size, step):
    return lax.ppermute(array, axis, [(i, (i + step) % size) for i in range(size)])


def turned(array, start, size, dim):
    doubled = lax.concatenate([array, array], dim)
    return lax.dynamic_slice_in_dim(doubled, start, size, dim)


def spread(array, axes, size):
    copies = jnp.broadcast_to(array[None], (size,) + array.shape)
    return lax.all_to_all(copies, axes, 0, 0, tiled=True)


def digits(targets):
    parts = [targets // 65536, (targets // 256) % 256, targets % 256]
    return jnp.concatenate([jnp.stack(parts), jnp.zeros((5, targets.shape[0]), jnp.int32)]).astype(BF16)


def undigits(rows):
    parts = rows.astype(jnp.int32)
    return parts[:, 0] * 65536 + parts[:, 1] * 256 + parts[:, 2]


def per_device(hidden, weight, targets):
    rows, feats = hidden.shape
    voc = weight.shape[0]
    half = Z // 2
    x, y, z, c = (lax.axis_index(name) for name in ("x", "y", "z", "c"))

    wt = weight.T.reshape(Y, Z, C, feats, voc)
    wt = turned(wt, y, Y, 0)
    mine = lax.dynamic_index_in_dim(wt, c, 2, keepdims=False)
    theirs = lax.dynamic_index_in_dim(wt, 1 - c, 2, keepdims=False)
    pair = jnp.concatenate([mine, pull(theirs, "c", C, 1)], -1)

    along_z = spread(hidden.T, "z", Z)
    a, b = along_z[:half], along_z[half:]
    b = jnp.concatenate([b.reshape(half * feats, rows), digits(targets)])
    a_y, b_x = [a], [b]
    for step in range(1, 4):
        a_y.append(pull(a, "y", Y, step))
        b_x.append(pull(b, "x", X, step))
    a2 = jnp.stack(a_y)
    b2 = jnp.stack(b_x)
    tgt = undigits(b2[:, half * feats :]).reshape(X * rows)
    b2 = b2[:, : half * feats]
    a_xy, b_xy = [a2], [b2]
    for step in range(1, 4):
        a_xy.append(pull(a2, "x", X, step))
        b_xy.append(pull(b2, "y", Y, step))
    a3 = jnp.stack(a_xy, 3).reshape(Y, half, feats, X * rows)
    b3 = jnp.stack(b_xy).reshape(Y, X, half, feats, rows)
    b3 = b3.transpose(0, 2, 3, 1, 4).reshape(Y, half, feats, X * rows)
    ht = jnp.concatenate([a3, b3], 1)

    part = lax.dot_general(
        pair.reshape(-1, C * voc), ht.reshape(-1, X * rows), (((0,), (0,)), ((), ())), preferred_element_type=F32
    )
    logits = part[:voc] + pull(part[voc:], "c", C, 1)
    capped = CAP * jnp.tanh(logits / CAP)
    offset = (((x * Y + y) * Z + z) * C + c) * voc
    columns = offset + jnp.arange(voc, dtype=jnp.int32)
    hit = columns[:, None] == tgt[None, :]
    stats = jnp.stack([jnp.sum(jnp.exp(capped - CAP), 0), jnp.sum(jnp.where(hit, capped, 0.0), 0)])
    stats = spread(stats.reshape(2, X, rows), ("z", "c"), Z * C).sum(0)
    stats = turned(stats, (X - x) % X, X, 1)
    stats = spread(stats, ("x", "y"), X * Y).sum(0)
    stats = turned(stats, x, X, 1)
    lse = CAP + jnp.log(stats[0])
    loss = lse[0] - stats[1, 0]
    probs = jnp.exp(capped - lse.reshape(1, X * rows))
    dlogits = ((probs - hit.astype(F32)) * (1.0 - (capped / CAP) ** 2)).astype(BF16)

    dl_pair = jnp.concatenate([dlogits, pull(dlogits, "c", C, 1)], 0)
    grad = jnp.dot(pair.reshape(-1, C * voc), dl_pair, preferred_element_type=F32)
    grad = grad.reshape(Y, Z, feats, X, rows)
    ga, gb = grad[:, :half], grad[:, half:]
    a_own, b_own = ga[:, :, :, 0], gb[0]
    for step in range(1, 4):
        a_own = a_own + push(ga[:, :, :, step].astype(BF16), "x", X, step).astype(F32)
        b_own = b_own + push(gb[step].astype(BF16), "y", Y, step).astype(F32)
    a_sum, b_sum = a_own[0], b_own[:, :, 0]
    for step in range(1, 4):
        a_sum = a_sum + push(a_own[step].astype(BF16), "y", Y, step).astype(F32)
        b_sum = b_sum + push(b_own[:, :, step].astype(BF16), "x", X, step).astype(F32)
    by_z = lax.all_to_all(jnp.concatenate([a_sum, b_sum], 0), "z", 0, 0, tiled=True)
    grad_hidden = by_z.sum(0).astype(BF16).T

    other = pull(ht, "c", C, 1)
    first = jnp.where(c == 0, ht, other)
    second = jnp.where(c == 0, other, ht)
    full = turned(jnp.stack([first, second], 2), (Y - y) % Y, Y, 0)
    full = full.reshape(Y * Z * C * feats, X * rows)
    grad_weight = lax.dot_general(
        dlogits, full, (((1,), (1,)), ((), ())), preferred_element_type=F32
    ).astype(BF16)
    return loss, grad_hidden, grad_weight


def solution(mesh):
    chips = Mesh(mesh.devices.reshape(X, Y, Z, C), ("x", "y", "z", "c"))
    in_specs = (P("x", ("y", "z", "c")), P(("x", "y", "z", "c"), None), P("x"))
    out_specs = (P("x"), P("x", ("y", "z", "c")), P(("x", "y", "z", "c"), None))
    return jax.shard_map(per_device, mesh=chips, in_specs=in_specs, out_specs=out_specs, check_vma=False)
```

time: 377 us -> 179 us (0.47)
  waiting for transfers between devices: 240 us -> 52.2 us
  blocking collectives: 96.9 us -> 18.3 us
  starting transfers between devices: 0.12 us -> 52.8 us
  other arithmetic: 1.38 us -> 19.4 us
  local copies, waits for them, and re-layouts: 0.58 us -> 18.5 us
  between operations: 13.8 us -> 1.03 us
  matrix products: 23.9 us -> 15.8 us
    reduce_scatter x2 -> x0, waiting for transfers between devices: 168 us -> none  [the longest x1 151 us: per_device(): lax.psum_scatter(partial_grad, 'vocab', scatter_dimension=1, tiled=True)]
    psum x1 -> x0, blocking collectives: 76 us -> none  [per_device(): lax.psum((jnp.sum(jnp.exp(capped - CAP), axis=1), picked_part), ('tok', '...]
    all_gather x1 -> x0, waiting for transfers between devices: 71.8 us -> none  [per_device(): full = lax.all_gather(gathered, 'vocab', axis=1, tiled=True)]
    ppermute x0 -> x28, waiting for transfers between devices: none -> 38.2 us  [the longest x16 23.2 us: pull(): lax.ppermute(array, axis, [((i + step) % size, i) for i in range(size)])]
    ppermute x0 -> x28, starting transfers between devices: none -> 37.7 us  [the longest x16 19.5 us: pull(): lax.ppermute(array, axis, [((i + step) % size, i) for i in range(size)])]
    all_gather x2 -> x0, blocking collectives: 21 us -> none  [the longest x1 12.1 us: per_device(): lax.all_gather(hidden, 'tok', axis=0, tiled=True)]
    all_to_all x0 -> x1, blocking collectives: none -> 18.3 us  [spread(): return lax.all_to_all(copies, axes, 0, 0, tiled=True)]
    all_to_all x0 -> x3, starting transfers between devices: none -> 15.1 us  [the longest x2 11.7 us: spread(): return lax.all_to_all(copies, axes, 0, 0, tiled=True)]
  transfers between devices with their start and end apart: 3 -> 31, of which waited for: 3 -> 18; matrix products, arithmetic and copies ran while one was open for 2% -> 18% of each run, Pallas kernels for 0% -> 0%
where the time goes in v1:
time: 179 us; the launch traced here: 178 us
  starting transfers between devices  52.8 us (29%)
  waiting for transfers between devices  52.2 us (29%)
  other arithmetic  19.4 us (11%)
  local copies, waits for them, and re-layouts  18.5 us (10%)
  blocking collectives  18.3 us (10%)
  matrix products  15.8 us (9%)
    ppermute x16, waiting for transfers between devices, pull(): lax.ppermute(array, axis, [((i + step) % size, i) for i in range(size)])  23.2 us
    ppermute x16, starting transfers between devices, pull(): lax.ppermute(array, axis, [((i + step) % size, i) for i in range(size)])  19.5 us
    all_to_all x1, blocking collectives, spread(): return lax.all_to_all(copies, axes, 0, 0, tiled=True)  18.3 us
    ppermute x12, starting transfers between devices, push(): lax.ppermute(array, axis, [(i, (i + step) % size) for i in range(size)])  18.1 us
    ppermute x12, waiting for transfers between devices, push(): lax.ppermute(array, axis, [(i, (i + step) % size) for i in range(size)])  15 us
    all_to_all x2, starting transfers between devices, spread(): return lax.all_to_all(copies, axes, 0, 0, tiled=True)  11.7 us
    all_to_all x2, waiting for transfers between devices, spread(): return lax.all_to_all(copies, axes, 0, 0, tiled=True)  9.93 us
    unnamed x29, local copies, waits for them, and re-layouts  8.3 us
  transfers between devices with their start and end apart: 31, of which 18 were waited for; matrix products, arithmetic and copies ran while one was open for 18% of the time, Pallas kernels for 0%

profile of v1, /device:TPU:8, one launch (start us, length us, event | category | flops | bytes accessed | tf_op | source)
XLA Modules:
  0.0 178.2 jit_solution(14462139639144058694)
XLA Ops:
  0.6 6.6 %copy.55 = bf16[512,4608]{0,1:T(8,128)(2,1)} copy(bf16[512,4608]{1,0:T(8,128)(2,1)} %param.4) | data formatting | bytes 9437184 | tf_op args[1]
  7.3 4.8 %fusion.9 = (bf16[4,8,72,512]{3,2,1,0:T(8,128)(2,1)}, bf16[4,8,72,512]{3,2,1,0:T(8,128)(2,1)}) fusion(s32[]{:T(128)S(6)} %select_n.71, s32[]{:T(128)S(6)} %select_n.73, bf16[4,8,2,72,512]{4,3,2,1,0:T(8,128)(2,1)} %bitcast.141, s32[]{:T(128)S(6)} %select_n.75), kind=kLoop, calls=%fused_computation.19 | loop fusion | flops 2359296 | bytes 9437196 | tf_op jit(solution)/shard_map/jit(dynamic_index_in_dim)/squeeze | solution.py:47
  12.1 18.3 %all_to_all.20 = bf16[8,72,128]{2,1,0:T(8,128)(2,1)S(1)} all-to-all(bf16[8,72,128]{2,1,0:T(8,128)(2,1)S(1)} %broadcast_in_dim.14), channel_id=1, replica_groups=mesh['x'=4,'y'=4,'z'=8,'c'=2] {'z'}, dimensions={0} | all-to-all | bytes 294912 | tf_op jit(solution)/shard_map/all_to_all | solution.py:26
  30.4 1.7 collective-permute-start.3
  33.0 2.4 %collective-permute-start.1 = (bf16[4,72,128]{2,1,0:T(8,128)(2,1)S(1)}, bf16[4,72,128]{2,1,0:T(8,128)(2,1)S(1)}, u32[]{:S(2)}, u32[]{:S(2)}) collective-permute-start(bf16[4,72,128]{2,1,0:T(8,128)(2,1)S(1)} %get-tuple-element.29), channel_id=1, source_target_pairs={{16,0},{32,16},{48,32},{0,48},{17,1},{33,17},{49,33},{1,49},{18,2}... | collective-permute-start | bytes 221192 | tf_op jit(solution)/shard_map/ppermute | solution.py:12
  35.4 2.6 %collective-permute-done.2 = bf16[4,72,128]{2,1,0:T(8,128)(2,1)S(1)} collective-permute-done((bf16[4,72,128]{2,1,0:T(8,128)(2,1)S(1)}, bf16[4,72,128]{2,1,0:T(8,128)(2,1)S(1)}, u32[]{:S(2)}, u32[]{:S(2)}) %collective-permute-start.2) | collective-permute-done | bytes 73760 | tf_op jit(solution)/shard_map/ppermute | solution.py:12
  38.2 1.6 collective-permute-start.6
  39.8 2.7 %collective-permute-start.5 = (bf16[4,4,72,128]{3,2,1,0:T(8,128)(2,1)S(1)}, bf16[4,4,72,128]{3,2,1,0:T(8,128)(2,1)S(1)}, u32[]{:S(2)}, u32[]{:S(2)}) collective-permute-start(bf16[4,4,72,128]{3,2,1,0:T(8,128)(2,1)S(1)} %get-tuple-element.26), channel_id=1, source_target_pairs={{128,0},{192,64},{0,128},{64,192},{129,1},{193,65},{1,129},{65,193... | collective-permute-start | bytes 884744 | tf_op jit(solution)/shard_map/ppermute | solution.py:12
  42.7 2.9 %collective-permute-start.8 = (bf16[296,128]{1,0:T(8,128)(2,1)S(1)}, bf16[296,128]{1,0:T(8,128)(2,1)S(1)}, u32[]{:S(2)}, u32[]{:S(2)}) collective-permute-start(bf16[296,128]{1,0:T(8,128)(2,1)S(1)} %concatenate.36), channel_id=1, source_target_pairs={{128,0},{192,64},{0,128},{64,192},{129,1},{193,65},{1,129},{65,193... | collective-permute-start | bytes 227336 | tf_op jit(solution)/shard_map/ppermute | solution.py:12
  45.6 9.4 %collective-permute-done.9 = bf16[296,128]{1,0:T(8,128)(2,1)S(1)} collective-permute-done((bf16[296,128]{1,0:T(8,128)(2,1)S(1)}, bf16[296,128]{1,0:T(8,128)(2,1)S(1)}, u32[]{:S(2)}, u32[]{:S(2)}) %collective-permute-start.9) | collective-permute-done | bytes 75808 | tf_op jit(solution)/shard_map/ppermute | solution.py:12
  55.0 1.2 collective-permute-start.7
  57.0 2.5 %collective-permute-done.7 = bf16[296,128]{1,0:T(8,128)(2,1)S(1)} collective-permute-done((bf16[296,128]{1,0:T(8,128)(2,1)S(1)}, bf16[296,128]{1,0:T(8,128)(2,1)S(1)}, u32[]{:S(2)}, u32[]{:S(2)}) %collective-permute-start.7) | collective-permute-done | bytes 75808 | tf_op jit(solution)/shard_map/ppermute | solution.py:12
  59.9 2.9 %collective-permute-start.11 = (bf16[4,288,128]{2,1,0:T(8,128)(2,1)S(1)}, bf16[4,288,128]{2,1,0:T(8,128)(2,1)S(1)}, u32[]{:S(2)}, u32[]{:S(2)}) collective-permute-start(bf16[4,288,128]{2,1,0:T(8,128)(2,1)S(1)} %slice.137), channel_id=1, source_target_pairs={{32,0},{48,16},{0,32},{16,48},{33,1},{49,17},{1,33},{17,49},{34,2}... | collective-permute-start | bytes 884744 | tf_op jit(solution)/shard_map/ppermute | solution.py:12
  62.8 1.9 %collective-permute-start.10 = (bf16[4,288,128]{2,1,0:T(8,128)(2,1)S(1)}, bf16[4,288,128]{2,1,0:T(8,128)(2,1)S(1)}, u32[]{:S(2)}, u32[]{:S(2)}) collective-permute-start(bf16[4,288,128]{2,1,0:T(8,128)(2,1)S(1)} %slice.137), channel_id=1, source_target_pairs={{16,0},{32,16},{48,32},{0,48},{17,1},{33,17},{49,33},{1,49},{18,2}... | collective-permute-start | bytes 884744 | tf_op jit(solution)/shard_map/ppermute | solution.py:12
  65.1 1.8 %collective-permute-done.12 = bf16[4,288,128]{2,1,0:T(8,128)(2,1)S(1)} collective-permute-done((bf16[4,288,128]{2,1,0:T(8,128)(2,1)S(1)}, bf16[4,288,128]{2,1,0:T(8,128)(2,1)S(1)}, u32[]{:S(2)}, u32[]{:S(2)}) %collective-permute-start.12) | collective-permute-done | bytes 294944 | tf_op jit(solution)/shard_map/ppermute | solution.py:12
  67.0 1.6 collective-permute-done.11
  68.8 2.9 %collective-permute-done.10 = bf16[4,288,128]{2,1,0:T(8,128)(2,1)S(1)} collective-permute-done((bf16[4,288,128]{2,1,0:T(8,128)(2,1)S(1)}, bf16[4,288,128]{2,1,0:T(8,128)(2,1)S(1)}, u32[]{:S(2)}, u32[]{:S(2)}) %collective-permute-start.10) | collective-permute-done | bytes 294944 | tf_op jit(solution)/shard_map/ppermute | solution.py:12
  72.9 1.3 reshape.106
  74.2 1.5 constant_dynamic-update-slice_fusion
  76.2 4.6 %fusion.10 = f32[1024,512]{1,0:T(8,128)S(1)} fusion(bf16[4,8,72,512]{3,2,1,0:T(8,128)(2,1)S(1)} %constant_dynamic-update-slice_fusion, bf16[4,8,72,512]{3,2,1,0:T(8,128)(2,1)} %collective-permute-done, bf16[4,8,72,512]{3,2,1,0:T(8,128)(2,1)S(1)} %copy-done.3), kind=kOutput, calls=%fused_computation.22 | convolution fusion | flops 2425356288 | bytes 9175040 | tf_op jit(solution)/shard_map/dot_general | solution.py:71
  80.9 1.1 slice.139
  83.5 2.0 %collective-permute-done.13 = f32[512,512]{1,0:T(8,128)S(1)} collective-permute-done((f32[512,512]{1,0:T(8,128)}, f32[512,512]{1,0:T(8,128)S(1)}, u32[]{:S(2)}, u32[]{:S(2)}) %collective-permute-start.13) | collective-permute-done | bytes 1048608 | tf_op jit(solution)/shard_map/ppermute | solution.py:12
  85.5 1.6 exponential_reduce_fusion
  87.8 3.5 %all-to-all-start.1 = ((f32[16,2,4,128]{3,2,1,0:T(4,128)}), f32[16,2,4,128]{3,2,1,0:T(4,128)S(1)}, u32[]{:S(2)}, u32[]{:S(2)}) async-start(f32[16,2,4,128]{3,2,1,0:T(4,128)} %broadcast_in_dim.31), calls=%async_computation.1 | async-start | bytes 131072 | tf_op jit(solution)/shard_map/all_to_all | solution.py:26
  91.3 7.7 %all-to-all-done.1 = f32[16,2,4,128]{3,2,1,0:T(4,128)S(1)} async-done(((f32[16,2,4,128]{3,2,1,0:T(4,128)}), f32[16,2,4,128]{3,2,1,0:T(4,128)S(1)}, u32[]{:S(2)}, u32[]{:S(2)}) %all-to-all-start.1) | async-done | bytes 65568 | tf_op jit(solution)/shard_map/all_to_all | solution.py:26
  99.7 8.2 %all-to-all-start.2 = ((f32[16,2,4,128]{3,2,1,0:T(4,128)}), f32[16,2,4,128]{3,2,1,0:T(4,128)S(1)}, u32[]{:S(2)}, u32[]{:S(2)}) async-start(f32[16,2,4,128]{3,2,1,0:T(4,128)} %broadcast_in_dim.32), calls=%async_computation.2 | async-start | bytes 131072 | tf_op jit(solution)/shard_map/all_to_all | solution.py:26
  108.0 4.1 %select_bitcast_fusion = (bf16[4,8,1,72,512]{4,3,1,0,2:T(8,128)(2,1)S(1)}, bf16[4,8,1,72,512]{4,3,1,0,2:T(8,128)(2,1)}) fusion(bf16[4,8,72,512]{3,2,1,0:T(8,128)(2,1)} %collective-permute-done.27, bf16[4,8,72,512]{3,2,1,0:T(8,128)(2,1)} %copy-done.1, pred[]{:T(512)S(6)} %eq.26), kind=kLoop, calls=%fused_computation.20 | loop fusion | flops 2359296 | bytes 9437185 | tf_op jit(solution)/shard_map/stack | solution.py:107
  112.0 2.2 %all-to-all-done.2 = f32[16,2,4,128]{3,2,1,0:T(4,128)S(1)} async-done(((f32[16,2,4,128]{3,2,1,0:T(4,128)}), f32[16,2,4,128]{3,2,1,0:T(4,128)S(1)}, u32[]{:S(2)}, u32[]{:S(2)}) %all-to-all-start.2) | async-done | bytes 65568 | tf_op jit(solution)/shard_map/all_to_all | solution.py:26
  114.3 1.9 %fusion.14 = bf16[512,512]{1,0:T(8,128)(2,1)S(1)} fusion(f32[512]{0:T(512)S(1)} %get-tuple-element.30, s32[512]{0:T(512)S(1)} %bitcast.166, s32[512]{0:T(512)S(1)} %iota_add_fusion, f32[512,512]{1,0:T(8,128)S(1)} %collective-permute-done.13, f32[1024,512]{1,0:T(8,128)} %copy-done.2), kind=kLoop, calls=%fused_computation.31 | loop fusion | flops 2883584 | bytes 2627584 | tf_op jit(solution)/shard_map/convert_element_type | solution.py:87
  116.5 2.5 %fusion.1 = bf16[4,8,2,72,512]{4,3,1,0,2:T(8,128)(2,1)S(1)} fusion(s32[]{:T(128)S(6)} %select_n.88, bf16[4,8,1,72,512]{4,3,1,0,2:T(8,128)(2,1)S(1)} %copy-done, bf16[4,8,1,72,512]{4,3,1,0,2:T(8,128)(2,1)S(1)} %get-tuple-element.9), kind=kLoop, calls=%fused_computation.10 | loop fusion | flops 7077888 | bytes 9437188 | tf_op jit(solution)/shard_map/concatenate | solution.py:20
  119.0 2.7 %copy.72 = bf16[4,8,2,72,512]{4,3,2,1,0:T(8,128)(2,1)} copy(bf16[4,8,2,72,512]{4,3,1,0,2:T(8,128)(2,1)S(1)} %fusion.1) | data formatting | bytes 9437184 | tf_op jit(solution)/shard_map/dynamic_slice | solution.py:21
  121.8 1.3 copy.76
  123.8 4.6 %fusion.3 = f32[4,8,72,4,128]{4,2,3,1,0:T(8,128)S(1)} fusion(bf16[4,128,1024,1,1]{2,1,0,4,3:T(8,128)(2,1)} %bitcast.144, bf16[4,8,72,512]{3,2,1,0:T(8,128)(2,1)} %collective-permute-done, bf16[4,8,72,512]{3,2,1,0:T(8,128)(2,1)S(1)} %copy-done.4), kind=kOutput, calls=%fused_computation.13 | convolution fusion | flops 2425356288 | bytes 10485760 | tf_op jit(solution)/shard_map/dot_general | solution.py:90
  129.4 2.7 %collective-permute-start.22 = (bf16[4,72,4,128]{3,1,0,2:T(8,128)(2,1)S(1)}, bf16[4,72,4,128]{3,1,0,2:T(8,128)(2,1)S(1)}, u32[]{:S(2)}, u32[]{:S(2)}) collective-permute-start(bf16[4,72,4,128]{3,1,0,2:T(8,128)(2,1)S(1)} %get-tuple-element.18), channel_id=1, source_target_pairs={{0,32},{16,48},{32,0},{48,16},{1,33},{17,49},{33,1},{49,17},{2,34}... | collective-permute-start | bytes 884744 | tf_op jit(solution)/shard_map/ppermute | solution.py:16
  133.4 1.2 collective-permute-start.17
  134.5 1.5 collective-permute-start.16
  136.0 2.4 %collective-permute-done.21 = bf16[4,72,4,128]{3,1,0,2:T(8,128)(2,1)S(1)} collective-permute-done((bf16[4,72,4,128]{3,1,0,2:T(8,128)(2,1)S(1)}, bf16[4,72,4,128]{3,1,0,2:T(8,128)(2,1)S(1)}, u32[]{:S(2)}, u32[]{:S(2)}) %collective-permute-start.21) | collective-permute-done | bytes 294944 | tf_op jit(solution)/shard_map/ppermute | solution.py:16
  138.9 1.8 %collective-permute-done.22 = bf16[4,72,4,128]{3,1,0,2:T(8,128)(2,1)S(1)} collective-permute-done((bf16[4,72,4,128]{3,1,0,2:T(8,128)(2,1)S(1)}, bf16[4,72,4,128]{3,1,0,2:T(8,128)(2,1)S(1)}, u32[]{:S(2)}, u32[]{:S(2)}) %collective-permute-start.22) | collective-permute-done | bytes 294944 | tf_op jit(solution)/shard_map/ppermute | solution.py:16
  140.8 5.5 %collective-permute-done.23 = bf16[4,72,4,128]{3,1,0,2:T(8,128)(2,1)S(1)} collective-permute-done((bf16[4,72,4,128]{3,1,0,2:T(8,128)(2,1)S(1)}, bf16[4,72,4,128]{3,1,0,2:T(8,128)(2,1)S(1)}, u32[]{:S(2)}, u32[]{:S(2)}) %collective-permute-start.23) | collective-permute-done | bytes 294944 | tf_op jit(solution)/shard_map/ppermute | solution.py:16
  146.4 1.2 collective-permute-start.26
  147.7 1.4 collective-permute-start.25
  149.4 1.2 collective-permute-done.15
  150.8 5.9 %collective-permute-start.20 = (bf16[4,72,128]{2,1,0:T(8,128)(2,1)S(1)}, bf16[4,72,128]{2,1,0:T(8,128)(2,1)S(1)}, u32[]{:S(2)}, u32[]{:S(2)}) collective-permute-start(bf16[4,72,128]{2,1,0:T(8,128)(2,1)S(1)} %get-tuple-element.20), channel_id=1, source_target_pairs={{0,48},{16,0},{32,16},{48,32},{1,49},{17,1},{33,17},{49,33},{2,50}... | collective-permute-start | bytes 221192 | tf_op jit(solution)/shard_map/ppermute | solution.py:16
  156.7 1.8 %collective-permute-start.18 = (bf16[4,72,128]{2,1,0:T(8,128)(2,1)S(1)}, bf16[4,72,128]{2,1,0:T(8,128)(2,1)S(1)}, u32[]{:S(2)}, u32[]{:S(2)}) collective-permute-start(bf16[4,72,128]{2,1,0:T(8,128)(2,1)S(1)} %get-tuple-element.19), channel_id=1, source_target_pairs={{0,16},{16,32},{32,48},{48,0},{1,17},{17,33},{33,49},{49,1},{2,18}... | collective-permute-start | bytes 221192 | tf_op jit(solution)/shard_map/ppermute | solution.py:16
  158.7 3.9 %collective-permute-done.19 = bf16[4,72,128]{2,1,0:T(8,128)(2,1)S(1)} collective-permute-done((bf16[4,72,128]{2,1,0:T(8,128)(2,1)S(1)}, bf16[4,72,128]{2,1,0:T(8,128)(2,1)S(1)}, u32[]{:S(2)}, u32[]{:S(2)}) %collective-permute-start.19) | collective-permute-done | bytes 73760 | tf_op jit(solution)/shard_map/ppermute | solution.py:16
  163.4 3.4 %all-to-all-start.3 = ((f32[8,72,128]{2,1,0:T(8,128)}), f32[8,72,128]{2,1,0:T(8,128)S(1)}, u32[]{:S(2)}, u32[]{:S(2)}) async-start(f32[8,72,128]{2,1,0:T(8,128)} %pad_maximum_fusion.7), calls=%async_computation.3 | async-start | bytes 589824 | tf_op jit(solution)/shard_map/all_to_all | solution.py:101
  166.8 6.6 %convolution_convert_fusion = bf16[512,4608]{1,0:T(8,128)(2,1)} fusion(bf16[512,512]{1,0:T(8,128)(2,1)S(1)} %copy-done.6, bf16[4608,512]{1,0:T(8,128)(2,1)} %bitcast.142), kind=kOutput, calls=%fused_computation.8 | convolution fusion | flops 2418278400 | bytes 9961472 | tf_op jit(solution)/shard_map/dot_general | solution.py:109
  173.4 4.1 %all-to-all-done.3 = f32[8,72,128]{2,1,0:T(8,128)S(1)} async-done(((f32[8,72,128]{2,1,0:T(8,128)}), f32[8,72,128]{2,1,0:T(8,128)S(1)}, u32[]{:S(2)}, u32[]{:S(2)}) %all-to-all-start.3) | async-done | bytes 294944 | tf_op jit(solution)/shard_map/all_to_all | solution.py:101
  (93 shorter events, 13.7 us)
Async XLA Ops:
  7.3 4.8 %copy-start.12 = (bf16[128,72]{0,1:T(8,128)(2,1)S(1)}, bf16[128,72]{0,1:T(8,128)(2,1)}, u32[]{:S(2)}) copy-start(bf16[128,72]{0,1:T(8,128)(2,1)} %param.3) | copy-start | bytes 55300
  7.3 35.3 %copy-start.13 = (s32[128]{0:T(128)S(1)}, s32[128]{0:T(128)}, u32[]{:S(2)}) copy-start(s32[128]{0:T(128)} %param.5) | copy-start | bytes 1540
  12.0 63.8 %collective-permute-start = (bf16[4,8,72,512]{3,2,1,0:T(8,128)(2,1)}, bf16[4,8,72,512]{3,2,1,0:T(8,128)(2,1)}, u32[]{:S(2)}, u32[]{:S(2)}) collective-permute-start(bf16[4,8,72,512]{3,2,1,0:T(8,128)(2,1)} %get-tuple-element.12), channel_id=1, source_target_pairs={{1,0},{0,1},{3,2},{2,3},{5,4},{4,5},{7,6},{6,7},{9,8},{8,9},{11,10... | collective-permute-start | bytes 7077896 | tf_op jit(solution)/shard_map/ppermute | solution.py:12
  30.4 5.0 %collective-permute-start.3 = (bf16[4,72,128]{2,1,0:T(8,128)(2,1)S(1)}, bf16[4,72,128]{2,1,0:T(8,128)(2,1)S(1)}, u32[]{:S(2)}, u32[]{:S(2)}) collective-permute-start(bf16[4,72,128]{2,1,0:T(8,128)(2,1)S(1)} %get-tuple-element.29), channel_id=1, source_target_pairs={{48,0},{0,16},{16,32},{32,48},{49,1},{1,17},{17,33},{33,49},{50,2}... | collective-permute-start | bytes 221192 | tf_op jit(solution)/shard_map/ppermute | solution.py:12
  32.1 6.0 %collective-permute-start.2 = (bf16[4,72,128]{2,1,0:T(8,128)(2,1)S(1)}, bf16[4,72,128]{2,1,0:T(8,128)(2,1)S(1)}, u32[]{:S(2)}, u32[]{:S(2)}) collective-permute-start(bf16[4,72,128]{2,1,0:T(8,128)(2,1)S(1)} %get-tuple-element.29), channel_id=1, source_target_pairs={{32,0},{48,16},{0,32},{16,48},{33,1},{49,17},{1,33},{17,49},{34,2}... | collective-permute-start | bytes 221192 | tf_op jit(solution)/shard_map/ppermute | solution.py:12
  33.0 5.1 %collective-permute-start.1 = (bf16[4,72,128]{2,1,0:T(8,128)(2,1)S(1)}, bf16[4,72,128]{2,1,0:T(8,128)(2,1)S(1)}, u32[]{:S(2)}, u32[]{:S(2)}) collective-permute-start(bf16[4,72,128]{2,1,0:T(8,128)(2,1)S(1)} %get-tuple-element.29), channel_id=1, source_target_pairs={{16,0},{32,16},{48,32},{0,48},{17,1},{33,17},{49,33},{1,49},{18,2}... | collective-permute-start | bytes 221192 | tf_op jit(solution)/shard_map/ppermute | solution.py:12
  38.2 21.7 %collective-permute-start.6 = (bf16[4,4,72,128]{3,2,1,0:T(8,128)(2,1)S(1)}, bf16[4,4,72,128]{3,2,1,0:T(8,128)(2,1)S(1)}, u32[]{:S(2)}, u32[]{:S(2)}) collective-permute-start(bf16[4,4,72,128]{3,2,1,0:T(8,128)(2,1)S(1)} %get-tuple-element.26), channel_id=1, source_target_pairs={{192,0},{0,64},{64,128},{128,192},{193,1},{1,65},{65,129},{129,193... | collective-permute-start | bytes 884744 | tf_op jit(solution)/shard_map/ppermute | solution.py:12
  39.8 23.0 %collective-permute-start.5 = (bf16[4,4,72,128]{3,2,1,0:T(8,128)(2,1)S(1)}, bf16[4,4,72,128]{3,2,1,0:T(8,128)(2,1)S(1)}, u32[]{:S(2)}, u32[]{:S(2)}) collective-permute-start(bf16[4,4,72,128]{3,2,1,0:T(8,128)(2,1)S(1)} %get-tuple-element.26), channel_id=1, source_target_pairs={{128,0},{192,64},{0,128},{64,192},{129,1},{193,65},{1,129},{65,193... | collective-permute-start | bytes 884744 | tf_op jit(solution)/shard_map/ppermute | solution.py:12
  42.6 22.3 %copy-start.7 = (bf16[296,128]{1,0:T(8,128)(2,1)}, bf16[296,128]{1,0:T(8,128)(2,1)S(1)}, u32[]{:S(2)}) copy-start(bf16[296,128]{1,0:T(8,128)(2,1)S(1)} %concatenate.36) | copy-start | bytes 227332
  42.6 12.4 %collective-permute-start.9 = (bf16[296,128]{1,0:T(8,128)(2,1)S(1)}, bf16[296,128]{1,0:T(8,128)(2,1)S(1)}, u32[]{:S(2)}, u32[]{:S(2)}) collective-permute-start(bf16[296,128]{1,0:T(8,128)(2,1)S(1)} %concatenate.36), channel_id=1, source_target_pairs={{192,0},{0,64},{64,128},{128,192},{193,1},{1,65},{65,129},{129,193... | collective-permute-start | bytes 227336 | tf_op jit(solution)/shard_map/ppermute | solution.py:12
  42.7 13.7 %collective-permute-start.8 = (bf16[296,128]{1,0:T(8,128)(2,1)S(1)}, bf16[296,128]{1,0:T(8,128)(2,1)S(1)}, u32[]{:S(2)}, u32[]{:S(2)}) collective-permute-start(bf16[296,128]{1,0:T(8,128)(2,1)S(1)} %concatenate.36), channel_id=1, source_target_pairs={{128,0},{192,64},{0,128},{64,192},{129,1},{193,65},{1,129},{65,193... | collective-permute-start | bytes 227336 | tf_op jit(solution)/shard_map/ppermute | solution.py:12
  55.0 9.9 %copy-start.9 = (bf16[296,128]{1,0:T(8,128)(2,1)}, bf16[296,128]{1,0:T(8,128)(2,1)S(1)}, u32[]{:S(2)}) copy-start(bf16[296,128]{1,0:T(8,128)(2,1)S(1)} %collective-permute-done.9) | copy-start | bytes 227332
  55.0 4.5 %collective-permute-start.7 = (bf16[296,128]{1,0:T(8,128)(2,1)S(1)}, bf16[296,128]{1,0:T(8,128)(2,1)S(1)}, u32[]{:S(2)}, u32[]{:S(2)}) collective-permute-start(bf16[296,128]{1,0:T(8,128)(2,1)S(1)} %concatenate.36), channel_id=1, source_target_pairs={{64,0},{128,64},{192,128},{0,192},{65,1},{129,65},{193,129},{1,193... | collective-permute-start | bytes 227336 | tf_op jit(solution)/shard_map/ppermute | solution.py:12
  56.4 8.5 %copy-start.10 = (bf16[296,128]{1,0:T(8,128)(2,1)}, bf16[296,128]{1,0:T(8,128)(2,1)S(1)}, u32[]{:S(2)}) copy-start(bf16[296,128]{1,0:T(8,128)(2,1)S(1)} %collective-permute-done.8) | copy-start | bytes 227332
  56.4 8.5 %collective-permute-start.4 = (bf16[4,4,72,128]{3,2,1,0:T(8,128)(2,1)S(1)}, bf16[4,4,72,128]{3,2,1,0:T(8,128)(2,1)S(1)}, u32[]{:S(2)}, u32[]{:S(2)}) collective-permute-start(bf16[4,4,72,128]{3,2,1,0:T(8,128)(2,1)S(1)} %get-tuple-element.26), channel_id=1, source_target_pairs={{64,0},{128,64},{192,128},{0,192},{65,1},{129,65},{193,129},{1,193... | collective-permute-start | bytes 884744 | tf_op jit(solution)/shard_map/ppermute | solution.py:12
  59.5 5.4 %copy-start.11 = (bf16[296,128]{1,0:T(8,128)(2,1)}, bf16[296,128]{1,0:T(8,128)(2,1)S(1)}, u32[]{:S(2)}) copy-start(bf16[296,128]{1,0:T(8,128)(2,1)S(1)} %collective-permute-done.7) | copy-start | bytes 227332
  59.6 7.3 %collective-permute-start.12 = (bf16[4,288,128]{2,1,0:T(8,128)(2,1)S(1)}, bf16[4,288,128]{2,1,0:T(8,128)(2,1)S(1)}, u32[]{:S(2)}, u32[]{:S(2)}) collective-permute-start(bf16[4,288,128]{2,1,0:T(8,128)(2,1)S(1)} %slice.137), channel_id=1, source_target_pairs={{48,0},{0,16},{16,32},{32,48},{49,1},{1,17},{17,33},{33,49},{50,2}... | collective-permute-start | bytes 884744 | tf_op jit(solution)/shard_map/ppermute | solution.py:12
  59.9 8.7 %collective-permute-start.11 = (bf16[4,288,128]{2,1,0:T(8,128)(2,1)S(1)}, bf16[4,288,128]{2,1,0:T(8,128)(2,1)S(1)}, u32[]{:S(2)}, u32[]{:S(2)}) collective-permute-start(bf16[4,288,128]{2,1,0:T(8,128)(2,1)S(1)} %slice.137), channel_id=1, source_target_pairs={{32,0},{48,16},{0,32},{16,48},{33,1},{49,17},{1,33},{17,49},{34,2}... | collective-permute-start | bytes 884744 | tf_op jit(solution)/shard_map/ppermute | solution.py:12
  62.8 8.8 %collective-permute-start.10 = (bf16[4,288,128]{2,1,0:T(8,128)(2,1)S(1)}, bf16[4,288,128]{2,1,0:T(8,128)(2,1)S(1)}, u32[]{:S(2)}, u32[]{:S(2)}) collective-permute-start(bf16[4,288,128]{2,1,0:T(8,128)(2,1)S(1)} %slice.137), channel_id=1, source_target_pairs={{16,0},{32,16},{48,32},{0,48},{17,1},{33,17},{49,33},{1,49},{18,2}... | collective-permute-start | bytes 884744 | tf_op jit(solution)/shard_map/ppermute | solution.py:12
  74.2 2.0 %copy-start.3 = (bf16[4,8,72,512]{3,2,1,0:T(8,128)(2,1)S(1)}, bf16[4,8,72,512]{3,2,1,0:T(8,128)(2,1)}, u32[]{:S(2)}) copy-start(bf16[4,8,72,512]{3,2,1,0:T(8,128)(2,1)} %get-tuple-element.11) | copy-start | bytes 7077892
  75.7 5.1 %copy-start.1 = (bf16[4,8,72,512]{3,2,1,0:T(8,128)(2,1)}, bf16[4,8,72,512]{3,2,1,0:T(8,128)(2,1)S(1)}, u32[]{:S(2)}) copy-start(bf16[4,8,72,512]{3,2,1,0:T(8,128)(2,1)S(1)} %constant_dynamic-update-slice_fusion) | copy-start | bytes 7077892
  75.7 32.2 %collective-permute-start.27 = (bf16[4,8,72,512]{3,2,1,0:T(8,128)(2,1)S(1)}, bf16[4,8,72,512]{3,2,1,0:T(8,128)(2,1)}, u32[]{:S(2)}, u32[]{:S(2)}) collective-permute-start(bf16[4,8,72,512]{3,2,1,0:T(8,128)(2,1)S(1)} %constant_dynamic-update-slice_fusion), channel_id=1, source_target_pairs={{1,0},{0,1},{3,2},{2,3},{5,4},{4,5},{7,6},{6,7},{9,8},{8,9},{11,10... | collective-permute-start | bytes 7077896 | tf_op jit(solution)/shard_map/ppermute | solution.py:12
  76.2 6.4 %copy-start.8 = (bf16[296,128]{1,0:T(8,128)(2,1)S(1)}, bf16[296,128]{1,0:T(8,128)(2,1)}, u32[]{:S(2)}) copy-start(bf16[296,128]{1,0:T(8,128)(2,1)} %copy-done.7) | copy-start | bytes 227332
  80.9 1.8 copy-start.2
  82.6 2.9 %collective-permute-start.13 = (f32[512,512]{1,0:T(8,128)}, f32[512,512]{1,0:T(8,128)S(1)}, u32[]{:S(2)}, u32[]{:S(2)}) collective-permute-start(f32[512,512]{1,0:T(8,128)} %slice.139), channel_id=1, source_target_pairs={{1,0},{0,1},{3,2},{2,3},{5,4},{4,5},{7,6},{6,7},{9,8},{8,9},{11,10... | collective-permute-start | bytes 3145736 | tf_op jit(solution)/shard_map/ppermute | solution.py:12
  87.8 11.3 %all-to-all-start.1 = ((f32[16,2,4,128]{3,2,1,0:T(4,128)}), f32[16,2,4,128]{3,2,1,0:T(4,128)S(1)}, u32[]{:S(2)}, u32[]{:S(2)}) async-start(f32[16,2,4,128]{3,2,1,0:T(4,128)} %broadcast_in_dim.31), calls=%async_computation.1 | async-start | bytes 131072 | tf_op jit(solution)/shard_map/all_to_all | solution.py:26
  99.7 14.5 %all-to-all-start.2 = ((f32[16,2,4,128]{3,2,1,0:T(4,128)}), f32[16,2,4,128]{3,2,1,0:T(4,128)S(1)}, u32[]{:S(2)}, u32[]{:S(2)}) async-start(f32[16,2,4,128]{3,2,1,0:T(4,128)} %broadcast_in_dim.32), calls=%async_computation.2 | async-start | bytes 131072 | tf_op jit(solution)/shard_map/all_to_all | solution.py:26
  114.3 2.2 %copy-start = (bf16[4,8,1,72,512]{4,3,1,0,2:T(8,128)(2,1)S(1)}, bf16[4,8,1,72,512]{4,3,1,0,2:T(8,128)(2,1)}, u32[]{:S(2)}) copy-start(bf16[4,8,1,72,512]{4,3,1,0,2:T(8,128)(2,1)} %get-tuple-element.10) | copy-start | bytes 7077892
  116.2 5.6 %copy-start.5 = (bf16[512,512]{1,0:T(8,128)(2,1)}, bf16[512,512]{1,0:T(8,128)(2,1)S(1)}, u32[]{:S(2)}) copy-start(bf16[512,512]{1,0:T(8,128)(2,1)S(1)} %fusion.14) | copy-start | bytes 1572868
  116.2 5.5 %collective-permute-start.14 = (bf16[512,512]{1,0:T(8,128)(2,1)S(1)}, bf16[512,512]{1,0:T(8,128)(2,1)S(1)}, u32[]{:S(2)}, u32[]{:S(2)}) collective-permute-start(bf16[512,512]{1,0:T(8,128)(2,1)S(1)} %fusion.14), channel_id=1, source_target_pairs={{1,0},{0,1},{3,2},{2,3},{5,4},{4,5},{7,6},{6,7},{9,8},{8,9},{11,10... | collective-permute-start | bytes 1572872 | tf_op jit(solution)/shard_map/ppermute | solution.py:12
  121.7 2.0 %copy-start.4 = (bf16[4,8,72,512]{3,2,1,0:T(8,128)(2,1)S(1)}, bf16[4,8,72,512]{3,2,1,0:T(8,128)(2,1)}, u32[]{:S(2)}) copy-start(bf16[4,8,72,512]{3,2,1,0:T(8,128)(2,1)} %get-tuple-element.11) | copy-start | bytes 7077892
  128.5 9.9 %collective-permute-start.21 = (bf16[4,72,4,128]{3,1,0,2:T(8,128)(2,1)S(1)}, bf16[4,72,4,128]{3,1,0,2:T(8,128)(2,1)S(1)}, u32[]{:S(2)}, u32[]{:S(2)}) collective-permute-start(bf16[4,72,4,128]{3,1,0,2:T(8,128)(2,1)S(1)} %get-tuple-element.16), channel_id=1, source_target_pairs={{0,16},{16,32},{32,48},{48,0},{1,17},{17,33},{33,49},{49,1},{2,18}... | collective-permute-start | bytes 884744 | tf_op jit(solution)/shard_map/ppermute | solution.py:16
  129.4 11.4 %collective-permute-start.22 = (bf16[4,72,4,128]{3,1,0,2:T(8,128)(2,1)S(1)}, bf16[4,72,4,128]{3,1,0,2:T(8,128)(2,1)S(1)}, u32[]{:S(2)}, u32[]{:S(2)}) collective-permute-start(bf16[4,72,4,128]{3,1,0,2:T(8,128)(2,1)S(1)} %get-tuple-element.18), channel_id=1, source_target_pairs={{0,32},{16,48},{32,0},{48,16},{1,33},{17,49},{33,1},{49,17},{2,34}... | collective-permute-start | bytes 884744 | tf_op jit(solution)/shard_map/ppermute | solution.py:16
  132.1 14.2 %collective-permute-start.23 = (bf16[4,72,4,128]{3,1,0,2:T(8,128)(2,1)S(1)}, bf16[4,72,4,128]{3,1,0,2:T(8,128)(2,1)S(1)}, u32[]{:S(2)}, u32[]{:S(2)}) collective-permute-start(bf16[4,72,4,128]{3,1,0,2:T(8,128)(2,1)S(1)} %get-tuple-element.17), channel_id=1, source_target_pairs={{0,48},{16,0},{32,16},{48,32},{1,49},{17,1},{33,17},{49,33},{2,50}... | collective-permute-start | bytes 884744 | tf_op jit(solution)/shard_map/ppermute | solution.py:16
  133.4 15.7 %collective-permute-start.17 = (bf16[4,4,72,128]{3,2,1,0:T(8,128)(2,1)S(1)}, bf16[4,4,72,128]{3,2,1,0:T(8,128)(2,1)S(1)}, u32[]{:S(2)}, u32[]{:S(2)}) collective-permute-start(bf16[4,4,72,128]{3,2,1,0:T(8,128)(2,1)S(1)} %get-tuple-element.14), channel_id=1, source_target_pairs={{0,192},{64,0},{128,64},{192,128},{1,193},{65,1},{129,65},{193,129... | collective-permute-start | bytes 884744 | tf_op jit(solution)/shard_map/ppermute | solution.py:16
  134.5 14.9 %collective-permute-start.16 = (bf16[4,4,72,128]{3,2,1,0:T(8,128)(2,1)S(1)}, bf16[4,4,72,128]{3,2,1,0:T(8,128)(2,1)S(1)}, u32[]{:S(2)}, u32[]{:S(2)}) collective-permute-start(bf16[4,4,72,128]{3,2,1,0:T(8,128)(2,1)S(1)} %get-tuple-element.15), channel_id=1, source_target_pairs={{0,128},{64,192},{128,0},{192,64},{1,129},{65,193},{129,1},{193,65... | collective-permute-start | bytes 884744 | tf_op jit(solution)/shard_map/ppermute | solution.py:16
  138.4 12.2 %collective-permute-start.15 = (bf16[4,4,72,128]{3,2,1,0:T(8,128)(2,1)S(1)}, bf16[4,4,72,128]{3,2,1,0:T(8,128)(2,1)S(1)}, u32[]{:S(2)}, u32[]{:S(2)}) collective-permute-start(bf16[4,4,72,128]{3,2,1,0:T(8,128)(2,1)S(1)} %get-tuple-element.13), channel_id=1, source_target_pairs={{0,64},{64,128},{128,192},{192,0},{1,65},{65,129},{129,193},{193,1... | collective-permute-start | bytes 884744 | tf_op jit(solution)/shard_map/ppermute | solution.py:16
  146.4 10.3 %collective-permute-start.26 = (bf16[4,72,128]{2,1,0:T(8,128)(2,1)S(1)}, bf16[4,72,128]{2,1,0:T(8,128)(2,1)S(1)}, u32[]{:S(2)}, u32[]{:S(2)}) collective-permute-start(bf16[4,72,128]{2,1,0:T(8,128)(2,1)S(1)} %get-tuple-element.23), channel_id=1, source_target_pairs={{0,192},{64,0},{128,64},{192,128},{1,193},{65,1},{129,65},{193,129... | collective-permute-start | bytes 221192 | tf_op jit(solution)/shard_map/ppermute | solution.py:16
  147.7 10.9 %collective-permute-start.25 = (bf16[4,72,128]{2,1,0:T(8,128)(2,1)S(1)}, bf16[4,72,128]{2,1,0:T(8,128)(2,1)S(1)}, u32[]{:S(2)}, u32[]{:S(2)}) collective-permute-start(bf16[4,72,128]{2,1,0:T(8,128)(2,1)S(1)} %get-tuple-element.24), channel_id=1, source_target_pairs={{0,128},{64,192},{128,0},{192,64},{1,129},{65,193},{129,1},{193,65... | collective-permute-start | bytes 221192 | tf_op jit(solution)/shard_map/ppermute | solution.py:16
  149.1 17.7 %copy-start.6 = (bf16[512,512]{1,0:T(8,128)(2,1)S(1)}, bf16[512,512]{1,0:T(8,128)(2,1)}, u32[]{:S(2)}) copy-start(bf16[512,512]{1,0:T(8,128)(2,1)} %copy-done.5) | copy-start | bytes 1572868
  149.1 9.4 %collective-permute-start.24 = (bf16[4,72,128]{2,1,0:T(8,128)(2,1)S(1)}, bf16[4,72,128]{2,1,0:T(8,128)(2,1)S(1)}, u32[]{:S(2)}, u32[]{:S(2)}) collective-permute-start(bf16[4,72,128]{2,1,0:T(8,128)(2,1)S(1)} %get-tuple-element.22), channel_id=1, source_target_pairs={{0,64},{64,128},{128,192},{192,0},{1,65},{65,129},{129,193},{193,1... | collective-permute-start | bytes 221192 | tf_op jit(solution)/shard_map/ppermute | solution.py:16
  150.8 7.9 %collective-permute-start.20 = (bf16[4,72,128]{2,1,0:T(8,128)(2,1)S(1)}, bf16[4,72,128]{2,1,0:T(8,128)(2,1)S(1)}, u32[]{:S(2)}, u32[]{:S(2)}) collective-permute-start(bf16[4,72,128]{2,1,0:T(8,128)(2,1)S(1)} %get-tuple-element.20), channel_id=1, source_target_pairs={{0,48},{16,0},{32,16},{48,32},{1,49},{17,1},{33,17},{49,33},{2,50}... | collective-permute-start | bytes 221192 | tf_op jit(solution)/shard_map/ppermute | solution.py:16
  156.7 5.9 %collective-permute-start.19 = (bf16[4,72,128]{2,1,0:T(8,128)(2,1)S(1)}, bf16[4,72,128]{2,1,0:T(8,128)(2,1)S(1)}, u32[]{:S(2)}, u32[]{:S(2)}) collective-permute-start(bf16[4,72,128]{2,1,0:T(8,128)(2,1)S(1)} %get-tuple-element.21), channel_id=1, source_target_pairs={{0,32},{16,48},{32,0},{48,16},{1,33},{17,49},{33,1},{49,17},{2,34}... | collective-permute-start | bytes 221192 | tf_op jit(solution)/shard_map/ppermute | solution.py:16
  156.7 5.9 %collective-permute-start.18 = (bf16[4,72,128]{2,1,0:T(8,128)(2,1)S(1)}, bf16[4,72,128]{2,1,0:T(8,128)(2,1)S(1)}, u32[]{:S(2)}, u32[]{:S(2)}) collective-permute-start(bf16[4,72,128]{2,1,0:T(8,128)(2,1)S(1)} %get-tuple-element.19), channel_id=1, source_target_pairs={{0,16},{16,32},{32,48},{48,0},{1,17},{17,33},{33,49},{49,1},{2,18}... | collective-permute-start | bytes 221192 | tf_op jit(solution)/shard_map/ppermute | solution.py:16
  163.4 14.2 %all-to-all-start.3 = ((f32[8,72,128]{2,1,0:T(8,128)}), f32[8,72,128]{2,1,0:T(8,128)S(1)}, u32[]{:S(2)}, u32[]{:S(2)}) async-start(f32[8,72,128]{2,1,0:T(8,128)} %pad_maximum_fusion.7), calls=%async_computation.3 | async-start | bytes 589824 | tf_op jit(solution)/shard_map/all_to_all | solution.py:101

commit v2 on v1

v2 whole, which is shorter than its diff:
```python
import jax
import jax.numpy as jnp
from jax import lax
from jax.experimental import pallas as pl
from jax.experimental.pallas import tpu as pltpu
from jax.sharding import Mesh, PartitionSpec as P

CAP = 30
F32, BF16 = jnp.float32, jnp.bfloat16
X, Y, Z, C = 4, 4, 8, 2


def flip(array, axis, size, change):
    return lax.ppermute(array, axis, [(i, i ^ change) for i in range(size)])


def reordered(array, own, dim):
    return jnp.concatenate([lax.dynamic_slice_in_dim(array, own ^ k, 1, dim) for k in range(4)], dim)


def at_once(*arrays):
    return lax.optimization_barrier(arrays)


def spread(array, axes, size):
    copies = jnp.broadcast_to(array[None], (size,) + array.shape)
    return lax.all_to_all(copies, axes, 0, 0, tiled=True)


def digits(targets):
    parts = [targets // 65536, (targets // 256) % 256, targets % 256]
    return jnp.concatenate([jnp.stack(parts), jnp.zeros((5, targets.shape[0]), jnp.int32)]).astype(BF16)


def undigits(rows):
    parts = rows.astype(jnp.int32)
    return parts[:, 0] * 65536 + parts[:, 1] * 256 + parts[:, 2]


VMEM_LIMIT = 18 * 1024 * 1024


def fetch_columns(meta_ref, sources, slots, sems, wide):
    copies = []
    for step in range(Y):
        columns = pl.ds(pl.multiple_of(meta_ref[step], 128), wide)
        row = []
        for place, ref in enumerate(sources):
            row.append(pltpu.make_async_copy(ref.at[:, columns], slots.at[step, place], sems.at[step, place]))
        copies.append(row)
    for row in copies:
        for copy in row:
            copy.start()
    return copies


def in_hbm(arrays):
    return [pltpu.with_memory_space_constraint(array, pltpu.HBM) for array in arrays]


def logits_kernel(meta_ref, own_ref, other_ref, *refs):
    a_refs, b_refs = refs[:5], refs[5:10]
    mine_ref, theirs_ref, ht_ref, slots, tall, sems, piece_sems, out_sem = refs[10:]
    part, rows = a_refs[0].shape[1:]
    wide = slots.shape[-1]
    shift = pl.multiple_of(meta_ref[Y], 64)
    pieces = ((0, 0, Y), (1, 0, Y), (3, 0, Y), (2, 0, Y // 2), (2, Y // 2, Y // 2))
    a_copies, b_copies = [], [[] for _ in range(Y)]
    for i, (place, first, count) in enumerate(pieces):
        target = tall.at[pl.ds(first, count), pl.ds(shift, part), pl.ds(place * rows, rows)]
        a_copies.append(pltpu.make_async_copy(a_refs[i], target, piece_sems.at[Y, i]))
        for k in range(count):
            target = tall.at[place, pl.ds(shift + part, part), pl.ds((first + k) * rows, rows)]
            b_copies[place].append(pltpu.make_async_copy(b_refs[i].at[k], target, piece_sems.at[place, first + k]))
    for copy in a_copies:
        copy.start()
    for row in b_copies:
        for copy in row:
            copy.start()
    copies = fetch_columns(meta_ref, (own_ref, other_ref), slots, sems, wide)
    edge = wide - 2 * part
    zeros = jnp.zeros((edge, X * rows), tall.dtype)
    empty = pl.multiple_of(2 * part * (1 - meta_ref[Y] // edge), 64)
    for step in range(Y):
        tall[step, pl.ds(empty, edge)] = zeros
    for copy in a_copies:
        copy.wait()
    for step in range(Y):
        for copy in b_copies[step]:
            copy.wait()
        for place, out_ref in enumerate((mine_ref, theirs_ref)):
            copies[step][place].wait()
            term = jnp.dot(slots[step, place], tall[step], preferred_element_type=F32)
            if step == 0:
                out_ref[...] = term
            else:
                out_ref[...] += term
    keep = pltpu.make_async_copy(tall.at[:, pl.ds(shift, 2 * part)], ht_ref, out_sem)
    keep.start()
    keep.wait()


def logits_of(meta, own, other, a_pieces, b_pieces, wide):
    voc = own.shape[0]
    part, rows = a_pieces[0].shape[1:]
    vmem = pl.BlockSpec(memory_space=pltpu.VMEM)
    hbm = pl.BlockSpec(memory_space=pltpu.HBM)
    square = jax.ShapeDtypeStruct((voc, X * rows), F32)
    return pl.pallas_call(
        logits_kernel,
        out_shape=(square, square, pltpu.HBM((Y, 2 * part, X * rows), BF16)),
        in_specs=[pl.BlockSpec(memory_space=pltpu.SMEM), hbm, hbm] + [hbm] * 10,
        out_specs=(vmem, vmem, hbm),
        scratch_shapes=[
            pltpu.VMEM((Y, 2, voc, wide), BF16),
            pltpu.VMEM((Y, wide, X * rows), BF16),
            pltpu.SemaphoreType.DMA((Y, 2)),
            pltpu.SemaphoreType.DMA((Y + 1, 5)),
            pltpu.SemaphoreType.DMA,
        ],
        compiler_params=pltpu.CompilerParams(vmem_limit_bytes=VMEM_LIMIT),
        cost_estimate=pl.CostEstimate(
            flops=4 * Y * voc * wide * X * rows, bytes_accessed=4 * Y * voc * wide, transcendentals=0
        ),
    )(meta, *in_hbm([own, other, *a_pieces, *b_pieces]))


def turn_kernel(meta_ref, own_ref, other_ref, out_ref, slots, whole, made, sems, out_sems):
    part = out_ref.shape[2]
    voc, wide = slots.shape[2:]
    copies, outs = [], []
    for i in range(2 * Y):
        columns = pl.ds(pl.multiple_of(meta_ref[i], 128), wide)
        row = [
            pltpu.make_async_copy(ref.at[:, columns], slots.at[i, place], sems.at[i, place])
            for place, ref in enumerate((own_ref, other_ref))
        ]
        copies.append(row)
    for row in copies:
        for copy in row:
            copy.start()
    for i in range(2 * Y):
        shift = pl.multiple_of(meta_ref[2 * Y + i // Y], 32)
        for place in range(2):
            copies[i][place].wait()
            whole[i % 2, place] = slots[i, place].T
            made[i, :, place * voc : (place + 1) * voc] = whole[i % 2, place, pl.ds(shift, part)]
        out = pltpu.make_async_copy(made.at[i], out_ref.at[i % Y, i // Y], out_sems.at[i])
        out.start()
        outs.append(out)
    for out in outs:
        out.wait()


def turned_weights(meta, own, other, part, wide):
    voc = own.shape[0]
    hbm = pl.BlockSpec(memory_space=pltpu.HBM)
    return pl.pallas_call(
        turn_kernel,
        out_shape=pltpu.HBM((Y, 2, part, 2 * voc), BF16),
        in_specs=[pl.BlockSpec(memory_space=pltpu.SMEM), hbm, hbm],
        out_specs=hbm,
        scratch_shapes=[
            pltpu.VMEM((2 * Y, 2, voc, wide), BF16),
            pltpu.VMEM((2, 2, wide, voc), BF16),
            pltpu.VMEM((2 * Y, part, 2 * voc), BF16),
            pltpu.SemaphoreType.DMA((2 * Y, 2)),
            pltpu.SemaphoreType.DMA((2 * Y,)),
        ],
        compiler_params=pltpu.CompilerParams(vmem_limit_bytes=VMEM_LIMIT),
        cost_estimate=pl.CostEstimate(flops=0, bytes_accessed=12 * Y * voc * wide, transcendentals=0),
    )(meta, *in_hbm([own, other]))


def product(wt, dl, dlo):
    voc = dl.shape[0]
    return jnp.dot(wt[:, :voc], dl, preferred_element_type=F32) + jnp.dot(
        wt[:, voc:], dlo, preferred_element_type=F32
    )


FIRST_BLOCKS = ((0, 0), (1, 0), (2, 0), (3, 0), (2, 1))
REST_BLOCKS = ((0, 0), (1, 0), (2, 0), (3, 0), (0, 1), (1, 1), (3, 1))


def fetch_blocks(wt_ref, blocks, slots, sems):
    copies = []
    for i, (step, side) in enumerate(blocks):
        copies.append(pltpu.make_async_copy(wt_ref.at[step, side], slots.at[i], sems.at[i]))
    for copy in copies:
        copy.start()
    return copies


def first_kernel(wt_ref, dl_ref, dlo_ref, alo_ref, ahi_ref, blo_ref, bhi_ref, slots, sems):
    part, rows = alo_ref.shape[1:]
    copies = fetch_blocks(wt_ref, FIRST_BLOCKS, slots, sems)
    lanes = slice(2 * rows, 3 * rows)
    for i, (step, side) in enumerate(FIRST_BLOCKS):
        copies[i].wait()
        if side == 1:
            piece = product(slots[i], dl_ref[...], dlo_ref[...]).astype(BF16)
            blo_ref[...], bhi_ref[...] = piece[: part // 2], piece[part // 2 :]
            continue
        piece = product(slots[i], dl_ref[:, lanes], dlo_ref[:, lanes]).astype(BF16)
        if step < Y // 2:
            alo_ref[step] = piece
        else:
            ahi_ref[step - Y // 2] = piece


def rest_kernel(wt_ref, dl_ref, dlo_ref, *refs):
    a_outs, b_outs = refs[:3], refs[3:6]
    slots, sems = refs[6:]
    rows = a_outs[0].shape[2]
    copies = fetch_blocks(wt_ref, REST_BLOCKS, slots, sems)
    for i, (step, side) in enumerate(REST_BLOCKS):
        copies[i].wait()
        piece = product(slots[i], dl_ref[...], dlo_ref[...])
        if side == 1:
            b_outs[min(step, 2)][...] = piece
            continue
        for out_ref, place in zip(a_outs, (0, 1, 3)):
            out_ref[step] = piece[:, place * rows : (place + 1) * rows]


def gradient_call(kernel, blocks, outs, wt, dl, dlo):
    vmem = pl.BlockSpec(memory_space=pltpu.VMEM)
    part, wide = wt.shape[2:]
    count = len(blocks)
    return pl.pallas_call(
        kernel,
        out_shape=tuple(outs),
        in_specs=[pl.BlockSpec(memory_space=pltpu.HBM), vmem, vmem],
        out_specs=tuple([vmem] * len(outs)),
        scratch_shapes=[pltpu.VMEM((count, part, wide), BF16), pltpu.SemaphoreType.DMA((count,))],
        compiler_params=pltpu.CompilerParams(vmem_limit_bytes=VMEM_LIMIT),
        cost_estimate=pl.CostEstimate(
            flops=2 * count * part * wide * dl.shape[1], bytes_accessed=2 * count * part * wide, transcendentals=0
        ),
    )(*in_hbm([wt]), dl, dlo)


def weight_kernel(places_ref, dl_ref, here_ref, there_ref, out_ref, both):
    half = here_ref.shape[1]
    core = places_ref[Y]
    both[pl.ds(pl.multiple_of(core * half, 64), half)] = here_ref[0]
    both[pl.ds(pl.multiple_of((1 - core) * half, 64), half)] = there_ref[0]
    over_last = (((1,), (1,)), ((), ()))
    out_ref[...] = lax.dot_general(dl_ref[...], both[...], over_last, preferred_element_type=F32).astype(BF16)


def weight_of(places, dl, here, there):
    voc, all_rows = dl.shape
    half = here.shape[1]
    one = pl.BlockSpec((1, half, all_rows), lambda i, places: (i, 0, 0))
    return pl.pallas_call(
        weight_kernel,
        out_shape=jax.ShapeDtypeStruct((voc, Y * 2 * half), BF16),
        grid_spec=pltpu.PrefetchScalarGridSpec(
            num_scalar_prefetch=1,
            grid=(Y,),
            in_specs=[pl.BlockSpec((voc, all_rows), lambda i, places: (0, 0)), one, one],
            out_specs=pl.BlockSpec((voc, 2 * half), lambda i, places: (0, places[i])),
            scratch_shapes=[pltpu.VMEM((2 * half, all_rows), BF16)],
        ),
        compiler_params=pltpu.CompilerParams(vmem_limit_bytes=VMEM_LIMIT),
        cost_estimate=pl.CostEstimate(
            flops=4 * Y * voc * half * all_rows, bytes_accessed=8 * Y * half * all_rows, transcendentals=0
        ),
    )(places, dl, *in_hbm([here, there]))


def per_device(hidden, weight, targets):
    rows, feats = hidden.shape
    voc = weight.shape[0]
    block = Z * C * feats
    half = block // 2
    part = half // 2
    pad = -half % 128
    wide = half + pad
    x, y, z, c = (lax.axis_index(name) for name in ("x", "y", "z", "c"))

    partner = flip(weight, "c", C, 1)
    along = spread(hidden.T, "z", Z)
    along, partner = lax.optimization_barrier((along, partner))
    along = along.reshape(2, Z // 2, feats, rows)
    keep = lax.dynamic_index_in_dim(along, c, 0, keepdims=False)
    give = lax.dynamic_index_in_dim(along, 1 - c, 0, keepdims=False)
    got = flip(give, "c", C, 1)
    along = jnp.stack([jnp.where(c == 0, keep, got), jnp.where(c == 0, got, keep)], 1).reshape(half, rows)
    a, b = along[:part], jnp.concatenate([along[part:], digits(targets)])
    a, b = at_once(a, b)
    a1, b1 = at_once(flip(a, "y", Y, 1), flip(b, "x", X, 1))
    a01, b01 = jnp.stack([a, a1]), jnp.stack([b, b1])
    a32, b32 = at_once(flip(a01, "y", Y, 3), flip(b01, "x", X, 3))
    a2 = jnp.stack([a01[0], a01[1], a32[1], a32[0]])
    b2 = jnp.stack([b01[0], b01[1], b32[1], b32[0]])
    tgt = undigits(b2[:, part:]).reshape(X * rows)
    a2, b2 = at_once(a2, b2[:, :part])
    ax1, by1, ax3, by3 = at_once(flip(a2, "x", X, 1), flip(b2, "y", Y, 1), flip(a2, "x", X, 3), flip(b2, "y", Y, 3))
    ax2lo, by2lo = flip(ax1[: Y // 2], "x", X, 3), flip(by1[: X // 2], "y", Y, 3)
    ax2hi, by2hi = flip(ax3[Y // 2 :], "x", X, 1), flip(by3[X // 2 :], "y", Y, 1)
    ax2lo, by2lo, ax2hi, by2hi = at_once(ax2lo, by2lo, ax2hi, by2hi)
    places = jnp.stack([y ^ step for step in range(Y)])
    meta = jnp.append(places * block + c * (half - pad), c * pad)

    logits, theirs, ht = logits_of(
        meta, weight, partner, [a2, ax1, ax3, ax2lo, ax2hi], [b2, by1, by3, by2lo, by2hi], wide
    )
    logits = logits + flip(theirs, "c", C, 1)
    capped = CAP * jnp.tanh(logits / CAP)
    offset = (((x * Y + y) * Z + z) * C + c) * voc
    columns = offset + jnp.arange(voc, dtype=jnp.int32)
    hit = columns[:, None] == tgt[None, :]
    stats = jnp.stack([jnp.sum(jnp.exp(capped - CAP), 0), jnp.sum(jnp.where(hit, capped, 0.0), 0)])
    stats, ht, weight, partner = at_once(stats, ht, weight, partner)
    other = flip(ht, "c", C, 1)
    lows = [c * half, c * half + part]
    windows = [places * block + low // 128 * 128 for low in lows]
    meta = jnp.concatenate(windows + [jnp.stack([low % 128 for low in lows])])
    wt = turned_weights(meta, weight, partner, part, -(-part // 128) * 128)
    stats = spread(stats.reshape(2, X, rows), ("z", "c"), Z * C).sum(0)
    stats = reordered(stats, x, 1)
    stats, wt, other = at_once(stats, wt, other)
    stats = spread(stats, ("x", "y"), X * Y).sum(0)
    stats = reordered(stats, x, 1)
    lse = CAP + jnp.log(stats[0])
    loss = lse[0] - stats[1, 0]
    probs = jnp.exp(capped - lse.reshape(1, X * rows))
    dlogits = ((probs - hit.astype(F32)) * (1.0 - (capped / CAP) ** 2)).astype(BF16)

    dlo = flip(dlogits, "c", C, 1)
    a_half = jax.ShapeDtypeStruct((Y // 2, part, rows), BF16)
    b_half = jax.ShapeDtypeStruct((part // 2, X * rows), BF16)
    a_lo, a_hi, b_lo, b_hi = gradient_call(
        first_kernel, FIRST_BLOCKS, [a_half] * 2 + [b_half] * 2, wt, dlogits, dlo
    )
    a_lo, b_lo, a_hi, b_hi = at_once(
        flip(a_lo, "x", X, 1), flip(b_lo, "y", Y, 1), flip(a_hi, "x", X, 3), flip(b_hi, "y", Y, 3)
    )
    a_kind = jax.ShapeDtypeStruct((Y, part, rows), F32)
    b_kind = jax.ShapeDtypeStruct((part, X * rows), F32)
    a0, a1, a3, b0, b1, b3 = gradient_call(
        rest_kernel, REST_BLOCKS, [a_kind] * 3 + [b_kind] * 3, wt, dlogits, dlo
    )
    a1 = jnp.concatenate([a1[: Y // 2], a1[Y // 2 :] + a_hi.astype(F32)]).astype(BF16)
    a3 = jnp.concatenate([a3[: Y // 2] + a_lo.astype(F32), a3[Y // 2 :]]).astype(BF16)
    b1 = jnp.concatenate([b1[: part // 2], b1[part // 2 :] + b_hi.astype(F32)]).astype(BF16)
    b3 = jnp.concatenate([b3[: part // 2] + b_lo.astype(F32), b3[part // 2 :]]).astype(BF16)
    a1, b1, a3, b3 = at_once(a1, b1, a3, b3)
    a1, b1, a3, b3 = at_once(flip(a1, "x", X, 1), flip(b1, "y", Y, 1), flip(a3, "x", X, 3), flip(b3, "y", Y, 3))
    a_own = a0 + a1.astype(F32) + a3.astype(F32)
    b_own = b0 + b1.astype(F32) + b3.astype(F32)
    a_out, b_out = at_once(a_own[1:3].astype(BF16), b_own[:, rows : 3 * rows].astype(BF16))
    a_in, b_in = at_once(flip(a_out, "y", Y, 1), flip(b_out, "x", X, 1))
    a_out = (a_own[3] + a_in[1].astype(F32)).astype(BF16)
    b_out = (b_own[:, 3 * rows :] + b_in[:, rows:].astype(F32)).astype(BF16)
    a_out, b_out = at_once(a_out, b_out)
    a_out, b_out = at_once(flip(a_out, "y", Y, 3), flip(b_out, "x", X, 3))
    a_sum = a_own[0] + a_in[0].astype(F32) + a_out.astype(F32)
    b_sum = b_own[:, :rows] + b_in[:, :rows].astype(F32) + b_out.astype(F32)
    total = jnp.concatenate([a_sum, b_sum]).reshape(Z // 2, C, feats, rows)
    mine = lax.dynamic_index_in_dim(total, c, 1, keepdims=False)
    theirs = flip(lax.dynamic_index_in_dim(total, 1 - c, 1, keepdims=False), "c", C, 1)
    by_z = jnp.concatenate([jnp.where(c == 0, mine, theirs), jnp.where(c == 0, theirs, mine)])
    by_z, dlogits = lax.optimization_barrier((by_z, dlogits))
    grad_weight = weight_of(jnp.append(places, c), dlogits, ht, other)
    grad_hidden = lax.all_to_all(by_z, "z", 0, 0, tiled=True).sum(0).astype(BF16).T
    return loss, grad_hidden, grad_weight


def solution(mesh):
    chips = Mesh(mesh.devices.reshape(X, Y, Z, C), ("x", "y", "z", "c"))
    in_specs = (P("x", ("y", "z", "c")), P(("x", "y", "z", "c"), None), P("x"))
    out_specs = (P("x"), P("x", ("y", "z", "c")), P(("x", "y", "z", "c"), None))
    return jax.shard_map(per_device, mesh=chips, in_specs=in_specs, out_specs=out_specs, check_vma=False)
```

time: 179 us -> 156 us (0.87)
  Pallas kernels: 0 us -> 28 us
  matrix products: 15.8 us -> 0 us
  local copies, waits for them, and re-layouts: 18.5 us -> 3.16 us
  other arithmetic: 19.4 us -> 6.99 us
  blocking collectives: 18.3 us -> 10.5 us
  starting transfers between devices: 52.8 us -> 50.2 us
  waiting for transfers between devices: 52.2 us -> 54.4 us
    pallas_call x0 -> x5, Pallas kernels: none -> 28 us  [the longest x2 7.82 us: gradient_call(): pl.pallas_call(kernel, out_shape=tuple(outs), in_specs=[pl.BlockSpec(memo...]
    dot_general x3 -> x0, matrix products: 15.8 us -> none  [the longest x1 6.62 us: per_device(): lax.dot_general(dlogits, full, (((1,), (1,)), ((), ())), preferred_elemen...]
    all_to_all x1, blocking collectives: 18.3 us -> 10.5 us  [spread(): return lax.all_to_all(copies, axes, 0, 0, tiled=True)]
    unnamed x29 -> x20, local copies, waits for them, and re-layouts: 8.3 us -> 0.7 us
    squeeze x1 -> x0, other arithmetic: 4.75 us -> none  [per_device(): mine = lax.dynamic_index_in_dim(wt, c, 2, keepdims=False)]
    ppermute x28 -> x30, starting transfers between devices: 37.7 us -> 33.3 us  [flip(): return lax.ppermute(array, axis, [(i, i ^ change) for i in range(size)])]
    another operation x5 -> x9, other arithmetic: 4.46 us -> 0.31 us  [the longest x1 4.09 us: per_device(): full = turned(jnp.stack([first, second], 2), (Y - y) % Y, Y, 0)]
    dynamic_slice x1 -> x2, local copies, waits for them, and re-layouts: 2.72 us -> 0.03 us  [reordered(): lax.dynamic_slice_in_dim(array, own ^ k, 1, dim)]
  transfers between devices with their start and end apart: 31 -> 33, of which waited for: 18 -> 24; matrix products, arithmetic and copies ran while one was open for 18% -> 2% of each run, Pallas kernels for 0% -> 11%
where the time goes in v2:
time: 156 us; the launch traced here: 154 us
  waiting for transfers between devices  54.4 us (35%)
  starting transfers between devices  50.2 us (32%)
  Pallas kernels  28 us (18%)
  blocking collectives  10.5 us (7%)
  other arithmetic  6.99 us (4%)
  local copies, waits for them, and re-layouts  3.16 us (2%)
    ppermute x30, waiting for transfers between devices, flip(): return lax.ppermute(array, axis, [(i, i ^ change) for i in range(size)])  37.5 us
    ppermute x30, starting transfers between devices, flip(): return lax.ppermute(array, axis, [(i, i ^ change) for i in range(size)])  33.3 us
    all_to_all x2, starting transfers between devices, spread(): return lax.all_to_all(copies, axes, 0, 0, tiled=True)  12.1 us
    all_to_all x2, waiting for transfers between devices, spread(): return lax.all_to_all(copies, axes, 0, 0, tiled=True)  12.1 us
    all_to_all x1, blocking collectives, spread(): return lax.all_to_all(copies, axes, 0, 0, tiled=True)  10.5 us
    pallas_call x2, Pallas kernels, gradient_call(): pl.pallas_call(kernel, out_shape=tuple(outs), in_specs=[pl.BlockSpec(memo...  7.82 us
    pallas_call x1, Pallas kernels, weight_of(): pl.pallas_call(weight_kernel, out_shape=jax.ShapeDtypeStruct((voc, Y * 2...  7.48 us
    pallas_call x1, Pallas kernels, logits_of(): pl.pallas_call(logits_kernel, out_shape=(square, square, pltpu.HBM((Y, 2...  7.29 us
  transfers between devices with their start and end apart: 33, of which 24 were waited for; matrix products, arithmetic and copies ran while one was open for 2% of the time, Pallas kernels for 11%

profile of v2, /device:TPU:8, one launch (start us, length us, event | category | flops | bytes accessed | tf_op | source)
XLA Modules:
  0.0 154.5 jit_solution(15496843378146980710)
XLA Ops:
  0.7 1.4 broadcast_in_dim.14
  2.1 8.5 %all-to-all-start = ((bf16[8,72,128]{2,1,0:T(8,128)(2,1)}), bf16[8,72,128]{2,1,0:T(8,128)(2,1)S(1)}, u32[]{:S(2)}, u32[]{:S(2)}) async-start(bf16[8,72,128]{2,1,0:T(8,128)(2,1)} %broadcast_in_dim.14), calls=%async_computation | async-start | bytes 294912 | tf_op jit(solution)/shard_map/all_to_all | solution.py:27
  10.6 10.1 %all-to-all-done = bf16[8,72,128]{2,1,0:T(8,128)(2,1)S(1)} async-done(((bf16[8,72,128]{2,1,0:T(8,128)(2,1)}), bf16[8,72,128]{2,1,0:T(8,128)(2,1)S(1)}, u32[]{:S(2)}, u32[]{:S(2)}) %all-to-all-start) | async-done | bytes 147488 | tf_op jit(solution)/shard_map/all_to_all | solution.py:27
  22.2 1.6 %collective-permute-start.3 = (bf16[296,128]{1,0:T(8,128)(2,1)S(1)}, bf16[296,128]{1,0:T(8,128)(2,1)S(1)}, u32[]{:S(2)}, u32[]{:S(2)}) collective-permute-start(bf16[296,128]{1,0:T(8,128)(2,1)S(1)} %concatenate.46), channel_id=1, source_target_pairs={{0,64},{64,0},{128,192},{192,128},{1,65},{65,1},{129,193},{193,129... | collective-permute-start | bytes 227336 | tf_op jit(solution)/shard_map/ppermute | solution.py:14
  24.2 3.9 %collective-permute-done.2 = bf16[288,128]{1,0:T(8,128)(2,1)S(1)} collective-permute-done((bf16[288,128]{1,0:T(8,128)(2,1)S(1)}, bf16[288,128]{1,0:T(8,128)(2,1)S(1)}, u32[]{:S(2)}, u32[]{:S(2)}) %collective-permute-start.2) | collective-permute-done | bytes 73760 | tf_op jit(solution)/shard_map/ppermute | solution.py:14
  28.1 2.2 %collective-permute-start.5 = (bf16[2,296,128]{2,1,0:T(8,128)(2,1)S(1)}, bf16[2,296,128]{2,1,0:T(8,128)(2,1)S(1)}, u32[]{:S(2)}, u32[]{:S(2)}) collective-permute-start(bf16[2,296,128]{2,1,0:T(8,128)(2,1)S(1)} %pad_maximum_fusion.8), channel_id=1, source_target_pairs={{0,192},{64,128},{128,64},{192,0},{1,193},{65,129},{129,65},{193,1... | collective-permute-start | bytes 454664 | tf_op jit(solution)/shard_map/ppermute | solution.py:14
  30.3 1.7 %collective-permute-start.4 = (bf16[2,288,128]{2,1,0:T(8,128)(2,1)S(1)}, bf16[2,288,128]{2,1,0:T(8,128)(2,1)S(1)}, u32[]{:S(2)}, u32[]{:S(2)}) collective-permute-start(bf16[2,288,128]{2,1,0:T(8,128)(2,1)S(1)} %pad_maximum_fusion.9), channel_id=1, source_target_pairs={{0,48},{16,32},{32,16},{48,0},{1,49},{17,33},{33,17},{49,1},{2,50}... | collective-permute-start | bytes 442376 | tf_op jit(solution)/shard_map/ppermute | solution.py:14
  32.0 3.6 %collective-permute-done.4 = bf16[2,288,128]{2,1,0:T(8,128)(2,1)S(1)} collective-permute-done((bf16[2,288,128]{2,1,0:T(8,128)(2,1)S(1)}, bf16[2,288,128]{2,1,0:T(8,128)(2,1)S(1)}, u32[]{:S(2)}, u32[]{:S(2)}) %collective-permute-start.4) | collective-permute-done | bytes 147488 | tf_op jit(solution)/shard_map/ppermute | solution.py:14
  36.4 1.7 %collective-permute-start.7 = (bf16[4,288,128]{2,1,0:T(8,128)(2,1)S(1)}, bf16[4,288,128]{2,1,0:T(8,128)(2,1)S(1)}, u32[]{:S(2)}, u32[]{:S(2)}) collective-permute-start(bf16[4,288,128]{2,1,0:T(8,128)(2,1)S(1)} %slice.161.refs_5_), channel_id=1, source_target_pairs={{0,16},{16,0},{32,48},{48,32},{1,17},{17,1},{33,49},{49,33},{2,18}... | collective-permute-start | bytes 884744 | tf_op jit(solution)/shard_map/ppermute | solution.py:14
  38.7 2.4 %collective-permute-start.9 = (bf16[4,288,128]{2,1,0:T(8,128)(2,1)S(1)}, bf16[4,288,128]{2,1,0:T(8,128)(2,1)S(1)}, u32[]{:S(2)}, u32[]{:S(2)}) collective-permute-start(bf16[4,288,128]{2,1,0:T(8,128)(2,1)S(1)} %slice.161.refs_5_), channel_id=1, source_target_pairs={{0,48},{16,32},{32,16},{48,0},{1,49},{17,33},{33,17},{49,1},{2,50}... | collective-permute-start | bytes 884744 | tf_op jit(solution)/shard_map/ppermute | solution.py:14
  41.2 1.4 collective-permute-done.6.refs_1_
  43.1 2.9 %collective-permute-done.8.refs_2_ = bf16[4,288,128]{2,1,0:T(8,128)(2,1)S(1)} collective-permute-done((bf16[4,288,128]{2,1,0:T(8,128)(2,1)S(1)}, bf16[4,288,128]{2,1,0:T(8,128)(2,1)S(1)}, u32[]{:S(2)}, u32[]{:S(2)}) %collective-permute-start.8) | collective-permute-done | bytes 294944 | tf_op jit(solution)/shard_map/ppermute | solution.py:14
  46.0 2.5 %collective-permute-start.10 = (bf16[2,288,128]{2,1,0:T(8,128)(2,1)S(1)}, bf16[2,288,128]{2,1,0:T(8,128)(2,1)S(1)}, u32[]{:S(2)}, u32[]{:S(2)}) collective-permute-start(bf16[2,288,128]{2,1,0:T(8,128)(2,1)S(1)} %slice.130), channel_id=1, source_target_pairs={{0,192},{64,128},{128,64},{192,0},{1,193},{65,129},{129,65},{193,1... | collective-permute-start | bytes 442376 | tf_op jit(solution)/shard_map/ppermute | solution.py:14
  48.5 2.3 %collective-permute-start.11 = (bf16[2,288,128]{2,1,0:T(8,128)(2,1)S(1)}, bf16[2,288,128]{2,1,0:T(8,128)(2,1)S(1)}, u32[]{:S(2)}, u32[]{:S(2)}) collective-permute-start(bf16[2,288,128]{2,1,0:T(8,128)(2,1)S(1)} %slice.131), channel_id=1, source_target_pairs={{0,48},{16,32},{32,16},{48,0},{1,49},{17,33},{33,17},{49,1},{2,50}... | collective-permute-start | bytes 442376 | tf_op jit(solution)/shard_map/ppermute | solution.py:14
  50.9 1.0 collective-permute-start.12
  51.9 1.0 collective-permute-start.13
  53.0 1.0 collective-permute-done.11.refs_8_
  54.0 2.1 %collective-permute-done.12.refs_4_ = bf16[2,288,128]{2,1,0:T(8,128)(2,1)S(1)} collective-permute-done((bf16[2,288,128]{2,1,0:T(8,128)(2,1)S(1)}, bf16[2,288,128]{2,1,0:T(8,128)(2,1)S(1)}, u32[]{:S(2)}, u32[]{:S(2)}) %collective-permute-start.12) | collective-permute-done | bytes 147488 | tf_op jit(solution)/shard_map/ppermute | solution.py:14
  57.3 7.3 %shard_map.58 = (f32[512,512]{1,0:T(8,128)S(1)}, f32[512,512]{1,0:T(8,128)S(1)}, bf16[4,576,512]{2,1,0:T(8,128)(2,1)}) custom-call(s32[5]{0:T(128)S(1)} %pad_add_fusion.meta_ref, bf16[512,4608]{1,0:T(8,128)(2,1)} %own_ref.2, bf16[512,4608]{1,0:T(8,128)(2,1)} %collective-permute-done.other_ref, bf16[4,288,128]{2,1,0:T(8,128)(2,1)} %copy-done.2, ...), custom_call_target="tpu_custom_call" | custom-call | flops 2684354560 | bytes 5242880 | tf_op jit(solution)/shard_map/pallas_call | solution.py:109
  64.7 2.7 %collective-permute-done.14 = f32[512,512]{1,0:T(8,128)} collective-permute-done((f32[512,512]{1,0:T(8,128)S(1)}, f32[512,512]{1,0:T(8,128)}, u32[]{:S(2)}, u32[]{:S(2)}) %collective-permute-start.14) | collective-permute-done | bytes 1048608 | tf_op jit(solution)/shard_map/ppermute | solution.py:14
  67.4 1.6 %exponential_reduce_fusion = (f32[512]{0:T(512)S(1)}, f32[512]{0:T(512)S(1)}) fusion(f32[512,512]{1,0:T(8,128)S(1)} %get-tuple-element.81, f32[512,512]{1,0:T(8,128)} %collective-permute-done.14, s32[512]{0:T(512)S(1)} %bitcast.76, s32[512]{0:T(512)S(1)} %iota_add_fusion), kind=kLoop, calls=%fused_computation.6 | loop fusion | flops 2096128 | bytes 2105344 | tf_op jit(solution)/shard_map/reduce_sum | solution.py:316
  69.9 3.7 %all-to-all-start.1 = ((f32[16,2,4,128]{3,2,1,0:T(4,128)}), f32[16,2,4,128]{3,2,1,0:T(4,128)S(1)}, u32[]{:S(2)}, u32[]{:S(2)}) async-start(f32[16,2,4,128]{3,2,1,0:T(4,128)} %broadcast_in_dim.31), calls=%async_computation.1 | async-start | bytes 131072 | tf_op jit(solution)/shard_map/all_to_all | solution.py:27
  73.8 5.4 %shard_map.59.wt_ref = bf16[4,2,288,1024]{3,2,1,0:T(8,128)(2,1)} custom-call(s32[10]{0:T(128)S(1)} %pad_add_fusion.1.meta_ref, bf16[512,4608]{1,0:T(8,128)(2,1)} %own_ref.2, bf16[512,4608]{1,0:T(8,128)(2,1)} %collective-permute-done.other_ref), custom_call_target="tpu_custom_call" | custom-call | bytes 9437184 | tf_op jit(solution)/shard_map/pallas_call | solution.py:158
  79.2 2.0 %all-to-all-done.1 = f32[16,2,4,128]{3,2,1,0:T(4,128)S(1)} async-done(((f32[16,2,4,128]{3,2,1,0:T(4,128)}), f32[16,2,4,128]{3,2,1,0:T(4,128)S(1)}, u32[]{:S(2)}, u32[]{:S(2)}) %all-to-all-start.1) | async-done | bytes 65568 | tf_op jit(solution)/shard_map/all_to_all | solution.py:27
  81.3 10.5 %all_to_all.20 = f32[16,2,4,128]{3,2,1,0:T(4,128)S(1)} all-to-all(f32[16,2,4,128]{3,2,1,0:T(4,128)S(1)} %broadcast_in_dim.32), channel_id=1, replica_groups=mesh['x'=4,'y'=4,'z'=8,'c'=2] {'x','y'}, dimensions={0} | all-to-all | bytes 131072 | tf_op jit(solution)/shard_map/all_to_all | solution.py:27
  92.0 1.7 %fusion.3.dl_ref = bf16[512,512]{1,0:T(8,128)(2,1)S(1)} fusion(f32[512]{0:T(512)S(1)} %bitcast.78, s32[512]{0:T(512)S(1)} %bitcast.77, s32[512]{0:T(512)S(1)} %iota_add_fusion, f32[512,512]{1,0:T(8,128)S(1)} %get-tuple-element.81, f32[512,512]{1,0:T(8,128)} %collective-permute-done.14), kind=kLoop, calls=%fused_computation.5 | loop fusion | flops 2883584 | bytes 2627584 | tf_op jit(solution)/shard_map/convert_element_type | solution.py:331
  93.8 1.9 %collective-permute-done.16.dlo_ref = bf16[512,512]{1,0:T(8,128)(2,1)S(1)} collective-permute-done((bf16[512,512]{1,0:T(8,128)(2,1)S(1)}, bf16[512,512]{1,0:T(8,128)(2,1)S(1)}, u32[]{:S(2)}, u32[]{:S(2)}) %collective-permute-start.16) | collective-permute-done | bytes 524320 | tf_op jit(solution)/shard_map/ppermute | solution.py:14
  95.7 3.4 %shard_map.61 = (bf16[2,288,128]{2,1,0:T(8,128)(2,1)S(1)}, bf16[2,288,128]{2,1,0:T(8,128)(2,1)S(1)}, bf16[144,512]{1,0:T(8,128)(2,1)S(1)}, bf16[144,512]{1,0:T(8,128)(2,1)S(1)}) custom-call(bf16[4,2,288,1024]{3,2,1,0:T(8,128)(2,1)} %shard_map.59.wt_ref, bf16[512,512]{1,0:T(8,128)(2,1)S(1)} %fusion.3.dl_ref, bf16[512,512]{1,0:T(8,128)(2,1)S(1)} %collective-permute-done.16.dlo_ref), custom_call_target="tpu_custom_call" | custom-call | flops 1509949440 | bytes 2949120 | tf_op jit(solution)/shard_map/pallas_call | solution.py:231
  99.7 1.5 collective-permute-start.18
  101.1 1.3 collective-permute-start.19
  103.0 4.4 %shard_map.60 = (f32[4,288,128]{2,1,0:T(8,128)S(1)}, f32[4,288,128]{2,1,0:T(8,128)S(1)}, f32[4,288,128]{2,1,0:T(8,128)S(1)}, f32[288,512]{1,0:T(8,128)S(1)}, f32...) custom-call(bf16[4,2,288,1024]{3,2,1,0:T(8,128)(2,1)} %shard_map.59.wt_ref, bf16[512,512]{1,0:T(8,128)(2,1)S(1)} %fusion.3.dl_ref, ...), custom_call_target="tpu_custom_call" | custom-call | flops 2113929216 | bytes 4128768 | tf_op jit(solution)/shard_map/pallas_call | solution.py:231
  108.0 0.8 collective-permute-start.21
  108.7 1.7 %collective-permute-start.22 = (bf16[288,512]{1,0:T(8,128)(2,1)S(1)}, bf16[288,512]{1,0:T(8,128)(2,1)S(1)}, u32[]{:S(2)}, u32[]{:S(2)}) collective-permute-start(bf16[288,512]{1,0:T(8,128)(2,1)S(1)} %pad_maximum_fusion.3), channel_id=1, source_target_pairs={{0,16},{16,0},{32,48},{48,32},{1,17},{17,1},{33,49},{49,33},{2,18}... | collective-permute-start | bytes 884744 | tf_op jit(solution)/shard_map/ppermute | solution.py:14
  110.4 2.1 %collective-permute-start.23 = (bf16[4,288,128]{2,1,0:T(8,128)(2,1)S(1)}, bf16[4,288,128]{2,1,0:T(8,128)(2,1)S(1)}, u32[]{:S(2)}, u32[]{:S(2)}) collective-permute-start(bf16[4,288,128]{2,1,0:T(8,128)(2,1)S(1)} %pad_maximum_fusion.4), channel_id=1, source_target_pairs={{0,192},{64,128},{128,64},{192,0},{1,193},{65,129},{129,65},{193,1... | collective-permute-start | bytes 884744 | tf_op jit(solution)/shard_map/ppermute | solution.py:14
  112.6 0.9 collective-permute-start.24
  113.4 2.5 %collective-permute-done.21 = bf16[4,288,128]{2,1,0:T(8,128)(2,1)S(1)} collective-permute-done((bf16[4,288,128]{2,1,0:T(8,128)(2,1)S(1)}, bf16[4,288,128]{2,1,0:T(8,128)(2,1)S(1)}, u32[]{:S(2)}, u32[]{:S(2)}) %collective-permute-start.21) | collective-permute-done | bytes 294944 | tf_op jit(solution)/shard_map/ppermute | solution.py:14
  116.4 2.3 %collective-permute-done.23 = bf16[4,288,128]{2,1,0:T(8,128)(2,1)S(1)} collective-permute-done((bf16[4,288,128]{2,1,0:T(8,128)(2,1)S(1)}, bf16[4,288,128]{2,1,0:T(8,128)(2,1)S(1)}, u32[]{:S(2)}, u32[]{:S(2)}) %collective-permute-start.23) | collective-permute-done | bytes 294944 | tf_op jit(solution)/shard_map/ppermute | solution.py:14
  119.5 2.0 %collective-permute-start.25 = (bf16[2,288,128]{2,1,0:T(8,128)(2,1)S(1)}, bf16[2,288,128]{2,1,0:T(8,128)(2,1)S(1)}, u32[]{:S(2)}, u32[]{:S(2)}) collective-permute-start(bf16[2,288,128]{2,1,0:T(8,128)(2,1)S(1)} %slice.210), channel_id=1, source_target_pairs={{0,16},{16,0},{32,48},{48,32},{1,17},{17,1},{33,49},{49,33},{2,18}... | collective-permute-start | bytes 442376 | tf_op jit(solution)/shard_map/ppermute | solution.py:14
  122.1 2.7 %collective-permute-done.25 = bf16[2,288,128]{2,1,0:T(8,128)(2,1)S(1)} collective-permute-done((bf16[2,288,128]{2,1,0:T(8,128)(2,1)S(1)}, bf16[2,288,128]{2,1,0:T(8,128)(2,1)S(1)}, u32[]{:S(2)}, u32[]{:S(2)}) %collective-permute-start.25) | collective-permute-done | bytes 147488 | tf_op jit(solution)/shard_map/ppermute | solution.py:14
  124.8 1.9 %collective-permute-done.26 = bf16[288,256]{1,0:T(8,128)(2,1)S(1)} collective-permute-done((bf16[288,256]{1,0:T(8,128)(2,1)S(1)}, bf16[288,256]{1,0:T(8,128)(2,1)S(1)}, u32[]{:S(2)}, u32[]{:S(2)}) %collective-permute-start.26) | collective-permute-done | bytes 147488 | tf_op jit(solution)/shard_map/ppermute | solution.py:14
  126.8 1.5 collective-permute-start.27
  128.2 1.1 collective-permute-start.28
  129.4 1.9 %collective-permute-done.27 = bf16[288,128]{1,0:T(8,128)(2,1)S(1)} collective-permute-done((bf16[288,128]{1,0:T(8,128)(2,1)S(1)}, bf16[288,128]{1,0:T(8,128)(2,1)S(1)}, u32[]{:S(2)}, u32[]{:S(2)}) %collective-permute-start.27) | collective-permute-done | bytes 73760 | tf_op jit(solution)/shard_map/ppermute | solution.py:14
  131.2 2.6 %collective-permute-done.28 = bf16[288,128]{1,0:T(8,128)(2,1)S(1)} collective-permute-done((bf16[288,128]{1,0:T(8,128)(2,1)S(1)}, bf16[288,128]{1,0:T(8,128)(2,1)S(1)}, u32[]{:S(2)}, u32[]{:S(2)}) %collective-permute-start.28) | collective-permute-done | bytes 73760 | tf_op jit(solution)/shard_map/ppermute | solution.py:14
  134.0 1.4 collective-permute-done.29
  136.2 4.8 %all-to-all-start.3 = ((f32[8,72,128]{2,1,0:T(8,128)}), f32[8,72,128]{2,1,0:T(8,128)S(1)}, u32[]{:S(2)}, u32[]{:S(2)}) async-start(f32[8,72,128]{2,1,0:T(8,128)} %pad_maximum_fusion.7), calls=%async_computation.3 | async-start | bytes 589824 | tf_op jit(solution)/shard_map/all_to_all | solution.py:369
  141.5 7.5 %shard_map.62 = bf16[512,4608]{1,0:T(8,128)(2,1)} custom-call(s32[5]{0:T(128)S(1)} %concatenate.56.places_ref, bf16[512,512]{1,0:T(8,128)(2,1)S(1)} %fusion.3.dl_ref, bf16[4,576,512]{2,1,0:T(8,128)(2,1)} %get-tuple-element.87.here_ref, bf16[4,576,512]{2,1,0:T(8,128)(2,1)} %copy-done), custom_call_target="tpu_custom_call" | custom-call | flops 2415919104 | bytes 9437184 | tf_op jit(solution)/shard_map/pallas_call | solution.py:257
  149.0 4.8 %all-to-all-done.3 = f32[8,72,128]{2,1,0:T(8,128)S(1)} async-done(((f32[8,72,128]{2,1,0:T(8,128)}), f32[8,72,128]{2,1,0:T(8,128)S(1)}, u32[]{:S(2)}, u32[]{:S(2)}) %all-to-all-start.3) | async-done | bytes 294944 | tf_op jit(solution)/shard_map/all_to_all | solution.py:369
  (105 shorter events, 12.3 us)
Async XLA Ops:
  0.6 20.1 %collective-permute-start = (bf16[512,4608]{1,0:T(8,128)(2,1)}, bf16[512,4608]{1,0:T(8,128)(2,1)}, u32[]{:S(2)}, u32[]{:S(2)}) collective-permute-start(bf16[512,4608]{1,0:T(8,128)(2,1)} %own_ref.2), channel_id=1, source_target_pairs={{0,1},{1,0},{2,3},{3,2},{4,5},{5,4},{6,7},{7,6},{8,9},{9,8},{10,11... | collective-permute-start | bytes 14155784 | tf_op jit(solution)/shard_map/ppermute | solution.py:14
  2.1 18.5 %all-to-all-start = ((bf16[8,72,128]{2,1,0:T(8,128)(2,1)}), bf16[8,72,128]{2,1,0:T(8,128)(2,1)S(1)}, u32[]{:S(2)}, u32[]{:S(2)}) async-start(bf16[8,72,128]{2,1,0:T(8,128)(2,1)} %broadcast_in_dim.14), calls=%async_computation | async-start | bytes 294912 | tf_op jit(solution)/shard_map/all_to_all | solution.py:27
  20.7 1.4 collective-permute-start.1
  22.2 5.9 %collective-permute-start.3 = (bf16[296,128]{1,0:T(8,128)(2,1)S(1)}, bf16[296,128]{1,0:T(8,128)(2,1)S(1)}, u32[]{:S(2)}, u32[]{:S(2)}) collective-permute-start(bf16[296,128]{1,0:T(8,128)(2,1)S(1)} %concatenate.46), channel_id=1, source_target_pairs={{0,64},{64,0},{128,192},{192,128},{1,65},{65,1},{129,193},{193,129... | collective-permute-start | bytes 227336 | tf_op jit(solution)/shard_map/ppermute | solution.py:14
  23.7 4.4 %collective-permute-start.2 = (bf16[288,128]{1,0:T(8,128)(2,1)S(1)}, bf16[288,128]{1,0:T(8,128)(2,1)S(1)}, u32[]{:S(2)}, u32[]{:S(2)}) collective-permute-start(bf16[288,128]{1,0:T(8,128)(2,1)S(1)} %bitcast.66), channel_id=1, source_target_pairs={{0,16},{16,0},{32,48},{48,32},{1,17},{17,1},{33,49},{49,33},{2,18}... | collective-permute-start | bytes 221192 | tf_op jit(solution)/shard_map/ppermute | solution.py:14
  28.1 7.4 %collective-permute-start.5 = (bf16[2,296,128]{2,1,0:T(8,128)(2,1)S(1)}, bf16[2,296,128]{2,1,0:T(8,128)(2,1)S(1)}, u32[]{:S(2)}, u32[]{:S(2)}) collective-permute-start(bf16[2,296,128]{2,1,0:T(8,128)(2,1)S(1)} %pad_maximum_fusion.8), channel_id=1, source_target_pairs={{0,192},{64,128},{128,64},{192,0},{1,193},{65,129},{129,65},{193,1... | collective-permute-start | bytes 454664 | tf_op jit(solution)/shard_map/ppermute | solution.py:14
  30.3 5.2 %collective-permute-start.4 = (bf16[2,288,128]{2,1,0:T(8,128)(2,1)S(1)}, bf16[2,288,128]{2,1,0:T(8,128)(2,1)S(1)}, u32[]{:S(2)}, u32[]{:S(2)}) collective-permute-start(bf16[2,288,128]{2,1,0:T(8,128)(2,1)S(1)} %pad_maximum_fusion.9), channel_id=1, source_target_pairs={{0,48},{16,32},{32,16},{48,0},{1,49},{17,33},{33,17},{49,1},{2,50}... | collective-permute-start | bytes 442376 | tf_op jit(solution)/shard_map/ppermute | solution.py:14
  35.6 21.6 %copy-start.1 = (bf16[4,288,128]{2,1,0:T(8,128)(2,1)}, bf16[4,288,128]{2,1,0:T(8,128)(2,1)S(1)}, u32[]{:S(2)}) copy-start(bf16[4,288,128]{2,1,0:T(8,128)(2,1)S(1)} %slice.161.refs_5_) | copy-start | bytes 884740
  35.7 21.5 %copy-start.2 = (bf16[4,288,128]{2,1,0:T(8,128)(2,1)}, bf16[4,288,128]{2,1,0:T(8,128)(2,1)S(1)}, u32[]{:S(2)}) copy-start(bf16[4,288,128]{2,1,0:T(8,128)(2,1)S(1)} %pad_maximum_fusion.1.refs_0_) | copy-start | bytes 884740
  35.7 6.9 %collective-permute-start.6 = (bf16[4,288,128]{2,1,0:T(8,128)(2,1)S(1)}, bf16[4,288,128]{2,1,0:T(8,128)(2,1)S(1)}, u32[]{:S(2)}, u32[]{:S(2)}) collective-permute-start(bf16[4,288,128]{2,1,0:T(8,128)(2,1)S(1)} %pad_maximum_fusion.1.refs_0_), channel_id=1, source_target_pairs={{0,64},{64,0},{128,192},{192,128},{1,65},{65,1},{129,193},{193,129... | collective-permute-start | bytes 884744 | tf_op jit(solution)/shard_map/ppermute | solution.py:14
  36.4 6.7 %collective-permute-start.7 = (bf16[4,288,128]{2,1,0:T(8,128)(2,1)S(1)}, bf16[4,288,128]{2,1,0:T(8,128)(2,1)S(1)}, u32[]{:S(2)}, u32[]{:S(2)}) collective-permute-start(bf16[4,288,128]{2,1,0:T(8,128)(2,1)S(1)} %slice.161.refs_5_), channel_id=1, source_target_pairs={{0,16},{16,0},{32,48},{48,32},{1,17},{17,1},{33,49},{49,33},{2,18}... | collective-permute-start | bytes 884744 | tf_op jit(solution)/shard_map/ppermute | solution.py:14
  38.1 7.9 %collective-permute-start.8 = (bf16[4,288,128]{2,1,0:T(8,128)(2,1)S(1)}, bf16[4,288,128]{2,1,0:T(8,128)(2,1)S(1)}, u32[]{:S(2)}, u32[]{:S(2)}) collective-permute-start(bf16[4,288,128]{2,1,0:T(8,128)(2,1)S(1)} %pad_maximum_fusion.1.refs_0_), channel_id=1, source_target_pairs={{0,192},{64,128},{128,64},{192,0},{1,193},{65,129},{129,65},{193,1... | collective-permute-start | bytes 884744 | tf_op jit(solution)/shard_map/ppermute | solution.py:14
  38.7 7.3 %collective-permute-start.9 = (bf16[4,288,128]{2,1,0:T(8,128)(2,1)S(1)}, bf16[4,288,128]{2,1,0:T(8,128)(2,1)S(1)}, u32[]{:S(2)}, u32[]{:S(2)}) collective-permute-start(bf16[4,288,128]{2,1,0:T(8,128)(2,1)S(1)} %slice.161.refs_5_), channel_id=1, source_target_pairs={{0,48},{16,32},{32,16},{48,0},{1,49},{17,33},{33,17},{49,1},{2,50}... | collective-permute-start | bytes 884744 | tf_op jit(solution)/shard_map/ppermute | solution.py:14
  42.6 14.6 %copy-start.3 = (bf16[4,288,128]{2,1,0:T(8,128)(2,1)}, bf16[4,288,128]{2,1,0:T(8,128)(2,1)S(1)}, u32[]{:S(2)}) copy-start(bf16[4,288,128]{2,1,0:T(8,128)(2,1)S(1)} %collective-permute-done.6.refs_1_) | copy-start | bytes 884740
  43.1 13.0 %copy-start.4 = (bf16[4,288,128]{2,1,0:T(8,128)(2,1)}, bf16[4,288,128]{2,1,0:T(8,128)(2,1)S(1)}, u32[]{:S(2)}) copy-start(bf16[4,288,128]{2,1,0:T(8,128)(2,1)S(1)} %collective-permute-done.7.refs_6_) | copy-start | bytes 884740
  46.0 10.1 %copy-start.5 = (bf16[4,288,128]{2,1,0:T(8,128)(2,1)}, bf16[4,288,128]{2,1,0:T(8,128)(2,1)S(1)}, u32[]{:S(2)}) copy-start(bf16[4,288,128]{2,1,0:T(8,128)(2,1)S(1)} %collective-permute-done.8.refs_2_) | copy-start | bytes 884740
  46.0 10.1 %copy-start.6 = (bf16[4,288,128]{2,1,0:T(8,128)(2,1)}, bf16[4,288,128]{2,1,0:T(8,128)(2,1)S(1)}, u32[]{:S(2)}) copy-start(bf16[4,288,128]{2,1,0:T(8,128)(2,1)S(1)} %collective-permute-done.9.refs_7_) | copy-start | bytes 884740
  46.0 6.9 %collective-permute-start.10 = (bf16[2,288,128]{2,1,0:T(8,128)(2,1)S(1)}, bf16[2,288,128]{2,1,0:T(8,128)(2,1)S(1)}, u32[]{:S(2)}, u32[]{:S(2)}) collective-permute-start(bf16[2,288,128]{2,1,0:T(8,128)(2,1)S(1)} %slice.130), channel_id=1, source_target_pairs={{0,192},{64,128},{128,64},{192,0},{1,193},{65,129},{129,65},{193,1... | collective-permute-start | bytes 442376 | tf_op jit(solution)/shard_map/ppermute | solution.py:14
  48.5 5.5 %collective-permute-start.11 = (bf16[2,288,128]{2,1,0:T(8,128)(2,1)S(1)}, bf16[2,288,128]{2,1,0:T(8,128)(2,1)S(1)}, u32[]{:S(2)}, u32[]{:S(2)}) collective-permute-start(bf16[2,288,128]{2,1,0:T(8,128)(2,1)S(1)} %slice.131), channel_id=1, source_target_pairs={{0,48},{16,32},{32,16},{48,0},{1,49},{17,33},{33,17},{49,1},{2,50}... | collective-permute-start | bytes 442376 | tf_op jit(solution)/shard_map/ppermute | solution.py:14
  50.9 5.2 %collective-permute-start.12 = (bf16[2,288,128]{2,1,0:T(8,128)(2,1)S(1)}, bf16[2,288,128]{2,1,0:T(8,128)(2,1)S(1)}, u32[]{:S(2)}, u32[]{:S(2)}) collective-permute-start(bf16[2,288,128]{2,1,0:T(8,128)(2,1)S(1)} %slice.132), channel_id=1, source_target_pairs={{0,64},{64,0},{128,192},{192,128},{1,65},{65,1},{129,193},{193,129... | collective-permute-start | bytes 442376 | tf_op jit(solution)/shard_map/ppermute | solution.py:14
  51.9 5.3 %collective-permute-start.13 = (bf16[2,288,128]{2,1,0:T(8,128)(2,1)S(1)}, bf16[2,288,128]{2,1,0:T(8,128)(2,1)}, u32[]{:S(2)}, u32[]{:S(2)}) collective-permute-start(bf16[2,288,128]{2,1,0:T(8,128)(2,1)S(1)} %slice.133), channel_id=1, source_target_pairs={{0,16},{16,0},{32,48},{48,32},{1,17},{17,1},{33,49},{49,33},{2,18}... | collective-permute-start | bytes 442376 | tf_op jit(solution)/shard_map/ppermute | solution.py:14
  53.0 4.3 %copy-start.7 = (bf16[2,288,128]{2,1,0:T(8,128)(2,1)}, bf16[2,288,128]{2,1,0:T(8,128)(2,1)S(1)}, u32[]{:S(2)}) copy-start(bf16[2,288,128]{2,1,0:T(8,128)(2,1)S(1)} %collective-permute-done.10.refs_3_) | copy-start | bytes 442372
  54.0 2.1 %copy-start.8 = (bf16[2,288,128]{2,1,0:T(8,128)(2,1)}, bf16[2,288,128]{2,1,0:T(8,128)(2,1)S(1)}, u32[]{:S(2)}) copy-start(bf16[2,288,128]{2,1,0:T(8,128)(2,1)S(1)} %collective-permute-done.11.refs_8_) | copy-start | bytes 442372
  56.1 0.7 copy-start.9
  64.6 2.9 %collective-permute-start.14 = (f32[512,512]{1,0:T(8,128)S(1)}, f32[512,512]{1,0:T(8,128)}, u32[]{:S(2)}, u32[]{:S(2)}) collective-permute-start(f32[512,512]{1,0:T(8,128)S(1)} %get-tuple-element.82), channel_id=1, source_target_pairs={{0,1},{1,0},{2,3},{3,2},{4,5},{5,4},{6,7},{7,6},{8,9},{9,8},{10,11... | collective-permute-start | bytes 3145736 | tf_op jit(solution)/shard_map/ppermute | solution.py:14
  69.1 12.2 %collective-permute-start.15 = (bf16[4,576,512]{2,1,0:T(8,128)(2,1)}, bf16[4,576,512]{2,1,0:T(8,128)(2,1)S(1)}, u32[]{:S(2)}, u32[]{:S(2)}) collective-permute-start(bf16[4,576,512]{2,1,0:T(8,128)(2,1)} %get-tuple-element.87.here_ref), channel_id=1, source_target_pairs={{0,1},{1,0},{2,3},{3,2},{4,5},{5,4},{6,7},{7,6},{8,9},{9,8},{10,11... | collective-permute-start | bytes 7077896 | tf_op jit(solution)/shard_map/ppermute | solution.py:14
  69.9 11.3 %all-to-all-start.1 = ((f32[16,2,4,128]{3,2,1,0:T(4,128)}), f32[16,2,4,128]{3,2,1,0:T(4,128)S(1)}, u32[]{:S(2)}, u32[]{:S(2)}) async-start(f32[16,2,4,128]{3,2,1,0:T(4,128)} %broadcast_in_dim.31), calls=%async_computation.1 | async-start | bytes 131072 | tf_op jit(solution)/shard_map/all_to_all | solution.py:27
  81.3 10.6 %copy-start = (bf16[4,576,512]{2,1,0:T(8,128)(2,1)}, bf16[4,576,512]{2,1,0:T(8,128)(2,1)S(1)}, u32[]{:S(2)}) copy-start(bf16[4,576,512]{2,1,0:T(8,128)(2,1)S(1)} %collective-permute-done.15.there_ref) | copy-start | bytes 7077892
  93.7 2.0 %collective-permute-start.16 = (bf16[512,512]{1,0:T(8,128)(2,1)S(1)}, bf16[512,512]{1,0:T(8,128)(2,1)S(1)}, u32[]{:S(2)}, u32[]{:S(2)}) collective-permute-start(bf16[512,512]{1,0:T(8,128)(2,1)S(1)} %fusion.3.dl_ref), channel_id=1, source_target_pairs={{0,1},{1,0},{2,3},{3,2},{4,5},{5,4},{6,7},{7,6},{8,9},{9,8},{10,11... | collective-permute-start | bytes 1572872 | tf_op jit(solution)/shard_map/ppermute | solution.py:14
  99.1 8.5 %collective-permute-start.17 = (bf16[2,288,128]{2,1,0:T(8,128)(2,1)S(1)}, bf16[2,288,128]{2,1,0:T(8,128)(2,1)S(1)}, u32[]{:S(2)}, u32[]{:S(2)}) collective-permute-start(bf16[2,288,128]{2,1,0:T(8,128)(2,1)S(1)} %get-tuple-element.92), channel_id=1, source_target_pairs={{0,64},{64,0},{128,192},{192,128},{1,65},{65,1},{129,193},{193,129... | collective-permute-start | bytes 442376 | tf_op jit(solution)/shard_map/ppermute | solution.py:14
  99.7 7.9 %collective-permute-start.18 = (bf16[144,512]{1,0:T(8,128)(2,1)S(1)}, bf16[144,512]{1,0:T(8,128)(2,1)S(1)}, u32[]{:S(2)}, u32[]{:S(2)}) collective-permute-start(bf16[144,512]{1,0:T(8,128)(2,1)S(1)} %get-tuple-element.93), channel_id=1, source_target_pairs={{0,16},{16,0},{32,48},{48,32},{1,17},{17,1},{33,49},{49,33},{2,18}... | collective-permute-start | bytes 442376 | tf_op jit(solution)/shard_map/ppermute | solution.py:14
  101.1 6.5 %collective-permute-start.19 = (bf16[2,288,128]{2,1,0:T(8,128)(2,1)S(1)}, bf16[2,288,128]{2,1,0:T(8,128)(2,1)S(1)}, u32[]{:S(2)}, u32[]{:S(2)}) collective-permute-start(bf16[2,288,128]{2,1,0:T(8,128)(2,1)S(1)} %get-tuple-element.94), channel_id=1, source_target_pairs={{0,192},{64,128},{128,64},{192,0},{1,193},{65,129},{129,65},{193,1... | collective-permute-start | bytes 442376 | tf_op jit(solution)/shard_map/ppermute | solution.py:14
  102.4 5.3 %collective-permute-start.20 = (bf16[144,512]{1,0:T(8,128)(2,1)S(1)}, bf16[144,512]{1,0:T(8,128)(2,1)S(1)}, u32[]{:S(2)}, u32[]{:S(2)}) collective-permute-start(bf16[144,512]{1,0:T(8,128)(2,1)S(1)} %get-tuple-element.95), channel_id=1, source_target_pairs={{0,48},{16,32},{32,16},{48,0},{1,49},{17,33},{33,17},{49,1},{2,50}... | collective-permute-start | bytes 442376 | tf_op jit(solution)/shard_map/ppermute | solution.py:14
  108.0 7.9 %collective-permute-start.21 = (bf16[4,288,128]{2,1,0:T(8,128)(2,1)S(1)}, bf16[4,288,128]{2,1,0:T(8,128)(2,1)S(1)}, u32[]{:S(2)}, u32[]{:S(2)}) collective-permute-start(bf16[4,288,128]{2,1,0:T(8,128)(2,1)S(1)} %pad_maximum_fusion.2), channel_id=1, source_target_pairs={{0,64},{64,0},{128,192},{192,128},{1,65},{65,1},{129,193},{193,129... | collective-permute-start | bytes 884744 | tf_op jit(solution)/shard_map/ppermute | solution.py:14
  108.7 7.6 %collective-permute-start.22 = (bf16[288,512]{1,0:T(8,128)(2,1)S(1)}, bf16[288,512]{1,0:T(8,128)(2,1)S(1)}, u32[]{:S(2)}, u32[]{:S(2)}) collective-permute-start(bf16[288,512]{1,0:T(8,128)(2,1)S(1)} %pad_maximum_fusion.3), channel_id=1, source_target_pairs={{0,16},{16,0},{32,48},{48,32},{1,17},{17,1},{33,49},{49,33},{2,18}... | collective-permute-start | bytes 884744 | tf_op jit(solution)/shard_map/ppermute | solution.py:14
  110.4 8.2 %collective-permute-start.23 = (bf16[4,288,128]{2,1,0:T(8,128)(2,1)S(1)}, bf16[4,288,128]{2,1,0:T(8,128)(2,1)S(1)}, u32[]{:S(2)}, u32[]{:S(2)}) collective-permute-start(bf16[4,288,128]{2,1,0:T(8,128)(2,1)S(1)} %pad_maximum_fusion.4), channel_id=1, source_target_pairs={{0,192},{64,128},{128,64},{192,0},{1,193},{65,129},{129,65},{193,1... | collective-permute-start | bytes 884744 | tf_op jit(solution)/shard_map/ppermute | solution.py:14
  112.6 6.7 %collective-permute-start.24 = (bf16[288,512]{1,0:T(8,128)(2,1)S(1)}, bf16[288,512]{1,0:T(8,128)(2,1)S(1)}, u32[]{:S(2)}, u32[]{:S(2)}) collective-permute-start(bf16[288,512]{1,0:T(8,128)(2,1)S(1)} %pad_maximum_fusion.5), channel_id=1, source_target_pairs={{0,48},{16,32},{32,16},{48,0},{1,49},{17,33},{33,17},{49,1},{2,50}... | collective-permute-start | bytes 884744 | tf_op jit(solution)/shard_map/ppermute | solution.py:14
  119.5 5.2 %collective-permute-start.25 = (bf16[2,288,128]{2,1,0:T(8,128)(2,1)S(1)}, bf16[2,288,128]{2,1,0:T(8,128)(2,1)S(1)}, u32[]{:S(2)}, u32[]{:S(2)}) collective-permute-start(bf16[2,288,128]{2,1,0:T(8,128)(2,1)S(1)} %slice.210), channel_id=1, source_target_pairs={{0,16},{16,0},{32,48},{48,32},{1,17},{17,1},{33,49},{49,33},{2,18}... | collective-permute-start | bytes 442376 | tf_op jit(solution)/shard_map/ppermute | solution.py:14
  121.6 5.1 %collective-permute-start.26 = (bf16[288,256]{1,0:T(8,128)(2,1)S(1)}, bf16[288,256]{1,0:T(8,128)(2,1)S(1)}, u32[]{:S(2)}, u32[]{:S(2)}) collective-permute-start(bf16[288,256]{1,0:T(8,128)(2,1)S(1)} %slice.209), channel_id=1, source_target_pairs={{0,64},{64,0},{128,192},{192,128},{1,65},{65,1},{129,193},{193,129... | collective-permute-start | bytes 442376 | tf_op jit(solution)/shard_map/ppermute | solution.py:14
  126.8 4.4 %collective-permute-start.27 = (bf16[288,128]{1,0:T(8,128)(2,1)S(1)}, bf16[288,128]{1,0:T(8,128)(2,1)S(1)}, u32[]{:S(2)}, u32[]{:S(2)}) collective-permute-start(bf16[288,128]{1,0:T(8,128)(2,1)S(1)} %fusion.10), channel_id=1, source_target_pairs={{0,48},{16,32},{32,16},{48,0},{1,49},{17,33},{33,17},{49,1},{2,50}... | collective-permute-start | bytes 221192 | tf_op jit(solution)/shard_map/ppermute | solution.py:14
  128.2 5.6 %collective-permute-start.28 = (bf16[288,128]{1,0:T(8,128)(2,1)S(1)}, bf16[288,128]{1,0:T(8,128)(2,1)S(1)}, u32[]{:S(2)}, u32[]{:S(2)}) collective-permute-start(bf16[288,128]{1,0:T(8,128)(2,1)S(1)} %fusion.5), channel_id=1, source_target_pairs={{0,192},{64,128},{128,64},{192,0},{1,193},{65,129},{129,65},{193,1... | collective-permute-start | bytes 221192 | tf_op jit(solution)/shard_map/ppermute | solution.py:14
  133.9 1.5 collective-permute-start.29
  136.2 17.7 %all-to-all-start.3 = ((f32[8,72,128]{2,1,0:T(8,128)}), f32[8,72,128]{2,1,0:T(8,128)S(1)}, u32[]{:S(2)}, u32[]{:S(2)}) async-start(f32[8,72,128]{2,1,0:T(8,128)} %pad_maximum_fusion.7), calls=%async_computation.3 | async-start | bytes 589824 | tf_op jit(solution)/shard_map/all_to_all | solution.py:369

commit v3 on v2

v3 whole, which is shorter than its diff:
```python
import jax
import jax.numpy as jnp
from jax import lax
from jax.experimental import pallas as pl
from jax.experimental.pallas import tpu as pltpu
from jax.sharding import Mesh, PartitionSpec as P

CAP = 30
F32, BF16 = jnp.float32, jnp.bfloat16
X, Y, Z, C = 4, 4, 8, 2


def flip(array, axis, size, change):
    return lax.ppermute(array, axis, [(i, i ^ change) for i in range(size)])


def reordered(array, own, dim):
    return jnp.concatenate([lax.dynamic_slice_in_dim(array, own ^ k, 1, dim) for k in range(4)], dim)


def at_once(*arrays):
    return lax.optimization_barrier(arrays)


def spread(array, axes, size):
    copies = jnp.broadcast_to(array[None], (size,) + array.shape)
    return lax.all_to_all(copies, axes, 0, 0, tiled=True)


def digits(targets):
    parts = [targets // 65536, (targets // 256) % 256, targets % 256]
    return jnp.concatenate([jnp.stack(parts), jnp.zeros((5, targets.shape[0]), jnp.int32)]).astype(BF16)


def undigits(rows):
    parts = rows.astype(jnp.int32)
    return parts[:, 0] * 65536 + parts[:, 1] * 256 + parts[:, 2]


VMEM_LIMIT = 18 * 1024 * 1024


def start_all(copies):
    for copy in copies:
        copy.start()


def wait_all(copies):
    for copy in copies:
        copy.wait()


def in_hbm(arrays):
    return [pltpu.with_memory_space_constraint(array, pltpu.HBM) for array in arrays]


def logits_kernel(meta_ref, own_ref, other_ref, *refs):
    a_refs, b_refs = refs[:X], refs[X : X + Y]
    mine_ref, theirs_ref, ht_ref, slots, tall, sems, piece_sems, out_sem = refs[X + Y :]
    part, rows = a_refs[0].shape[1:]
    wide = tall.shape[1]
    shift = pl.multiple_of(meta_ref[Y], 64)
    pieces = []
    for place in range(X):
        target = tall.at[:, pl.ds(shift, part), pl.ds(place * rows, rows)]
        pieces.append(pltpu.make_async_copy(a_refs[place], target, piece_sems.at[Y, place]))
        for k in range(X):
            target = tall.at[place, pl.ds(shift + part, part), pl.ds(k * rows, rows)]
            pieces.append(pltpu.make_async_copy(b_refs[place].at[k], target, piece_sems.at[place, k]))
    start_all(pieces)
    halves = [[], []]
    for step in range(Y):
        columns = pl.ds(pl.multiple_of(meta_ref[step], 128), wide)
        for place, ref in enumerate((own_ref, other_ref)):
            target = slots.at[place, :, pl.ds(step * wide, wide)]
            copy = pltpu.make_async_copy(ref.at[:, columns], target, sems.at[step, place])
            halves[step // 2].append(copy)
    start_all(halves[0])
    edge = wide - 2 * part
    zeros = jnp.zeros((edge, X * rows), tall.dtype)
    empty = pl.multiple_of(2 * part * (1 - meta_ref[Y] // edge), 64)
    for step in range(Y):
        tall[step, pl.ds(empty, edge)] = zeros
    wait_all(pieces)
    wait_all(halves[0])
    start_all(halves[1])
    keep = pltpu.make_async_copy(tall.at[:, pl.ds(shift, 2 * part)], ht_ref, out_sem)
    depth = Y // 2 * wide
    for i, half in enumerate(halves):
        if i == 1:
            wait_all(half)
            keep.start()
        steps = tall[i * Y // 2 : (i + 1) * Y // 2].reshape(depth, X * rows)
        for place, out_ref in enumerate((mine_ref, theirs_ref)):
            term = jnp.dot(slots[place, :, i * depth : (i + 1) * depth], steps, preferred_element_type=F32)
            if i == 0:
                out_ref[...] = term
            else:
                out_ref[...] += term
    keep.wait()


def logits_of(meta, own, other, a_pieces, b_pieces, wide):
    voc = own.shape[0]
    part, rows = a_pieces[0].shape[1:]
    vmem = pl.BlockSpec(memory_space=pltpu.VMEM)
    hbm = pl.BlockSpec(memory_space=pltpu.HBM)
    square = pltpu.VMEM((voc, X * rows), F32)
    return pl.pallas_call(
        logits_kernel,
        out_shape=(square, square, pltpu.HBM((Y, 2 * part, X * rows), BF16)),
        in_specs=[pl.BlockSpec(memory_space=pltpu.SMEM), hbm, hbm] + [pl.BlockSpec(memory_space=pl.ANY)] * (X + Y),
        out_specs=(vmem, vmem, hbm),
        scratch_shapes=[
            pltpu.VMEM((2, voc, Y * wide), BF16),
            pltpu.VMEM((Y, wide, X * rows), BF16),
            pltpu.SemaphoreType.DMA((Y, 2)),
            pltpu.SemaphoreType.DMA((Y + 1, X)),
            pltpu.SemaphoreType.DMA,
        ],
        compiler_params=pltpu.CompilerParams(vmem_limit_bytes=VMEM_LIMIT),
        cost_estimate=pl.CostEstimate(
            flops=4 * Y * voc * wide * X * rows, bytes_accessed=4 * Y * voc * wide, transcendentals=0
        ),
    )(meta, *in_hbm([own, other]), *a_pieces, *b_pieces)


def turn_kernel(meta_ref, own_ref, other_ref, out_ref, slots, whole, made, sems, out_sems):
    part = out_ref.shape[2]
    voc, wide = slots.shape[2:]
    copies, outs = [], []
    for i in range(2 * Y):
        columns = pl.ds(pl.multiple_of(meta_ref[i], 128), wide)
        row = [
            pltpu.make_async_copy(ref.at[:, columns], slots.at[i, place], sems.at[i, place])
            for place, ref in enumerate((own_ref, other_ref))
        ]
        copies.append(row)
    for row in copies:
        for copy in row:
            copy.start()
    for i in range(2 * Y):
        shift = pl.multiple_of(meta_ref[2 * Y + i // Y], 32)
        for place in range(2):
            copies[i][place].wait()
            whole[i % 2, place] = slots[i, place].T
            made[i, :, place * voc : (place + 1) * voc] = whole[i % 2, place, pl.ds(shift, part)]
        out = pltpu.make_async_copy(made.at[i], out_ref.at[i % Y, i // Y], out_sems.at[i])
        out.start()
        outs.append(out)
    for out in outs:
        out.wait()


def turned_weights(meta, own, other, part, wide):
    voc = own.shape[0]
    hbm = pl.BlockSpec(memory_space=pltpu.HBM)
    return pl.pallas_call(
        turn_kernel,
        out_shape=pltpu.HBM((Y, 2, part, 2 * voc), BF16),
        in_specs=[pl.BlockSpec(memory_space=pltpu.SMEM), hbm, hbm],
        out_specs=hbm,
        scratch_shapes=[
            pltpu.VMEM((2 * Y, 2, voc, wide), BF16),
            pltpu.VMEM((2, 2, wide, voc), BF16),
            pltpu.VMEM((2 * Y, part, 2 * voc), BF16),
            pltpu.SemaphoreType.DMA((2 * Y, 2)),
            pltpu.SemaphoreType.DMA((2 * Y,)),
        ],
        compiler_params=pltpu.CompilerParams(vmem_limit_bytes=VMEM_LIMIT),
        cost_estimate=pl.CostEstimate(flops=0, bytes_accessed=12 * Y * voc * wide, transcendentals=0),
    )(meta, *in_hbm([own, other]))


FIRST_BLOCKS = ((0, 0), (1, 0), (2, 0), (3, 0), (2, 1))
REST_BLOCKS = ((0, 0), (1, 0), (2, 0), (3, 0), (0, 1), (1, 1), (3, 1))


def fetch_blocks(wt_ref, blocks, slots, sems):
    return [
        pltpu.make_async_copy(wt_ref.at[step, side], slots.at[i], sems.at[i]) for i, (step, side) in enumerate(blocks)
    ]


def product(slots, first, last, dls):
    blocks = slots[first:last].reshape((last - first) * slots.shape[1], slots.shape[2])
    return jnp.dot(blocks, dls, preferred_element_type=F32)


def first_kernel(base_ref, wt_ref, grown_ref, grown_other_ref, tgt_ref, vectors_ref, *refs):
    dls_ref, alo_ref, ahi_ref, blo_ref, bhi_ref, slots, sems = refs
    part, rows = alo_ref.shape[1:]
    copies = fetch_blocks(wt_ref, FIRST_BLOCKS, slots, sems)
    start_all(copies)
    chunk = 64
    voc = grown_ref.shape[0]
    for i, source_ref in enumerate((grown_ref, grown_other_ref)):
        for low in range(0, voc, chunk):
            columns = base_ref[i] + low + lax.broadcasted_iota(jnp.int32, (chunk, dls_ref.shape[1]), 0)
            value = source_ref[low : low + chunk] * vectors_ref[0:1]
            value = jnp.where(columns == tgt_ref[...], vectors_ref[1:2], value)
            dls_ref[i * voc + low : i * voc + low + chunk] = value.astype(BF16)
    wait_all(copies)
    a = product(slots, 0, Y, dls_ref[:, 2 * rows : 3 * rows]).astype(BF16)
    for step in range(Y):
        out_ref = alo_ref if step < Y // 2 else ahi_ref
        out_ref[step % (Y // 2)] = a[step * part : (step + 1) * part]
    b = product(slots, Y, Y + 1, dls_ref[...]).astype(BF16)
    blo_ref[...], bhi_ref[...] = b[: part // 2], b[part // 2 :]


def first_call(base, wt, grown, grown_other, tgt, vectors):
    vmem = pl.BlockSpec(memory_space=pltpu.VMEM)
    hbm = pl.BlockSpec(memory_space=pltpu.HBM)
    voc, all_rows = grown.shape
    part = wt.shape[2]
    dls = jax.ShapeDtypeStruct((2 * voc, all_rows), BF16)
    a_half = jax.ShapeDtypeStruct((Y // 2, part, all_rows // X), BF16)
    b_half = jax.ShapeDtypeStruct((part // 2, all_rows), BF16)
    count = len(FIRST_BLOCKS)
    return pl.pallas_call(
        first_kernel,
        out_shape=(dls, a_half, a_half, b_half, b_half),
        in_specs=[pl.BlockSpec(memory_space=pltpu.SMEM), hbm] + [vmem] * 4,
        out_specs=tuple([vmem] * 5),
        scratch_shapes=[
            pltpu.VMEM((count, part, 2 * voc), BF16),
            pltpu.SemaphoreType.DMA((count,)),
        ],
        compiler_params=pltpu.CompilerParams(vmem_limit_bytes=VMEM_LIMIT),
        cost_estimate=pl.CostEstimate(
            flops=2 * wt.size * all_rows // 4, bytes_accessed=wt.size + 8 * grown.size, transcendentals=0
        ),
    )(base, *in_hbm([wt]), grown, grown_other, tgt, vectors)


def rest_kernel(wt_ref, dls_ref, *refs):
    a_outs, b_outs = refs[:3], refs[3:6]
    slots, sems = refs[6:]
    part, rows = a_outs[0].shape[1:]
    copies = fetch_blocks(wt_ref, REST_BLOCKS, slots, sems)
    start_all(copies[:Y])
    wait_all(copies[:Y])
    start_all(copies[Y:])
    a = product(slots, 0, Y, dls_ref[...])
    for step in range(Y):
        for out_ref, place in zip(a_outs, (0, 1, 3)):
            out_ref[step] = a[step * part : (step + 1) * part, place * rows : (place + 1) * rows]
    wait_all(copies[Y:])
    b = product(slots, Y, Y + 3, dls_ref[...])
    for i, out_ref in enumerate(b_outs):
        out_ref[...] = b[i * part : (i + 1) * part]


def rest_call(outs, wt, dls):
    vmem = pl.BlockSpec(memory_space=pltpu.VMEM)
    part, wide = wt.shape[2:]
    count = len(REST_BLOCKS)
    return pl.pallas_call(
        rest_kernel,
        out_shape=tuple(outs),
        in_specs=[pl.BlockSpec(memory_space=pltpu.HBM), vmem],
        out_specs=tuple([vmem] * len(outs)),
        scratch_shapes=[pltpu.VMEM((count, part, wide), BF16), pltpu.SemaphoreType.DMA((count,))],
        compiler_params=pltpu.CompilerParams(vmem_limit_bytes=VMEM_LIMIT),
        cost_estimate=pl.CostEstimate(
            flops=2 * count * part * wide * dls.shape[1], bytes_accessed=2 * count * part * wide, transcendentals=0
        ),
    )(*in_hbm([wt]), dls)


def weight_kernel(places_ref, dl_ref, here_ref, there_ref, out_ref, both):
    half = here_ref.shape[1]
    core = places_ref[Y]
    both[pl.ds(pl.multiple_of(core * half, 64), half)] = here_ref[0]
    both[pl.ds(pl.multiple_of((1 - core) * half, 64), half)] = there_ref[0]
    over_last = (((1,), (1,)), ((), ()))
    out_ref[...] = lax.dot_general(dl_ref[...], both[...], over_last, preferred_element_type=F32).astype(BF16)


def weight_of(places, dls, here, there):
    voc, all_rows = dls.shape[0] // 2, dls.shape[1]
    half = here.shape[1]
    one = pl.BlockSpec((1, half, all_rows), lambda i, places: (i, 0, 0))
    return pl.pallas_call(
        weight_kernel,
        out_shape=jax.ShapeDtypeStruct((voc, Y * 2 * half), BF16),
        grid_spec=pltpu.PrefetchScalarGridSpec(
            num_scalar_prefetch=1,
            grid=(Y,),
            in_specs=[pl.BlockSpec((voc, all_rows), lambda i, places: (0, 0)), one, one],
            out_specs=pl.BlockSpec((voc, 2 * half), lambda i, places: (0, places[i])),
            scratch_shapes=[pltpu.VMEM((2 * half, all_rows), BF16)],
        ),
        compiler_params=pltpu.CompilerParams(vmem_limit_bytes=VMEM_LIMIT),
        cost_estimate=pl.CostEstimate(
            flops=4 * Y * voc * half * all_rows, bytes_accessed=8 * Y * half * all_rows, transcendentals=0
        ),
    )(places, dls, *in_hbm([here, there]))


def per_device(hidden, weight, targets):
    rows, feats = hidden.shape
    voc = weight.shape[0]
    block = Z * C * feats
    half = block // 2
    part = half // 2
    pad = -half % 128
    wide = half + pad
    x, y, z, c = (lax.axis_index(name) for name in ("x", "y", "z", "c"))

    partner = flip(weight, "c", C, 1)
    along = spread(hidden.T, "z", Z)
    places = jnp.stack([y ^ step for step in range(Y)])
    lows = [c * half, c * half + part]
    windows = [places * block + low // 128 * 128 for low in lows]
    meta = jnp.concatenate(windows + [jnp.stack([low % 128 for low in lows])])
    wt = turned_weights(meta, weight, partner, part, -(-part // 128) * 128)
    along, wt = at_once(along, wt)
    along = along.reshape(2, Z // 2, feats, rows)
    keep = lax.dynamic_index_in_dim(along, c, 0, keepdims=False)
    give = lax.dynamic_index_in_dim(along, 1 - c, 0, keepdims=False)
    got = flip(give, "c", C, 1)
    along = jnp.stack([jnp.where(c == 0, keep, got), jnp.where(c == 0, got, keep)], 1).reshape(half, rows)
    a, b = along[:part], jnp.concatenate([along[part:], digits(targets)])
    a, b = at_once(a, b)
    a1, b1 = at_once(flip(a, "y", Y, 1), flip(b, "x", X, 1))
    a01, b01 = jnp.stack([a, a1]), jnp.stack([b, b1])
    a32, b32 = at_once(flip(a01, "y", Y, 3), flip(b01, "x", X, 3))
    a2 = jnp.stack([a01[0], a01[1], a32[1], a32[0]])
    b2 = jnp.stack([b01[0], b01[1], b32[1], b32[0]])
    tgt = undigits(b2[:, part:]).reshape(X * rows)
    a2, b2 = at_once(a2, b2[:, :part])
    ax1, by1, ax3, by3, ax2, by2 = at_once(
        *[flip(array, axis, 4, step) for step in (1, 3, 2) for array, axis in ((a2, "x"), (b2, "y"))]
    )
    meta = jnp.append(places * block + c * (half - pad), c * pad)

    mine, theirs, ht = logits_of(
        meta, weight, partner, [a2, ax1, ax2, ax3], [b2, by1, by2, by3], wide
    )
    theirs = flip(theirs, "c", C, 1)
    capped = CAP * jnp.tanh((mine + theirs) / CAP)
    offset = (((x * Y + y) * Z + z) * C + c) * voc
    columns = offset + jnp.arange(voc, dtype=jnp.int32)
    hit = columns[:, None] == tgt[None, :]
    stats = jnp.stack([jnp.sum(jnp.exp(capped - CAP), 0), jnp.sum(jnp.where(hit, capped, 0.0), 0)])
    stats, ht, mine, theirs = at_once(stats, ht, mine, theirs)
    other = flip(ht, "c", C, 1)
    capped = CAP * jnp.tanh((mine + theirs) / CAP)
    grown = jnp.exp(capped - CAP) * (1.0 - (capped / CAP) ** 2)
    stats = spread(stats.reshape(2, X, rows), ("z", "c"), Z * C).sum(0)
    stats = reordered(stats, x, 1)
    stats, grown, other = at_once(stats, grown, other)
    grown_other = flip(grown, "c", C, 1)
    stats = spread(stats, ("x", "y"), X * Y).sum(0)
    stats = reordered(stats, x, 1)
    stats, grown_other = at_once(stats, grown_other)
    lse = CAP + jnp.log(stats[0])
    loss = lse[0] - stats[1, 0]
    at_target = (jnp.exp(stats[1] - lse) - 1.0) * (1.0 - (stats[1] / CAP) ** 2)
    vectors = jnp.stack([(1.0 / stats[0]).reshape(-1), at_target.reshape(-1)])
    base = jnp.stack([offset, offset + (1 - 2 * c) * voc])

    dls, a_lo, a_hi, b_lo, b_hi = first_call(base, wt, grown, grown_other, tgt[None], vectors)
    a_lo, b_lo, a_hi, b_hi = at_once(
        flip(a_lo, "x", X, 1), flip(b_lo, "y", Y, 1), flip(a_hi, "x", X, 3), flip(b_hi, "y", Y, 3)
    )
    a_kind = jax.ShapeDtypeStruct((Y, part, rows), F32)
    b_kind = jax.ShapeDtypeStruct((part, X * rows), F32)
    a0, a1, a3, b0, b1, b3 = rest_call([a_kind] * 3 + [b_kind] * 3, wt, dls)
    a1 = jnp.concatenate([a1[: Y // 2], a1[Y // 2 :] + a_hi.astype(F32)]).astype(BF16)
    a3 = jnp.concatenate([a3[: Y // 2] + a_lo.astype(F32), a3[Y // 2 :]]).astype(BF16)
    b1 = jnp.concatenate([b1[: part // 2], b1[part // 2 :] + b_hi.astype(F32)]).astype(BF16)
    b3 = jnp.concatenate([b3[: part // 2] + b_lo.astype(F32), b3[part // 2 :]]).astype(BF16)
    a1, b1, a3, b3 = at_once(a1, b1, a3, b3)
    a1, b1, a3, b3 = at_once(flip(a1, "x", X, 1), flip(b1, "y", Y, 1), flip(a3, "x", X, 3), flip(b3, "y", Y, 3))
    a_own = a0 + a1.astype(F32) + a3.astype(F32)
    b_own = b0 + b1.astype(F32) + b3.astype(F32)
    a_out, b_out = at_once(a_own[1:3].astype(BF16), b_own[:, rows : 3 * rows].astype(BF16))
    a_in, b_in = at_once(flip(a_out, "y", Y, 1), flip(b_out, "x", X, 1))
    a_out = (a_own[3] + a_in[1].astype(F32)).astype(BF16)
    b_out = (b_own[:, 3 * rows :] + b_in[:, rows:].astype(F32)).astype(BF16)
    a_out, b_out = at_once(a_out, b_out)
    a_out, b_out = at_once(flip(a_out, "y", Y, 3), flip(b_out, "x", X, 3))
    a_sum = a_own[0] + a_in[0].astype(F32) + a_out.astype(F32)
    b_sum = b_own[:, :rows] + b_in[:, :rows].astype(F32) + b_out.astype(F32)
    total = jnp.concatenate([a_sum, b_sum]).reshape(Z // 2, C, feats, rows)
    mine = lax.dynamic_index_in_dim(total, c, 1, keepdims=False)
    theirs = flip(lax.dynamic_index_in_dim(total, 1 - c, 1, keepdims=False), "c", C, 1)
    by_z = jnp.concatenate([jnp.where(c == 0, mine, theirs), jnp.where(c == 0, theirs, mine)])
    by_z, dls = at_once(by_z, dls)
    grad_weight = weight_of(jnp.append(places, c), dls, ht, other)
    grad_hidden = lax.all_to_all(by_z, "z", 0, 0, tiled=True).sum(0).astype(BF16).T
    return loss, grad_hidden, grad_weight


def solution(mesh):
    chips = Mesh(mesh.devices.reshape(X, Y, Z, C), ("x", "y", "z", "c"))
    in_specs = (P("x", ("y", "z", "c")), P(("x", "y", "z", "c"), None), P("x"))
    out_specs = (P("x"), P("x", ("y", "z", "c")), P(("x", "y", "z", "c"), None))
    return jax.shard_map(per_device, mesh=chips, in_specs=in_specs, out_specs=out_specs, check_vma=False)
```

time: 156 us -> 152 us (0.974)
  blocking collectives: 10.5 us -> 0 us
  waiting for transfers between devices: 54.4 us -> 59.2 us
  starting transfers between devices: 50.2 us -> 53.2 us
  other arithmetic: 6.99 us -> 4.74 us
    all_to_all x1 -> x0, blocking collectives: 10.5 us -> none  [spread(): return lax.all_to_all(copies, axes, 0, 0, tiled=True)]
    all_to_all x2 -> x3, starting transfers between devices: 12.1 us -> 19.5 us  [spread(): return lax.all_to_all(copies, axes, 0, 0, tiled=True)]
    all_to_all x2 -> x3, waiting for transfers between devices: 12.1 us -> 18.1 us  [spread(): return lax.all_to_all(copies, axes, 0, 0, tiled=True)]
    ppermute x30 -> x28, starting transfers between devices: 33.3 us -> 30.3 us  [flip(): return lax.ppermute(array, axis, [(i, i ^ change) for i in range(size)])]
    convert_element_type x1 -> x0, other arithmetic: 1.7 us -> none  [per_device(): ((probs - hit.astype(F32)) * (1.0 - (capped / CAP) ** 2)).astype(BF16)]
    ppermute x30 -> x28, waiting for transfers between devices: 37.5 us -> 36.1 us  [flip(): return lax.ppermute(array, axis, [(i, i ^ change) for i in range(size)])]
  transfers between devices with their start and end apart: 33 -> 32, of which waited for: 24 -> 22; matrix products, arithmetic and copies ran while one was open for 2% -> 3% of each run, Pallas kernels for 11% -> 11%
where the time goes in v3:
time: 152 us; the launch traced here: 150 us
  waiting for transfers between devices  59.2 us (39%)
  starting transfers between devices  53.2 us (35%)
  Pallas kernels  28.5 us (19%)
  other arithmetic  4.74 us (3%)
  local copies, waits for them, and re-layouts  3.6 us (2%)
    ppermute x28, waiting for transfers between devices, flip(): return lax.ppermute(array, axis, [(i, i ^ change) for i in range(size)])  36.1 us
    ppermute x28, starting transfers between devices, flip(): return lax.ppermute(array, axis, [(i, i ^ change) for i in range(size)])  30.3 us
    all_to_all x3, starting transfers between devices, spread(): return lax.all_to_all(copies, axes, 0, 0, tiled=True)  19.5 us
    all_to_all x3, waiting for transfers between devices, spread(): return lax.all_to_all(copies, axes, 0, 0, tiled=True)  18.1 us
    pallas_call x1, Pallas kernels, logits_of(): pl.pallas_call(logits_kernel, out_shape=(square, square, pltpu.HBM((Y, 2...  7.94 us
    pallas_call x1, Pallas kernels, weight_of(): pl.pallas_call(weight_kernel, out_shape=jax.ShapeDtypeStruct((voc, Y * 2...  7.48 us
    pallas_call x1, Pallas kernels, turned_weights(): pl.pallas_call(turn_kernel, out_shape=pltpu.HBM((Y, 2, part, 2 * voc), BF...  5.44 us
    all_to_all x1, waiting for transfers between devices, per_device(): lax.all_to_all(by_z, 'z', 0, 0, tiled=True).sum(0).astype(BF16)  5 us
  transfers between devices with their start and end apart: 32, of which 22 were waited for; matrix products, arithmetic and copies ran while one was open for 3% of the time, Pallas kernels for 11%

profile of v3, /device:TPU:8, one launch (start us, length us, event | category | flops | bytes accessed | tf_op | source)
XLA Modules:
  0.0 150.2 jit_solution(7998018530139364265)
XLA Ops:
  0.7 1.4 broadcast_in_dim.14
  2.1 8.5 %all-to-all-start = ((bf16[8,72,128]{2,1,0:T(8,128)(2,1)}), bf16[8,72,128]{2,1,0:T(8,128)(2,1)S(1)}, u32[]{:S(2)}, u32[]{:S(2)}) async-start(bf16[8,72,128]{2,1,0:T(8,128)(2,1)} %broadcast_in_dim.14), calls=%async_computation | async-start | bytes 294912 | tf_op jit(solution)/shard_map/all_to_all | solution.py:27
  10.8 5.4 %shard_map.58.wt_ref = bf16[4,2,288,1024]{3,2,1,0:T(8,128)(2,1)} custom-call(s32[10]{0:T(128)S(1)} %pad_add_fusion.1.meta_ref, bf16[512,4608]{1,0:T(8,128)(2,1)} %own_ref.3, bf16[512,4608]{1,0:T(8,128)(2,1)} %collective-permute-done.other_ref), custom_call_target="tpu_custom_call" | custom-call | bytes 9437184 | tf_op jit(solution)/shard_map/pallas_call | solution.py:158
  16.2 4.5 %all-to-all-done = bf16[8,72,128]{2,1,0:T(8,128)(2,1)S(1)} async-done(((bf16[8,72,128]{2,1,0:T(8,128)(2,1)}), bf16[8,72,128]{2,1,0:T(8,128)(2,1)S(1)}, u32[]{:S(2)}, u32[]{:S(2)}) %all-to-all-start) | async-done | bytes 147488 | tf_op jit(solution)/shard_map/all_to_all | solution.py:27
  20.7 1.2 collective-permute-done.1
  22.1 1.6 %collective-permute-start.3 = (bf16[296,128]{1,0:T(8,128)(2,1)S(1)}, bf16[296,128]{1,0:T(8,128)(2,1)S(1)}, u32[]{:S(2)}, u32[]{:S(2)}) collective-permute-start(bf16[296,128]{1,0:T(8,128)(2,1)S(1)} %concatenate.47), channel_id=1, source_target_pairs={{0,64},{64,0},{128,192},{192,128},{1,65},{65,1},{129,193},{193,129... | collective-permute-start | bytes 227336 | tf_op jit(solution)/shard_map/ppermute | solution.py:14
  24.1 3.9 %collective-permute-done.2 = bf16[288,128]{1,0:T(8,128)(2,1)S(1)} collective-permute-done((bf16[288,128]{1,0:T(8,128)(2,1)S(1)}, bf16[288,128]{1,0:T(8,128)(2,1)S(1)}, u32[]{:S(2)}, u32[]{:S(2)}) %collective-permute-start.2) | collective-permute-done | bytes 73760 | tf_op jit(solution)/shard_map/ppermute | solution.py:14
  28.0 2.2 %collective-permute-start.5 = (bf16[2,296,128]{2,1,0:T(8,128)(2,1)S(1)}, bf16[2,296,128]{2,1,0:T(8,128)(2,1)S(1)}, u32[]{:S(2)}, u32[]{:S(2)}) collective-permute-start(bf16[2,296,128]{2,1,0:T(8,128)(2,1)S(1)} %pad_maximum_fusion.8), channel_id=1, source_target_pairs={{0,192},{64,128},{128,64},{192,0},{1,193},{65,129},{129,65},{193,1... | collective-permute-start | bytes 454664 | tf_op jit(solution)/shard_map/ppermute | solution.py:14
  30.2 1.7 %collective-permute-start.4 = (bf16[2,288,128]{2,1,0:T(8,128)(2,1)S(1)}, bf16[2,288,128]{2,1,0:T(8,128)(2,1)S(1)}, u32[]{:S(2)}, u32[]{:S(2)}) collective-permute-start(bf16[2,288,128]{2,1,0:T(8,128)(2,1)S(1)} %pad_maximum_fusion.9), channel_id=1, source_target_pairs={{0,48},{16,32},{32,16},{48,0},{1,49},{17,33},{33,17},{49,1},{2,50}... | collective-permute-start | bytes 442376 | tf_op jit(solution)/shard_map/ppermute | solution.py:14
  31.9 3.6 %collective-permute-done.4 = bf16[2,288,128]{2,1,0:T(8,128)(2,1)S(1)} collective-permute-done((bf16[2,288,128]{2,1,0:T(8,128)(2,1)S(1)}, bf16[2,288,128]{2,1,0:T(8,128)(2,1)S(1)}, u32[]{:S(2)}, u32[]{:S(2)}) %collective-permute-start.4) | collective-permute-done | bytes 147488 | tf_op jit(solution)/shard_map/ppermute | solution.py:14
  36.9 1.3 collective-permute-start.6
  38.3 3.5 %collective-permute-start.11 = (bf16[4,288,128]{2,1,0:T(8,128)(2,1)S(1)}, bf16[4,288,128]{2,1,0:T(8,128)(2,1)S(1)}, u32[]{:S(2)}, u32[]{:S(2)}) collective-permute-start(bf16[4,288,128]{2,1,0:T(8,128)(2,1)S(1)} %slice.151.refs_4_), channel_id=1, source_target_pairs={{0,32},{16,48},{32,0},{48,16},{1,33},{17,49},{33,1},{49,17},{2,34}... | collective-permute-start | bytes 884744 | tf_op jit(solution)/shard_map/ppermute | solution.py:14
  41.9 2.1 %collective-permute-start.8 = (bf16[4,288,128]{2,1,0:T(8,128)(2,1)S(1)}, bf16[4,288,128]{2,1,0:T(8,128)(2,1)S(1)}, u32[]{:S(2)}, u32[]{:S(2)}) collective-permute-start(bf16[4,288,128]{2,1,0:T(8,128)(2,1)S(1)} %pad_maximum_fusion.1.refs_0_), channel_id=1, source_target_pairs={{0,192},{64,128},{128,64},{192,0},{1,193},{65,129},{129,65},{193,1... | collective-permute-start | bytes 884744 | tf_op jit(solution)/shard_map/ppermute | solution.py:14
  44.0 3.7 %collective-permute-done.10.refs_2_ = bf16[4,288,128]{2,1,0:T(8,128)(2,1)S(1)} collective-permute-done((bf16[4,288,128]{2,1,0:T(8,128)(2,1)S(1)}, bf16[4,288,128]{2,1,0:T(8,128)(2,1)S(1)}, u32[]{:S(2)}, u32[]{:S(2)}) %collective-permute-start.10) | collective-permute-done | bytes 294944 | tf_op jit(solution)/shard_map/ppermute | solution.py:14
  47.7 1.6 %collective-permute-start.9 = (bf16[4,288,128]{2,1,0:T(8,128)(2,1)S(1)}, bf16[4,288,128]{2,1,0:T(8,128)(2,1)S(1)}, u32[]{:S(2)}, u32[]{:S(2)}) collective-permute-start(bf16[4,288,128]{2,1,0:T(8,128)(2,1)S(1)} %slice.151.refs_4_), channel_id=1, source_target_pairs={{0,48},{16,32},{32,16},{48,0},{1,49},{17,33},{33,17},{49,1},{2,50}... | collective-permute-start | bytes 884744 | tf_op jit(solution)/shard_map/ppermute | solution.py:14
  49.4 3.1 %collective-permute-done.7.refs_5_ = bf16[4,288,128]{2,1,0:T(8,128)(2,1)S(1)} collective-permute-done((bf16[4,288,128]{2,1,0:T(8,128)(2,1)S(1)}, bf16[4,288,128]{2,1,0:T(8,128)(2,1)S(1)}, u32[]{:S(2)}, u32[]{:S(2)}) %collective-permute-start.7) | collective-permute-done | bytes 294944 | tf_op jit(solution)/shard_map/ppermute | solution.py:14
  52.4 2.0 %collective-permute-done.9.refs_7_ = bf16[4,288,128]{2,1,0:T(8,128)(2,1)S(1)} collective-permute-done((bf16[4,288,128]{2,1,0:T(8,128)(2,1)S(1)}, bf16[4,288,128]{2,1,0:T(8,128)(2,1)S(1)}, u32[]{:S(2)}, u32[]{:S(2)}) %collective-permute-start.9) | collective-permute-done | bytes 294944 | tf_op jit(solution)/shard_map/ppermute | solution.py:14
  54.4 7.9 %shard_map.59 = (f32[512,512]{1,0:T(8,128)S(1)}, f32[512,512]{1,0:T(8,128)}, bf16[4,576,512]{2,1,0:T(8,128)(2,1)}) custom-call(s32[5]{0:T(128)S(1)} %pad_add_fusion.meta_ref, bf16[512,4608]{1,0:T(8,128)(2,1)} %own_ref.3, bf16[512,4608]{1,0:T(8,128)(2,1)} %collective-permute-done.other_ref, bf16[4,288,128]{2,1,0:T(8,128)(2,1)S(1)} %pad_maximum_fusion.1.refs_0_, ...), custom_call_target="tpu_custom_call" | custom-call | flops 2684354560 | bytes 5242880 | tf_op jit(solution)/shard_map/pallas_call | solution.py:109
  62.7 0.8 fusion.10
  63.5 2.0 %collective-permute-done.12 = f32[512,512]{1,0:T(8,128)S(1)} collective-permute-done((f32[512,512]{1,0:T(8,128)}, f32[512,512]{1,0:T(8,128)S(1)}, u32[]{:S(2)}, u32[]{:S(2)}) %collective-permute-start.12) | collective-permute-done | bytes 1048608 | tf_op jit(solution)/shard_map/ppermute | solution.py:14
  66.8 3.5 %all-to-all-start.1 = ((f32[16,2,4,128]{3,2,1,0:T(4,128)}), f32[16,2,4,128]{3,2,1,0:T(4,128)S(1)}, u32[]{:S(2)}, u32[]{:S(2)}) async-start(f32[16,2,4,128]{3,2,1,0:T(4,128)} %broadcast_in_dim.31), calls=%async_computation.1 | async-start | bytes 131072 | tf_op jit(solution)/shard_map/all_to_all | solution.py:27
  70.7 7.4 %all-to-all-done.1 = f32[16,2,4,128]{3,2,1,0:T(4,128)S(1)} async-done(((f32[16,2,4,128]{3,2,1,0:T(4,128)}), f32[16,2,4,128]{3,2,1,0:T(4,128)S(1)}, u32[]{:S(2)}, u32[]{:S(2)}) %all-to-all-start.1) | async-done | bytes 65568 | tf_op jit(solution)/shard_map/all_to_all | solution.py:27
  79.3 7.5 %all-to-all-start.2 = ((f32[16,2,4,128]{3,2,1,0:T(4,128)}), f32[16,2,4,128]{3,2,1,0:T(4,128)S(1)}, u32[]{:S(2)}, u32[]{:S(2)}) async-start(f32[16,2,4,128]{3,2,1,0:T(4,128)} %broadcast_in_dim.32), calls=%async_computation.2 | async-start | bytes 131072 | tf_op jit(solution)/shard_map/all_to_all | solution.py:27
  86.8 6.2 %all-to-all-done.2 = f32[16,2,4,128]{3,2,1,0:T(4,128)S(1)} async-done(((f32[16,2,4,128]{3,2,1,0:T(4,128)}), f32[16,2,4,128]{3,2,1,0:T(4,128)S(1)}, u32[]{:S(2)}, u32[]{:S(2)}) %all-to-all-start.2) | async-done | bytes 65568 | tf_op jit(solution)/shard_map/all_to_all | solution.py:27
  93.2 3.5 %shard_map.60 = (bf16[1024,512]{1,0:T(8,128)(2,1)S(1)}, bf16[2,288,128]{2,1,0:T(8,128)(2,1)S(1)}, bf16[2,288,128]{2,1,0:T(8,128)(2,1)S(1)}, bf16[144,512]{1,0:T(8,128)(2,1)S(1)}, bf16[144,512]{1,0:T(8,128)(2,1)S(1)}) custom-call(s32[2]{0:T(128)S(1)} %pad_add_fusion.2.base_ref, bf16[4,2,288,1024]{3,2,1,0:T(8,128)(2,1)} %shard_map.58.wt_ref, ...), custom_call_target="tpu_custom_call" | custom-call | flops 603979776 | bytes 4456448 | tf_op jit(solution)/shard_map/pallas_call | solution.py:221
  97.2 1.5 collective-permute-start.16
  98.7 1.3 collective-permute-start.17
  100.6 4.1 %shard_map.61 = (f32[4,288,128]{2,1,0:T(8,128)S(1)}, f32[4,288,128]{2,1,0:T(8,128)S(1)}, f32[4,288,128]{2,1,0:T(8,128)S(1)}, f32[288,512]{1,0:T(8,128)S(1)}, f32...) custom-call(bf16[4,2,288,1024]{3,2,1,0:T(8,128)(2,1)} %shard_map.58.wt_ref, ...), custom_call_target="tpu_custom_call" | custom-call | flops 2113929216 | bytes 4128768 | tf_op jit(solution)/shard_map/pallas_call | solution.py:259
  105.4 0.9 collective-permute-start.19
  106.2 1.8 %collective-permute-start.20 = (bf16[288,512]{1,0:T(8,128)(2,1)S(1)}, bf16[288,512]{1,0:T(8,128)(2,1)S(1)}, u32[]{:S(2)}, u32[]{:S(2)}) collective-permute-start(bf16[288,512]{1,0:T(8,128)(2,1)S(1)} %pad_maximum_fusion.3), channel_id=1, source_target_pairs={{0,16},{16,0},{32,48},{48,32},{1,17},{17,1},{33,49},{49,33},{2,18}... | collective-permute-start | bytes 884744 | tf_op jit(solution)/shard_map/ppermute | solution.py:14
  108.0 2.1 %collective-permute-start.21 = (bf16[4,288,128]{2,1,0:T(8,128)(2,1)S(1)}, bf16[4,288,128]{2,1,0:T(8,128)(2,1)S(1)}, u32[]{:S(2)}, u32[]{:S(2)}) collective-permute-start(bf16[4,288,128]{2,1,0:T(8,128)(2,1)S(1)} %pad_maximum_fusion.4), channel_id=1, source_target_pairs={{0,192},{64,128},{128,64},{192,0},{1,193},{65,129},{129,65},{193,1... | collective-permute-start | bytes 884744 | tf_op jit(solution)/shard_map/ppermute | solution.py:14
  110.1 0.8 collective-permute-start.22
  110.9 1.3 collective-permute-done.19
  112.2 0.8 collective-permute-done.20
  113.0 3.0 %collective-permute-done.21 = bf16[4,288,128]{2,1,0:T(8,128)(2,1)S(1)} collective-permute-done((bf16[4,288,128]{2,1,0:T(8,128)(2,1)S(1)}, bf16[4,288,128]{2,1,0:T(8,128)(2,1)S(1)}, u32[]{:S(2)}, u32[]{:S(2)}) %collective-permute-start.21) | collective-permute-done | bytes 294944 | tf_op jit(solution)/shard_map/ppermute | solution.py:14
  116.0 0.9 collective-permute-done.22
  117.1 1.5 %collective-permute-start.23 = (bf16[2,288,128]{2,1,0:T(8,128)(2,1)S(1)}, bf16[2,288,128]{2,1,0:T(8,128)(2,1)S(1)}, u32[]{:S(2)}, u32[]{:S(2)}) collective-permute-start(bf16[2,288,128]{2,1,0:T(8,128)(2,1)S(1)} %slice.206), channel_id=1, source_target_pairs={{0,16},{16,0},{32,48},{48,32},{1,17},{17,1},{33,49},{49,33},{2,18}... | collective-permute-start | bytes 442376 | tf_op jit(solution)/shard_map/ppermute | solution.py:14
  119.2 3.2 %collective-permute-done.23 = bf16[2,288,128]{2,1,0:T(8,128)(2,1)S(1)} collective-permute-done((bf16[2,288,128]{2,1,0:T(8,128)(2,1)S(1)}, bf16[2,288,128]{2,1,0:T(8,128)(2,1)S(1)}, u32[]{:S(2)}, u32[]{:S(2)}) %collective-permute-start.23) | collective-permute-done | bytes 147488 | tf_op jit(solution)/shard_map/ppermute | solution.py:14
  122.4 1.5 collective-permute-done.24
  123.9 1.3 collective-permute-start.25
  125.2 1.1 collective-permute-start.26
  126.3 2.0 %collective-permute-done.25 = bf16[288,128]{1,0:T(8,128)(2,1)S(1)} collective-permute-done((bf16[288,128]{1,0:T(8,128)(2,1)S(1)}, bf16[288,128]{1,0:T(8,128)(2,1)S(1)}, u32[]{:S(2)}, u32[]{:S(2)}) %collective-permute-start.25) | collective-permute-done | bytes 73760 | tf_op jit(solution)/shard_map/ppermute | solution.py:14
  128.3 2.4 %collective-permute-done.26 = bf16[288,128]{1,0:T(8,128)(2,1)S(1)} collective-permute-done((bf16[288,128]{1,0:T(8,128)(2,1)S(1)}, bf16[288,128]{1,0:T(8,128)(2,1)S(1)}, u32[]{:S(2)}, u32[]{:S(2)}) %collective-permute-start.26) | collective-permute-done | bytes 73760 | tf_op jit(solution)/shard_map/ppermute | solution.py:14
  130.9 1.4 collective-permute-done.27
  132.3 0.8 pad_maximum_fusion.7
  133.1 3.4 %all-to-all-start.3 = ((f32[8,72,128]{2,1,0:T(8,128)}), f32[8,72,128]{2,1,0:T(8,128)S(1)}, u32[]{:S(2)}, u32[]{:S(2)}) async-start(f32[8,72,128]{2,1,0:T(8,128)} %pad_maximum_fusion.7), calls=%async_computation.3 | async-start | bytes 589824 | tf_op jit(solution)/shard_map/all_to_all | solution.py:394
  137.1 7.5 %shard_map.62 = bf16[512,4608]{1,0:T(8,128)(2,1)} custom-call(s32[5]{0:T(128)S(1)} %concatenate.56.places_ref, bf16[1024,512]{1,0:T(8,128)(2,1)S(1)} %get-tuple-element.123.dls_ref.dl_ref, bf16[4,576,512]{2,1,0:T(8,128)(2,1)} %get-tuple-element.85.here_ref, bf16[4,576,512]{2,1,0:T(8,128)(2,1)} %collective-permute-done.13.there_ref), custom_call_target="tpu_custom_call" | custom-call | flops 2415919104 | bytes 9437184 | tf_op jit(solution)/shard_map/pallas_call | solution.py:285
  144.6 5.0 %all-to-all-done.3 = f32[8,72,128]{2,1,0:T(8,128)S(1)} async-done(((f32[8,72,128]{2,1,0:T(8,128)}), f32[8,72,128]{2,1,0:T(8,128)S(1)}, u32[]{:S(2)}, u32[]{:S(2)}) %all-to-all-start.3) | async-done | bytes 294944 | tf_op jit(solution)/shard_map/all_to_all | solution.py:394
  (89 shorter events, 9.8 us)
Async XLA Ops:
  0.6 10.1 %collective-permute-start = (bf16[512,4608]{1,0:T(8,128)(2,1)}, bf16[512,4608]{1,0:T(8,128)(2,1)}, u32[]{:S(2)}, u32[]{:S(2)}) collective-permute-start(bf16[512,4608]{1,0:T(8,128)(2,1)} %own_ref.3), channel_id=1, source_target_pairs={{0,1},{1,0},{2,3},{3,2},{4,5},{5,4},{6,7},{7,6},{8,9},{9,8},{10,11... | collective-permute-start | bytes 14155784 | tf_op jit(solution)/shard_map/ppermute | solution.py:14
  2.1 18.5 %all-to-all-start = ((bf16[8,72,128]{2,1,0:T(8,128)(2,1)}), bf16[8,72,128]{2,1,0:T(8,128)(2,1)S(1)}, u32[]{:S(2)}, u32[]{:S(2)}) async-start(bf16[8,72,128]{2,1,0:T(8,128)(2,1)} %broadcast_in_dim.14), calls=%async_computation | async-start | bytes 294912 | tf_op jit(solution)/shard_map/all_to_all | solution.py:27
  10.8 9.9 %copy-start.3 = (s32[128]{0:T(128)S(1)}, s32[128]{0:T(128)}, u32[]{:S(2)}) copy-start(s32[128]{0:T(128)} %param.5) | copy-start | bytes 1540
  20.7 1.3 collective-permute-start.1
  22.1 5.9 %collective-permute-start.3 = (bf16[296,128]{1,0:T(8,128)(2,1)S(1)}, bf16[296,128]{1,0:T(8,128)(2,1)S(1)}, u32[]{:S(2)}, u32[]{:S(2)}) collective-permute-start(bf16[296,128]{1,0:T(8,128)(2,1)S(1)} %concatenate.47), channel_id=1, source_target_pairs={{0,64},{64,0},{128,192},{192,128},{1,65},{65,1},{129,193},{193,129... | collective-permute-start | bytes 227336 | tf_op jit(solution)/shard_map/ppermute | solution.py:14
  23.6 4.4 %collective-permute-start.2 = (bf16[288,128]{1,0:T(8,128)(2,1)S(1)}, bf16[288,128]{1,0:T(8,128)(2,1)S(1)}, u32[]{:S(2)}, u32[]{:S(2)}) collective-permute-start(bf16[288,128]{1,0:T(8,128)(2,1)S(1)} %bitcast.72), channel_id=1, source_target_pairs={{0,16},{16,0},{32,48},{48,32},{1,17},{17,1},{33,49},{49,33},{2,18}... | collective-permute-start | bytes 221192 | tf_op jit(solution)/shard_map/ppermute | solution.py:14
  28.0 7.6 %copy-start = (bf16[296,128]{1,0:T(8,128)(2,1)}, bf16[296,128]{1,0:T(8,128)(2,1)S(1)}, u32[]{:S(2)}) copy-start(bf16[296,128]{1,0:T(8,128)(2,1)S(1)} %collective-permute-done.3) | copy-start | bytes 227332
  28.0 7.4 %collective-permute-start.5 = (bf16[2,296,128]{2,1,0:T(8,128)(2,1)S(1)}, bf16[2,296,128]{2,1,0:T(8,128)(2,1)S(1)}, u32[]{:S(2)}, u32[]{:S(2)}) collective-permute-start(bf16[2,296,128]{2,1,0:T(8,128)(2,1)S(1)} %pad_maximum_fusion.8), channel_id=1, source_target_pairs={{0,192},{64,128},{128,64},{192,0},{1,193},{65,129},{129,65},{193,1... | collective-permute-start | bytes 454664 | tf_op jit(solution)/shard_map/ppermute | solution.py:14
  30.2 5.2 %collective-permute-start.4 = (bf16[2,288,128]{2,1,0:T(8,128)(2,1)S(1)}, bf16[2,288,128]{2,1,0:T(8,128)(2,1)S(1)}, u32[]{:S(2)}, u32[]{:S(2)}) collective-permute-start(bf16[2,288,128]{2,1,0:T(8,128)(2,1)S(1)} %pad_maximum_fusion.9), channel_id=1, source_target_pairs={{0,48},{16,32},{32,16},{48,0},{1,49},{17,33},{33,17},{49,1},{2,50}... | collective-permute-start | bytes 442376 | tf_op jit(solution)/shard_map/ppermute | solution.py:14
  35.5 0.6 copy-start.1
  35.5 0.7 copy-start.2
  36.2 11.5 %collective-permute-start.10 = (bf16[4,288,128]{2,1,0:T(8,128)(2,1)S(1)}, bf16[4,288,128]{2,1,0:T(8,128)(2,1)S(1)}, u32[]{:S(2)}, u32[]{:S(2)}) collective-permute-start(bf16[4,288,128]{2,1,0:T(8,128)(2,1)S(1)} %pad_maximum_fusion.1.refs_0_), channel_id=1, source_target_pairs={{0,128},{64,192},{128,0},{192,64},{1,129},{65,193},{129,1},{193,65... | collective-permute-start | bytes 884744 | tf_op jit(solution)/shard_map/ppermute | solution.py:14
  36.9 12.5 %collective-permute-start.6 = (bf16[4,288,128]{2,1,0:T(8,128)(2,1)S(1)}, bf16[4,288,128]{2,1,0:T(8,128)(2,1)S(1)}, u32[]{:S(2)}, u32[]{:S(2)}) collective-permute-start(bf16[4,288,128]{2,1,0:T(8,128)(2,1)S(1)} %pad_maximum_fusion.1.refs_0_), channel_id=1, source_target_pairs={{0,64},{64,0},{128,192},{192,128},{1,65},{65,1},{129,193},{193,129... | collective-permute-start | bytes 884744 | tf_op jit(solution)/shard_map/ppermute | solution.py:14
  38.3 11.1 %collective-permute-start.11 = (bf16[4,288,128]{2,1,0:T(8,128)(2,1)S(1)}, bf16[4,288,128]{2,1,0:T(8,128)(2,1)S(1)}, u32[]{:S(2)}, u32[]{:S(2)}) collective-permute-start(bf16[4,288,128]{2,1,0:T(8,128)(2,1)S(1)} %slice.151.refs_4_), channel_id=1, source_target_pairs={{0,32},{16,48},{32,0},{48,16},{1,33},{17,49},{33,1},{49,17},{2,34}... | collective-permute-start | bytes 884744 | tf_op jit(solution)/shard_map/ppermute | solution.py:14
  41.8 10.7 %collective-permute-start.7 = (bf16[4,288,128]{2,1,0:T(8,128)(2,1)S(1)}, bf16[4,288,128]{2,1,0:T(8,128)(2,1)S(1)}, u32[]{:S(2)}, u32[]{:S(2)}) collective-permute-start(bf16[4,288,128]{2,1,0:T(8,128)(2,1)S(1)} %slice.151.refs_4_), channel_id=1, source_target_pairs={{0,16},{16,0},{32,48},{48,32},{1,17},{17,1},{33,49},{49,33},{2,18}... | collective-permute-start | bytes 884744 | tf_op jit(solution)/shard_map/ppermute | solution.py:14
  41.9 10.5 %collective-permute-start.8 = (bf16[4,288,128]{2,1,0:T(8,128)(2,1)S(1)}, bf16[4,288,128]{2,1,0:T(8,128)(2,1)S(1)}, u32[]{:S(2)}, u32[]{:S(2)}) collective-permute-start(bf16[4,288,128]{2,1,0:T(8,128)(2,1)S(1)} %pad_maximum_fusion.1.refs_0_), channel_id=1, source_target_pairs={{0,192},{64,128},{128,64},{192,0},{1,193},{65,129},{129,65},{193,1... | collective-permute-start | bytes 884744 | tf_op jit(solution)/shard_map/ppermute | solution.py:14
  47.7 6.7 %collective-permute-start.9 = (bf16[4,288,128]{2,1,0:T(8,128)(2,1)S(1)}, bf16[4,288,128]{2,1,0:T(8,128)(2,1)S(1)}, u32[]{:S(2)}, u32[]{:S(2)}) collective-permute-start(bf16[4,288,128]{2,1,0:T(8,128)(2,1)S(1)} %slice.151.refs_4_), channel_id=1, source_target_pairs={{0,48},{16,32},{32,16},{48,0},{1,49},{17,33},{33,17},{49,1},{2,50}... | collective-permute-start | bytes 884744 | tf_op jit(solution)/shard_map/ppermute | solution.py:14
  62.4 3.1 %collective-permute-start.12 = (f32[512,512]{1,0:T(8,128)}, f32[512,512]{1,0:T(8,128)S(1)}, u32[]{:S(2)}, u32[]{:S(2)}) collective-permute-start(f32[512,512]{1,0:T(8,128)} %get-tuple-element.80), channel_id=1, source_target_pairs={{0,1},{1,0},{2,3},{3,2},{4,5},{5,4},{6,7},{7,6},{8,9},{9,8},{10,11... | collective-permute-start | bytes 3145736 | tf_op jit(solution)/shard_map/ppermute | solution.py:14
  66.0 12.2 %collective-permute-start.13 = (bf16[4,576,512]{2,1,0:T(8,128)(2,1)}, bf16[4,576,512]{2,1,0:T(8,128)(2,1)}, u32[]{:S(2)}, u32[]{:S(2)}) collective-permute-start(bf16[4,576,512]{2,1,0:T(8,128)(2,1)} %get-tuple-element.85.here_ref), channel_id=1, source_target_pairs={{0,1},{1,0},{2,3},{3,2},{4,5},{5,4},{6,7},{7,6},{8,9},{9,8},{10,11... | collective-permute-start | bytes 7077896 | tf_op jit(solution)/shard_map/ppermute | solution.py:14
  66.8 11.3 %all-to-all-start.1 = ((f32[16,2,4,128]{3,2,1,0:T(4,128)}), f32[16,2,4,128]{3,2,1,0:T(4,128)S(1)}, u32[]{:S(2)}, u32[]{:S(2)}) async-start(f32[16,2,4,128]{3,2,1,0:T(4,128)} %broadcast_in_dim.31), calls=%async_computation.1 | async-start | bytes 131072 | tf_op jit(solution)/shard_map/all_to_all | solution.py:27
  78.2 14.9 %collective-permute-start.14 = (f32[512,512]{1,0:T(8,128)S(1)}, f32[512,512]{1,0:T(8,128)S(1)}, u32[]{:S(2)}, u32[]{:S(2)}) collective-permute-start(f32[512,512]{1,0:T(8,128)S(1)} %subtract_multiply_fusion.grown_ref), channel_id=1, source_target_pairs={{0,1},{1,0},{2,3},{3,2},{4,5},{5,4},{6,7},{7,6},{8,9},{9,8},{10,11... | collective-permute-start | bytes 3145736 | tf_op jit(solution)/shard_map/ppermute | solution.py:14
  79.3 13.8 %all-to-all-start.2 = ((f32[16,2,4,128]{3,2,1,0:T(4,128)}), f32[16,2,4,128]{3,2,1,0:T(4,128)S(1)}, u32[]{:S(2)}, u32[]{:S(2)}) async-start(f32[16,2,4,128]{3,2,1,0:T(4,128)} %broadcast_in_dim.32), calls=%async_computation.2 | async-start | bytes 131072 | tf_op jit(solution)/shard_map/all_to_all | solution.py:27
  96.6 8.2 %collective-permute-start.15 = (bf16[2,288,128]{2,1,0:T(8,128)(2,1)S(1)}, bf16[2,288,128]{2,1,0:T(8,128)(2,1)S(1)}, u32[]{:S(2)}, u32[]{:S(2)}) collective-permute-start(bf16[2,288,128]{2,1,0:T(8,128)(2,1)S(1)} %get-tuple-element.94), channel_id=1, source_target_pairs={{0,64},{64,0},{128,192},{192,128},{1,65},{65,1},{129,193},{193,129... | collective-permute-start | bytes 442376 | tf_op jit(solution)/shard_map/ppermute | solution.py:14
  97.2 7.6 %collective-permute-start.16 = (bf16[144,512]{1,0:T(8,128)(2,1)S(1)}, bf16[144,512]{1,0:T(8,128)(2,1)S(1)}, u32[]{:S(2)}, u32[]{:S(2)}) collective-permute-start(bf16[144,512]{1,0:T(8,128)(2,1)S(1)} %get-tuple-element.95), channel_id=1, source_target_pairs={{0,16},{16,0},{32,48},{48,32},{1,17},{17,1},{33,49},{49,33},{2,18}... | collective-permute-start | bytes 442376 | tf_op jit(solution)/shard_map/ppermute | solution.py:14
  98.7 6.4 %collective-permute-start.17 = (bf16[2,288,128]{2,1,0:T(8,128)(2,1)S(1)}, bf16[2,288,128]{2,1,0:T(8,128)(2,1)S(1)}, u32[]{:S(2)}, u32[]{:S(2)}) collective-permute-start(bf16[2,288,128]{2,1,0:T(8,128)(2,1)S(1)} %get-tuple-element.96), channel_id=1, source_target_pairs={{0,192},{64,128},{128,64},{192,0},{1,193},{65,129},{129,65},{193,1... | collective-permute-start | bytes 442376 | tf_op jit(solution)/shard_map/ppermute | solution.py:14
  100.0 5.1 %collective-permute-start.18 = (bf16[144,512]{1,0:T(8,128)(2,1)S(1)}, bf16[144,512]{1,0:T(8,128)(2,1)S(1)}, u32[]{:S(2)}, u32[]{:S(2)}) collective-permute-start(bf16[144,512]{1,0:T(8,128)(2,1)S(1)} %get-tuple-element.97), channel_id=1, source_target_pairs={{0,48},{16,32},{32,16},{48,0},{1,49},{17,33},{33,17},{49,1},{2,50}... | collective-permute-start | bytes 442376 | tf_op jit(solution)/shard_map/ppermute | solution.py:14
  105.4 6.8 %collective-permute-start.19 = (bf16[4,288,128]{2,1,0:T(8,128)(2,1)S(1)}, bf16[4,288,128]{2,1,0:T(8,128)(2,1)S(1)}, u32[]{:S(2)}, u32[]{:S(2)}) collective-permute-start(bf16[4,288,128]{2,1,0:T(8,128)(2,1)S(1)} %pad_maximum_fusion.2), channel_id=1, source_target_pairs={{0,64},{64,0},{128,192},{192,128},{1,65},{65,1},{129,193},{193,129... | collective-permute-start | bytes 884744 | tf_op jit(solution)/shard_map/ppermute | solution.py:14
  106.2 6.7 %collective-permute-start.20 = (bf16[288,512]{1,0:T(8,128)(2,1)S(1)}, bf16[288,512]{1,0:T(8,128)(2,1)S(1)}, u32[]{:S(2)}, u32[]{:S(2)}) collective-permute-start(bf16[288,512]{1,0:T(8,128)(2,1)S(1)} %pad_maximum_fusion.3), channel_id=1, source_target_pairs={{0,16},{16,0},{32,48},{48,32},{1,17},{17,1},{33,49},{49,33},{2,18}... | collective-permute-start | bytes 884744 | tf_op jit(solution)/shard_map/ppermute | solution.py:14
  108.0 7.9 %collective-permute-start.21 = (bf16[4,288,128]{2,1,0:T(8,128)(2,1)S(1)}, bf16[4,288,128]{2,1,0:T(8,128)(2,1)S(1)}, u32[]{:S(2)}, u32[]{:S(2)}) collective-permute-start(bf16[4,288,128]{2,1,0:T(8,128)(2,1)S(1)} %pad_maximum_fusion.4), channel_id=1, source_target_pairs={{0,192},{64,128},{128,64},{192,0},{1,193},{65,129},{129,65},{193,1... | collective-permute-start | bytes 884744 | tf_op jit(solution)/shard_map/ppermute | solution.py:14
  110.1 6.7 %collective-permute-start.22 = (bf16[288,512]{1,0:T(8,128)(2,1)S(1)}, bf16[288,512]{1,0:T(8,128)(2,1)S(1)}, u32[]{:S(2)}, u32[]{:S(2)}) collective-permute-start(bf16[288,512]{1,0:T(8,128)(2,1)S(1)} %pad_maximum_fusion.5), channel_id=1, source_target_pairs={{0,48},{16,32},{32,16},{48,0},{1,49},{17,33},{33,17},{49,1},{2,50}... | collective-permute-start | bytes 884744 | tf_op jit(solution)/shard_map/ppermute | solution.py:14
  117.1 5.2 %collective-permute-start.23 = (bf16[2,288,128]{2,1,0:T(8,128)(2,1)S(1)}, bf16[2,288,128]{2,1,0:T(8,128)(2,1)S(1)}, u32[]{:S(2)}, u32[]{:S(2)}) collective-permute-start(bf16[2,288,128]{2,1,0:T(8,128)(2,1)S(1)} %slice.206), channel_id=1, source_target_pairs={{0,16},{16,0},{32,48},{48,32},{1,17},{17,1},{33,49},{49,33},{2,18}... | collective-permute-start | bytes 442376 | tf_op jit(solution)/shard_map/ppermute | solution.py:14
  118.7 5.1 %collective-permute-start.24 = (bf16[288,256]{1,0:T(8,128)(2,1)S(1)}, bf16[288,256]{1,0:T(8,128)(2,1)S(1)}, u32[]{:S(2)}, u32[]{:S(2)}) collective-permute-start(bf16[288,256]{1,0:T(8,128)(2,1)S(1)} %slice.205), channel_id=1, source_target_pairs={{0,64},{64,0},{128,192},{192,128},{1,65},{65,1},{129,193},{193,129... | collective-permute-start | bytes 442376 | tf_op jit(solution)/shard_map/ppermute | solution.py:14
  123.9 4.4 %collective-permute-start.25 = (bf16[288,128]{1,0:T(8,128)(2,1)S(1)}, bf16[288,128]{1,0:T(8,128)(2,1)S(1)}, u32[]{:S(2)}, u32[]{:S(2)}) collective-permute-start(bf16[288,128]{1,0:T(8,128)(2,1)S(1)} %fusion.6), channel_id=1, source_target_pairs={{0,48},{16,32},{32,16},{48,0},{1,49},{17,33},{33,17},{49,1},{2,50}... | collective-permute-start | bytes 221192 | tf_op jit(solution)/shard_map/ppermute | solution.py:14
  125.2 5.6 %collective-permute-start.26 = (bf16[288,128]{1,0:T(8,128)(2,1)S(1)}, bf16[288,128]{1,0:T(8,128)(2,1)S(1)}, u32[]{:S(2)}, u32[]{:S(2)}) collective-permute-start(bf16[288,128]{1,0:T(8,128)(2,1)S(1)} %fusion.1), channel_id=1, source_target_pairs={{0,192},{64,128},{128,64},{192,0},{1,193},{65,129},{129,65},{193,1... | collective-permute-start | bytes 221192 | tf_op jit(solution)/shard_map/ppermute | solution.py:14
  130.8 1.5 collective-permute-start.27
  133.1 16.5 %all-to-all-start.3 = ((f32[8,72,128]{2,1,0:T(8,128)}), f32[8,72,128]{2,1,0:T(8,128)S(1)}, u32[]{:S(2)}, u32[]{:S(2)}) async-start(f32[8,72,128]{2,1,0:T(8,128)} %pad_maximum_fusion.7), calls=%async_computation.3 | async-start | bytes 589824 | tf_op jit(solution)/shard_map/all_to_all | solution.py:394

commit v4 on v3

--- a/solution.py
+++ b/solution.py
@@ -188,8 +188,8 @@
 
 
 def first_kernel(base_ref, wt_ref, grown_ref, grown_other_ref, tgt_ref, vectors_ref, *refs):
-    dls_ref, alo_ref, ahi_ref, blo_ref, bhi_ref, slots, sems = refs
-    part, rows = alo_ref.shape[1:]
+    dls_ref, a_ref, b_ref, slots, sems = refs
+    part, rows = a_ref.shape[1:]
     copies = fetch_blocks(wt_ref, FIRST_BLOCKS, slots, sems)
     start_all(copies)
     chunk = 64
@@ -203,10 +203,8 @@
     wait_all(copies)
     a = product(slots, 0, Y, dls_ref[:, 2 * rows : 3 * rows]).astype(BF16)
     for step in range(Y):
-        out_ref = alo_ref if step < Y // 2 else ahi_ref
-        out_ref[step % (Y // 2)] = a[step * part : (step + 1) * part]
-    b = product(slots, Y, Y + 1, dls_ref[...]).astype(BF16)
-    blo_ref[...], bhi_ref[...] = b[: part // 2], b[part // 2 :]
+        a_ref[step] = a[step * part : (step + 1) * part]
+    b_ref[...] = product(slots, Y, Y + 1, dls_ref[...]).astype(BF16)
 
 
 def first_call(base, wt, grown, grown_other, tgt, vectors):
@@ -215,14 +213,14 @@
     voc, all_rows = grown.shape
     part = wt.shape[2]
     dls = jax.ShapeDtypeStruct((2 * voc, all_rows), BF16)
-    a_half = jax.ShapeDtypeStruct((Y // 2, part, all_rows // X), BF16)
-    b_half = jax.ShapeDtypeStruct((part // 2, all_rows), BF16)
+    a_far = jax.ShapeDtypeStruct((Y, part, all_rows // X), BF16)
+    b_far = jax.ShapeDtypeStruct((part, all_rows), BF16)
     count = len(FIRST_BLOCKS)
     return pl.pallas_call(
         first_kernel,
-        out_shape=(dls, a_half, a_half, b_half, b_half),
+        out_shape=(dls, a_far, b_far),
         in_specs=[pl.BlockSpec(memory_space=pltpu.SMEM), hbm] + [vmem] * 4,
-        out_specs=tuple([vmem] * 5),
+        out_specs=(vmem,) * 3,
         scratch_shapes=[
             pltpu.VMEM((count, part, 2 * voc), BF16),
             pltpu.SemaphoreType.DMA((count,)),
@@ -362,17 +360,13 @@
     vectors = jnp.stack([(1.0 / stats[0]).reshape(-1), at_target.reshape(-1)])
     base = jnp.stack([offset, offset + (1 - 2 * c) * voc])
 
-    dls, a_lo, a_hi, b_lo, b_hi = first_call(base, wt, grown, grown_other, tgt[None], vectors)
-    a_lo, b_lo, a_hi, b_hi = at_once(
-        flip(a_lo, "x", X, 1), flip(b_lo, "y", Y, 1), flip(a_hi, "x", X, 3), flip(b_hi, "y", Y, 3)
-    )
+    dls, a_far, b_far = first_call(base, wt, grown, grown_other, tgt[None], vectors)
+    a_far, b_far = at_once(flip(a_far, "x", X, 1), flip(b_far, "y", Y, 1))
     a_kind = jax.ShapeDtypeStruct((Y, part, rows), F32)
     b_kind = jax.ShapeDtypeStruct((part, X * rows), F32)
     a0, a1, a3, b0, b1, b3 = rest_call([a_kind] * 3 + [b_kind] * 3, wt, dls)
-    a1 = jnp.concatenate([a1[: Y // 2], a1[Y // 2 :] + a_hi.astype(F32)]).astype(BF16)
-    a3 = jnp.concatenate([a3[: Y // 2] + a_lo.astype(F32), a3[Y // 2 :]]).astype(BF16)
-    b1 = jnp.concatenate([b1[: part // 2], b1[part // 2 :] + b_hi.astype(F32)]).astype(BF16)
-    b3 = jnp.concatenate([b3[: part // 2] + b_lo.astype(F32), b3[part // 2 :]]).astype(BF16)
+    a1, a3 = a1.astype(BF16), (a3 + a_far.astype(F32)).astype(BF16)
+    b1, b3 = b1.astype(BF16), (b3 + b_far.astype(F32)).astype(BF16)
     a1, b1, a3, b3 = at_once(a1, b1, a3, b3)
     a1, b1, a3, b3 = at_once(flip(a1, "x", X, 1), flip(b1, "y", Y, 1), flip(a3, "x", X, 3), flip(b3, "y", Y, 3))
     a_own = a0 + a1.astype(F32) + a3.astype(F32)

time: 152 us -> 151 us (level)
  starting transfers between devices: 53.2 us -> 51.6 us
    ppermute x28 -> x26, starting transfers between devices: 30.3 us -> 28.7 us  [flip(): return lax.ppermute(array, axis, [(i, i ^ change) for i in range(size)])]
    ppermute x28 -> x26, waiting for transfers between devices: 36.1 us -> 37 us  [flip(): return lax.ppermute(array, axis, [(i, i ^ change) for i in range(size)])]
  transfers between devices with their start and end apart: 32 -> 30, of which waited for: 22 -> 21; matrix products, arithmetic and copies ran while one was open for 3% -> 3% of each run, Pallas kernels for 11% -> 12%
where the time goes in v4:
time: 151 us; the launch traced here: 149 us
  waiting for transfers between devices  60 us (40%)
  starting transfers between devices  51.6 us (34%)
  Pallas kernels  28.5 us (19%)
  other arithmetic  4.67 us (3%)
  local copies, waits for them, and re-layouts  3 us (2%)
    ppermute x26, waiting for transfers between devices, flip(): return lax.ppermute(array, axis, [(i, i ^ change) for i in range(size)])  37 us
    ppermute x26, starting transfers between devices, flip(): return lax.ppermute(array, axis, [(i, i ^ change) for i in range(size)])  28.7 us
    all_to_all x3, starting transfers between devices, spread(): return lax.all_to_all(copies, axes, 0, 0, tiled=True)  19.4 us
    all_to_all x3, waiting for transfers between devices, spread(): return lax.all_to_all(copies, axes, 0, 0, tiled=True)  18.1 us
    pallas_call x1, Pallas kernels, logits_of(): pl.pallas_call(logits_kernel, out_shape=(square, square, pltpu.HBM((Y, 2...  7.94 us
    pallas_call x1, Pallas kernels, weight_of(): pl.pallas_call(weight_kernel, out_shape=jax.ShapeDtypeStruct((voc, Y * 2...  7.52 us
    pallas_call x1, Pallas kernels, turned_weights(): pl.pallas_call(turn_kernel, out_shape=pltpu.HBM((Y, 2, part, 2 * voc), BF...  5.44 us
    all_to_all x1, waiting for transfers between devices, per_device(): lax.all_to_all(by_z, 'z', 0, 0, tiled=True).sum(0).astype(BF16)  4.96 us
  transfers between devices with their start and end apart: 30, of which 21 were waited for; matrix products, arithmetic and copies ran while one was open for 3% of the time, Pallas kernels for 12%

profile of v4, /device:TPU:8, one launch (start us, length us, event | category | flops | bytes accessed | tf_op | source)
XLA Modules:
  0.0 148.8 jit_solution(7463095315408073788)
XLA Ops:
  0.7 1.4 broadcast_in_dim.14
  2.1 8.5 %all-to-all-start = ((bf16[8,72,128]{2,1,0:T(8,128)(2,1)}), bf16[8,72,128]{2,1,0:T(8,128)(2,1)S(1)}, u32[]{:S(2)}, u32[]{:S(2)}) async-start(bf16[8,72,128]{2,1,0:T(8,128)(2,1)} %broadcast_in_dim.14), calls=%async_computation | async-start | bytes 294912 | tf_op jit(solution)/shard_map/all_to_all | solution.py:27
  10.8 5.4 %shard_map.58.wt_ref = bf16[4,2,288,1024]{3,2,1,0:T(8,128)(2,1)} custom-call(s32[10]{0:T(128)S(1)} %pad_add_fusion.1.meta_ref, bf16[512,4608]{1,0:T(8,128)(2,1)} %own_ref.3, bf16[512,4608]{1,0:T(8,128)(2,1)} %collective-permute-done.other_ref), custom_call_target="tpu_custom_call" | custom-call | bytes 9437184 | tf_op jit(solution)/shard_map/pallas_call | solution.py:158
  16.2 4.5 %all-to-all-done = bf16[8,72,128]{2,1,0:T(8,128)(2,1)S(1)} async-done(((bf16[8,72,128]{2,1,0:T(8,128)(2,1)}), bf16[8,72,128]{2,1,0:T(8,128)(2,1)S(1)}, u32[]{:S(2)}, u32[]{:S(2)}) %all-to-all-start) | async-done | bytes 147488 | tf_op jit(solution)/shard_map/all_to_all | solution.py:27
  20.7 1.2 collective-permute-done.1
  22.1 1.6 %collective-permute-start.3 = (bf16[296,128]{1,0:T(8,128)(2,1)S(1)}, bf16[296,128]{1,0:T(8,128)(2,1)S(1)}, u32[]{:S(2)}, u32[]{:S(2)}) collective-permute-start(bf16[296,128]{1,0:T(8,128)(2,1)S(1)} %concatenate.31), channel_id=1, source_target_pairs={{0,64},{64,0},{128,192},{192,128},{1,65},{65,1},{129,193},{193,129... | collective-permute-start | bytes 227336 | tf_op jit(solution)/shard_map/ppermute | solution.py:14
  24.1 3.9 %collective-permute-done.2 = bf16[288,128]{1,0:T(8,128)(2,1)S(1)} collective-permute-done((bf16[288,128]{1,0:T(8,128)(2,1)S(1)}, bf16[288,128]{1,0:T(8,128)(2,1)S(1)}, u32[]{:S(2)}, u32[]{:S(2)}) %collective-permute-start.2) | collective-permute-done | bytes 73760 | tf_op jit(solution)/shard_map/ppermute | solution.py:14
  28.0 2.2 %collective-permute-start.5 = (bf16[2,296,128]{2,1,0:T(8,128)(2,1)S(1)}, bf16[2,296,128]{2,1,0:T(8,128)(2,1)S(1)}, u32[]{:S(2)}, u32[]{:S(2)}) collective-permute-start(bf16[2,296,128]{2,1,0:T(8,128)(2,1)S(1)} %pad_maximum_fusion.4), channel_id=1, source_target_pairs={{0,192},{64,128},{128,64},{192,0},{1,193},{65,129},{129,65},{193,1... | collective-permute-start | bytes 454664 | tf_op jit(solution)/shard_map/ppermute | solution.py:14
  30.2 1.7 %collective-permute-start.4 = (bf16[2,288,128]{2,1,0:T(8,128)(2,1)S(1)}, bf16[2,288,128]{2,1,0:T(8,128)(2,1)S(1)}, u32[]{:S(2)}, u32[]{:S(2)}) collective-permute-start(bf16[2,288,128]{2,1,0:T(8,128)(2,1)S(1)} %pad_maximum_fusion.5), channel_id=1, source_target_pairs={{0,48},{16,32},{32,16},{48,0},{1,49},{17,33},{33,17},{49,1},{2,50}... | collective-permute-start | bytes 442376 | tf_op jit(solution)/shard_map/ppermute | solution.py:14
  31.9 3.6 %collective-permute-done.4 = bf16[2,288,128]{2,1,0:T(8,128)(2,1)S(1)} collective-permute-done((bf16[2,288,128]{2,1,0:T(8,128)(2,1)S(1)}, bf16[2,288,128]{2,1,0:T(8,128)(2,1)S(1)}, u32[]{:S(2)}, u32[]{:S(2)}) %collective-permute-start.4) | collective-permute-done | bytes 147488 | tf_op jit(solution)/shard_map/ppermute | solution.py:14
  35.6 0.7 collective-permute-start.10
  36.4 1.3 collective-permute-start.6
  37.7 3.5 %collective-permute-start.11 = (bf16[4,288,128]{2,1,0:T(8,128)(2,1)S(1)}, bf16[4,288,128]{2,1,0:T(8,128)(2,1)S(1)}, u32[]{:S(2)}, u32[]{:S(2)}) collective-permute-start(bf16[4,288,128]{2,1,0:T(8,128)(2,1)S(1)} %slice.115.refs_4_), channel_id=1, source_target_pairs={{0,32},{16,48},{32,0},{48,16},{1,33},{17,49},{33,1},{49,17},{2,34}... | collective-permute-start | bytes 884744 | tf_op jit(solution)/shard_map/ppermute | solution.py:14
  41.4 2.1 %collective-permute-start.8 = (bf16[4,288,128]{2,1,0:T(8,128)(2,1)S(1)}, bf16[4,288,128]{2,1,0:T(8,128)(2,1)S(1)}, u32[]{:S(2)}, u32[]{:S(2)}) collective-permute-start(bf16[4,288,128]{2,1,0:T(8,128)(2,1)S(1)} %pad_maximum_fusion.1.refs_0_), channel_id=1, source_target_pairs={{0,192},{64,128},{128,64},{192,0},{1,193},{65,129},{129,65},{193,1... | collective-permute-start | bytes 884744 | tf_op jit(solution)/shard_map/ppermute | solution.py:14
  43.5 3.7 %collective-permute-done.10.refs_2_ = bf16[4,288,128]{2,1,0:T(8,128)(2,1)S(1)} collective-permute-done((bf16[4,288,128]{2,1,0:T(8,128)(2,1)S(1)}, bf16[4,288,128]{2,1,0:T(8,128)(2,1)S(1)}, u32[]{:S(2)}, u32[]{:S(2)}) %collective-permute-start.10) | collective-permute-done | bytes 294944 | tf_op jit(solution)/shard_map/ppermute | solution.py:14
  47.2 1.7 %collective-permute-start.9 = (bf16[4,288,128]{2,1,0:T(8,128)(2,1)S(1)}, bf16[4,288,128]{2,1,0:T(8,128)(2,1)S(1)}, u32[]{:S(2)}, u32[]{:S(2)}) collective-permute-start(bf16[4,288,128]{2,1,0:T(8,128)(2,1)S(1)} %slice.115.refs_4_), channel_id=1, source_target_pairs={{0,48},{16,32},{32,16},{48,0},{1,49},{17,33},{33,17},{49,1},{2,50}... | collective-permute-start | bytes 884744 | tf_op jit(solution)/shard_map/ppermute | solution.py:14
  48.9 3.0 %collective-permute-done.7.refs_5_ = bf16[4,288,128]{2,1,0:T(8,128)(2,1)S(1)} collective-permute-done((bf16[4,288,128]{2,1,0:T(8,128)(2,1)S(1)}, bf16[4,288,128]{2,1,0:T(8,128)(2,1)S(1)}, u32[]{:S(2)}, u32[]{:S(2)}) %collective-permute-start.7) | collective-permute-done | bytes 294944 | tf_op jit(solution)/shard_map/ppermute | solution.py:14
  51.9 2.1 %collective-permute-done.9.refs_7_ = bf16[4,288,128]{2,1,0:T(8,128)(2,1)S(1)} collective-permute-done((bf16[4,288,128]{2,1,0:T(8,128)(2,1)S(1)}, bf16[4,288,128]{2,1,0:T(8,128)(2,1)S(1)}, u32[]{:S(2)}, u32[]{:S(2)}) %collective-permute-start.9) | collective-permute-done | bytes 294944 | tf_op jit(solution)/shard_map/ppermute | solution.py:14
  54.0 7.9 %shard_map.59 = (f32[512,512]{1,0:T(8,128)S(1)}, f32[512,512]{1,0:T(8,128)}, bf16[4,576,512]{2,1,0:T(8,128)(2,1)}) custom-call(s32[5]{0:T(128)S(1)} %pad_add_fusion.meta_ref, bf16[512,4608]{1,0:T(8,128)(2,1)} %own_ref.3, bf16[512,4608]{1,0:T(8,128)(2,1)} %collective-permute-done.other_ref, bf16[4,288,128]{2,1,0:T(8,128)(2,1)S(1)} %pad_maximum_fusion.1.refs_0_, ...), custom_call_target="tpu_custom_call" | custom-call | flops 2684354560 | bytes 5242880 | tf_op jit(solution)/shard_map/pallas_call | solution.py:109
  62.3 0.8 fusion.10
  63.1 2.0 %collective-permute-done.12 = f32[512,512]{1,0:T(8,128)S(1)} collective-permute-done((f32[512,512]{1,0:T(8,128)}, f32[512,512]{1,0:T(8,128)S(1)}, u32[]{:S(2)}, u32[]{:S(2)}) %collective-permute-start.12) | collective-permute-done | bytes 1048608 | tf_op jit(solution)/shard_map/ppermute | solution.py:14
  65.7 0.6 broadcast_in_dim.31
  66.4 3.5 %all-to-all-start.1 = ((f32[16,2,4,128]{3,2,1,0:T(4,128)}), f32[16,2,4,128]{3,2,1,0:T(4,128)S(1)}, u32[]{:S(2)}, u32[]{:S(2)}) async-start(f32[16,2,4,128]{3,2,1,0:T(4,128)} %broadcast_in_dim.31), calls=%async_computation.1 | async-start | bytes 131072 | tf_op jit(solution)/shard_map/all_to_all | solution.py:27
  70.3 7.4 %all-to-all-done.1 = f32[16,2,4,128]{3,2,1,0:T(4,128)S(1)} async-done(((f32[16,2,4,128]{3,2,1,0:T(4,128)}), f32[16,2,4,128]{3,2,1,0:T(4,128)S(1)}, u32[]{:S(2)}, u32[]{:S(2)}) %all-to-all-start.1) | async-done | bytes 65568 | tf_op jit(solution)/shard_map/all_to_all | solution.py:27
  78.8 7.5 %all-to-all-start.2 = ((f32[16,2,4,128]{3,2,1,0:T(4,128)}), f32[16,2,4,128]{3,2,1,0:T(4,128)S(1)}, u32[]{:S(2)}, u32[]{:S(2)}) async-start(f32[16,2,4,128]{3,2,1,0:T(4,128)} %broadcast_in_dim.32), calls=%async_computation.2 | async-start | bytes 131072 | tf_op jit(solution)/shard_map/all_to_all | solution.py:27
  86.4 6.2 %all-to-all-done.2 = f32[16,2,4,128]{3,2,1,0:T(4,128)S(1)} async-done(((f32[16,2,4,128]{3,2,1,0:T(4,128)}), f32[16,2,4,128]{3,2,1,0:T(4,128)S(1)}, u32[]{:S(2)}, u32[]{:S(2)}) %all-to-all-start.2) | async-done | bytes 65568 | tf_op jit(solution)/shard_map/all_to_all | solution.py:27
  92.7 3.5 %shard_map.60 = (bf16[1024,512]{1,0:T(8,128)(2,1)S(1)}, bf16[4,288,128]{2,1,0:T(8,128)(2,1)S(1)}, bf16[288,512]{1,0:T(8,128)(2,1)S(1)}) custom-call(s32[2]{0:T(128)S(1)} %pad_add_fusion.2.base_ref, bf16[4,2,288,1024]{3,2,1,0:T(8,128)(2,1)} %shard_map.58.wt_ref, f32[512,512]{1,0:T(8,128)S(1)} %subtract_multiply_fusion.grown_ref, ...), custom_call_target="tpu_custom_call" | custom-call | flops 603979776 | bytes 4456448 | tf_op jit(solution)/shard_map/pallas_call | solution.py:219
  96.8 1.5 collective-permute-start.16
  98.3 4.2 %shard_map.61 = (f32[4,288,128]{2,1,0:T(8,128)S(1)}, f32[4,288,128]{2,1,0:T(8,128)S(1)}, f32[4,288,128]{2,1,0:T(8,128)S(1)}, f32[288,512]{1,0:T(8,128)S(1)}, f32...) custom-call(bf16[4,2,288,1024]{3,2,1,0:T(8,128)(2,1)} %shard_map.58.wt_ref, ...), custom_call_target="tpu_custom_call" | custom-call | flops 2113929216 | bytes 4128768 | tf_op jit(solution)/shard_map/pallas_call | solution.py:257
  102.5 1.5 collective-permute-done.15
  104.3 1.7 %collective-permute-start.17 = (bf16[4,288,128]{2,1,0:T(8,128)(2,1)S(1)}, bf16[4,288,128]{2,1,0:T(8,128)(2,1)S(1)}, u32[]{:S(2)}, u32[]{:S(2)}) collective-permute-start(bf16[4,288,128]{2,1,0:T(8,128)(2,1)S(1)} %convert_element_type.73), channel_id=1, source_target_pairs={{0,64},{64,0},{128,192},{192,128},{1,65},{65,1},{129,193},{193,129... | collective-permute-start | bytes 884744 | tf_op jit(solution)/shard_map/ppermute | solution.py:14
  106.0 1.4 collective-permute-start.18
  107.4 1.1 collective-permute-start.19
  109.1 2.0 %collective-permute-done.17 = bf16[4,288,128]{2,1,0:T(8,128)(2,1)S(1)} collective-permute-done((bf16[4,288,128]{2,1,0:T(8,128)(2,1)S(1)}, bf16[4,288,128]{2,1,0:T(8,128)(2,1)S(1)}, u32[]{:S(2)}, u32[]{:S(2)}) %collective-permute-start.17) | collective-permute-done | bytes 294944 | tf_op jit(solution)/shard_map/ppermute | solution.py:14
  111.1 1.6 %collective-permute-done.18 = bf16[288,512]{1,0:T(8,128)(2,1)S(1)} collective-permute-done((bf16[288,512]{1,0:T(8,128)(2,1)S(1)}, bf16[288,512]{1,0:T(8,128)(2,1)S(1)}, u32[]{:S(2)}, u32[]{:S(2)}) %collective-permute-start.18) | collective-permute-done | bytes 294944 | tf_op jit(solution)/shard_map/ppermute | solution.py:14
  112.7 2.6 %collective-permute-done.19 = bf16[4,288,128]{2,1,0:T(8,128)(2,1)S(1)} collective-permute-done((bf16[4,288,128]{2,1,0:T(8,128)(2,1)S(1)}, bf16[4,288,128]{2,1,0:T(8,128)(2,1)S(1)}, u32[]{:S(2)}, u32[]{:S(2)}) %collective-permute-start.19) | collective-permute-done | bytes 294944 | tf_op jit(solution)/shard_map/ppermute | solution.py:14
  115.6 1.8 %collective-permute-start.21 = (bf16[2,288,128]{2,1,0:T(8,128)(2,1)S(1)}, bf16[2,288,128]{2,1,0:T(8,128)(2,1)S(1)}, u32[]{:S(2)}, u32[]{:S(2)}) collective-permute-start(bf16[2,288,128]{2,1,0:T(8,128)(2,1)S(1)} %slice.158), channel_id=1, source_target_pairs={{0,16},{16,0},{32,48},{48,32},{1,17},{17,1},{33,49},{49,33},{2,18}... | collective-permute-start | bytes 442376 | tf_op jit(solution)/shard_map/ppermute | solution.py:14
  117.7 3.1 %collective-permute-done.21 = bf16[2,288,128]{2,1,0:T(8,128)(2,1)S(1)} collective-permute-done((bf16[2,288,128]{2,1,0:T(8,128)(2,1)S(1)}, bf16[2,288,128]{2,1,0:T(8,128)(2,1)S(1)}, u32[]{:S(2)}, u32[]{:S(2)}) %collective-permute-start.21) | collective-permute-done | bytes 147488 | tf_op jit(solution)/shard_map/ppermute | solution.py:14
  120.8 1.7 %collective-permute-done.22 = bf16[288,256]{1,0:T(8,128)(2,1)S(1)} collective-permute-done((bf16[288,256]{1,0:T(8,128)(2,1)S(1)}, bf16[288,256]{1,0:T(8,128)(2,1)S(1)}, u32[]{:S(2)}, u32[]{:S(2)}) %collective-permute-start.22) | collective-permute-done | bytes 147488 | tf_op jit(solution)/shard_map/ppermute | solution.py:14
  122.5 1.2 collective-permute-start.23
  123.7 2.1 %collective-permute-start.24 = (bf16[288,128]{1,0:T(8,128)(2,1)S(1)}, bf16[288,128]{1,0:T(8,128)(2,1)S(1)}, u32[]{:S(2)}, u32[]{:S(2)}) collective-permute-start(bf16[288,128]{1,0:T(8,128)(2,1)S(1)} %fusion.1), channel_id=1, source_target_pairs={{0,192},{64,128},{128,64},{192,0},{1,193},{65,129},{129,65},{193,1... | collective-permute-start | bytes 221192 | tf_op jit(solution)/shard_map/ppermute | solution.py:14
  125.8 1.2 collective-permute-done.23
  127.0 2.3 %collective-permute-done.24 = bf16[288,128]{1,0:T(8,128)(2,1)S(1)} collective-permute-done((bf16[288,128]{1,0:T(8,128)(2,1)S(1)}, bf16[288,128]{1,0:T(8,128)(2,1)S(1)}, u32[]{:S(2)}, u32[]{:S(2)}) %collective-permute-start.24) | collective-permute-done | bytes 73760 | tf_op jit(solution)/shard_map/ppermute | solution.py:14
  129.5 1.4 collective-permute-done.25
  130.9 0.8 pad_maximum_fusion.3
  131.6 3.4 %all-to-all-start.3 = ((f32[8,72,128]{2,1,0:T(8,128)}), f32[8,72,128]{2,1,0:T(8,128)S(1)}, u32[]{:S(2)}, u32[]{:S(2)}) async-start(f32[8,72,128]{2,1,0:T(8,128)} %pad_maximum_fusion.3), calls=%async_computation.3 | async-start | bytes 589824 | tf_op jit(solution)/shard_map/all_to_all | solution.py:388
  135.7 7.5 %shard_map.62 = bf16[512,4608]{1,0:T(8,128)(2,1)} custom-call(s32[5]{0:T(128)S(1)} %concatenate.36.places_ref, bf16[1024,512]{1,0:T(8,128)(2,1)S(1)} %get-tuple-element.115.dls_ref.dl_ref, bf16[4,576,512]{2,1,0:T(8,128)(2,1)} %get-tuple-element.81.here_ref, bf16[4,576,512]{2,1,0:T(8,128)(2,1)} %collective-permute-done.13.there_ref), custom_call_target="tpu_custom_call" | custom-call | flops 2415919104 | bytes 9437184 | tf_op jit(solution)/shard_map/pallas_call | solution.py:283
  143.2 5.0 %all-to-all-done.3 = f32[8,72,128]{2,1,0:T(8,128)S(1)} async-done(((f32[8,72,128]{2,1,0:T(8,128)}), f32[8,72,128]{2,1,0:T(8,128)S(1)}, u32[]{:S(2)}, u32[]{:S(2)}) %all-to-all-start.3) | async-done | bytes 294944 | tf_op jit(solution)/shard_map/all_to_all | solution.py:388
  (78 shorter events, 7.5 us)
Async XLA Ops:
  0.6 10.2 %collective-permute-start = (bf16[512,4608]{1,0:T(8,128)(2,1)}, bf16[512,4608]{1,0:T(8,128)(2,1)}, u32[]{:S(2)}, u32[]{:S(2)}) collective-permute-start(bf16[512,4608]{1,0:T(8,128)(2,1)} %own_ref.3), channel_id=1, source_target_pairs={{0,1},{1,0},{2,3},{3,2},{4,5},{5,4},{6,7},{7,6},{8,9},{9,8},{10,11... | collective-permute-start | bytes 14155784 | tf_op jit(solution)/shard_map/ppermute | solution.py:14
  2.1 18.5 %all-to-all-start = ((bf16[8,72,128]{2,1,0:T(8,128)(2,1)}), bf16[8,72,128]{2,1,0:T(8,128)(2,1)S(1)}, u32[]{:S(2)}, u32[]{:S(2)}) async-start(bf16[8,72,128]{2,1,0:T(8,128)(2,1)} %broadcast_in_dim.14), calls=%async_computation | async-start | bytes 294912 | tf_op jit(solution)/shard_map/all_to_all | solution.py:27
  10.8 9.9 %copy-start.3 = (s32[128]{0:T(128)S(1)}, s32[128]{0:T(128)}, u32[]{:S(2)}) copy-start(s32[128]{0:T(128)} %param.5) | copy-start | bytes 1540
  20.7 1.3 collective-permute-start.1
  22.1 5.9 %collective-permute-start.3 = (bf16[296,128]{1,0:T(8,128)(2,1)S(1)}, bf16[296,128]{1,0:T(8,128)(2,1)S(1)}, u32[]{:S(2)}, u32[]{:S(2)}) collective-permute-start(bf16[296,128]{1,0:T(8,128)(2,1)S(1)} %concatenate.31), channel_id=1, source_target_pairs={{0,64},{64,0},{128,192},{192,128},{1,65},{65,1},{129,193},{193,129... | collective-permute-start | bytes 227336 | tf_op jit(solution)/shard_map/ppermute | solution.py:14
  23.6 4.4 %collective-permute-start.2 = (bf16[288,128]{1,0:T(8,128)(2,1)S(1)}, bf16[288,128]{1,0:T(8,128)(2,1)S(1)}, u32[]{:S(2)}, u32[]{:S(2)}) collective-permute-start(bf16[288,128]{1,0:T(8,128)(2,1)S(1)} %bitcast.72), channel_id=1, source_target_pairs={{0,16},{16,0},{32,48},{48,32},{1,17},{17,1},{33,49},{49,33},{2,18}... | collective-permute-start | bytes 221192 | tf_op jit(solution)/shard_map/ppermute | solution.py:14
  28.0 19.2 %copy-start = (bf16[296,128]{1,0:T(8,128)(2,1)}, bf16[296,128]{1,0:T(8,128)(2,1)S(1)}, u32[]{:S(2)}) copy-start(bf16[296,128]{1,0:T(8,128)(2,1)S(1)} %collective-permute-done.3) | copy-start | bytes 227332
  28.0 7.4 %collective-permute-start.5 = (bf16[2,296,128]{2,1,0:T(8,128)(2,1)S(1)}, bf16[2,296,128]{2,1,0:T(8,128)(2,1)S(1)}, u32[]{:S(2)}, u32[]{:S(2)}) collective-permute-start(bf16[2,296,128]{2,1,0:T(8,128)(2,1)S(1)} %pad_maximum_fusion.4), channel_id=1, source_target_pairs={{0,192},{64,128},{128,64},{192,0},{1,193},{65,129},{129,65},{193,1... | collective-permute-start | bytes 454664 | tf_op jit(solution)/shard_map/ppermute | solution.py:14
  30.2 5.2 %collective-permute-start.4 = (bf16[2,288,128]{2,1,0:T(8,128)(2,1)S(1)}, bf16[2,288,128]{2,1,0:T(8,128)(2,1)S(1)}, u32[]{:S(2)}, u32[]{:S(2)}) collective-permute-start(bf16[2,288,128]{2,1,0:T(8,128)(2,1)S(1)} %pad_maximum_fusion.5), channel_id=1, source_target_pairs={{0,48},{16,32},{32,16},{48,0},{1,49},{17,33},{33,17},{49,1},{2,50}... | collective-permute-start | bytes 442376 | tf_op jit(solution)/shard_map/ppermute | solution.py:14
  35.5 11.7 %copy-start.1 = (bf16[1,296,128]{2,1,0:T(8,128)(2,1)}, bf16[1,296,128]{2,1,0:T(8,128)(2,1)S(1)}, u32[]{:S(2)}) copy-start(bf16[1,296,128]{2,1,0:T(8,128)(2,1)S(1)} %get-tuple-element.125) | copy-start | bytes 227332
  35.5 11.7 %copy-start.2 = (bf16[1,296,128]{2,1,0:T(8,128)(2,1)}, bf16[1,296,128]{2,1,0:T(8,128)(2,1)S(1)}, u32[]{:S(2)}) copy-start(bf16[1,296,128]{2,1,0:T(8,128)(2,1)S(1)} %get-tuple-element.126) | copy-start | bytes 227332
  35.6 11.5 %collective-permute-start.10 = (bf16[4,288,128]{2,1,0:T(8,128)(2,1)S(1)}, bf16[4,288,128]{2,1,0:T(8,128)(2,1)S(1)}, u32[]{:S(2)}, u32[]{:S(2)}) collective-permute-start(bf16[4,288,128]{2,1,0:T(8,128)(2,1)S(1)} %pad_maximum_fusion.1.refs_0_), channel_id=1, source_target_pairs={{0,128},{64,192},{128,0},{192,64},{1,129},{65,193},{129,1},{193,65... | collective-permute-start | bytes 884744 | tf_op jit(solution)/shard_map/ppermute | solution.py:14
  36.4 12.6 %collective-permute-start.6 = (bf16[4,288,128]{2,1,0:T(8,128)(2,1)S(1)}, bf16[4,288,128]{2,1,0:T(8,128)(2,1)S(1)}, u32[]{:S(2)}, u32[]{:S(2)}) collective-permute-start(bf16[4,288,128]{2,1,0:T(8,128)(2,1)S(1)} %pad_maximum_fusion.1.refs_0_), channel_id=1, source_target_pairs={{0,64},{64,0},{128,192},{192,128},{1,65},{65,1},{129,193},{193,129... | collective-permute-start | bytes 884744 | tf_op jit(solution)/shard_map/ppermute | solution.py:14
  37.7 11.2 %collective-permute-start.11 = (bf16[4,288,128]{2,1,0:T(8,128)(2,1)S(1)}, bf16[4,288,128]{2,1,0:T(8,128)(2,1)S(1)}, u32[]{:S(2)}, u32[]{:S(2)}) collective-permute-start(bf16[4,288,128]{2,1,0:T(8,128)(2,1)S(1)} %slice.115.refs_4_), channel_id=1, source_target_pairs={{0,32},{16,48},{32,0},{48,16},{1,33},{17,49},{33,1},{49,17},{2,34}... | collective-permute-start | bytes 884744 | tf_op jit(solution)/shard_map/ppermute | solution.py:14
  41.2 10.7 %collective-permute-start.7 = (bf16[4,288,128]{2,1,0:T(8,128)(2,1)S(1)}, bf16[4,288,128]{2,1,0:T(8,128)(2,1)S(1)}, u32[]{:S(2)}, u32[]{:S(2)}) collective-permute-start(bf16[4,288,128]{2,1,0:T(8,128)(2,1)S(1)} %slice.115.refs_4_), channel_id=1, source_target_pairs={{0,16},{16,0},{32,48},{48,32},{1,17},{17,1},{33,49},{49,33},{2,18}... | collective-permute-start | bytes 884744 | tf_op jit(solution)/shard_map/ppermute | solution.py:14
  41.4 10.5 %collective-permute-start.8 = (bf16[4,288,128]{2,1,0:T(8,128)(2,1)S(1)}, bf16[4,288,128]{2,1,0:T(8,128)(2,1)S(1)}, u32[]{:S(2)}, u32[]{:S(2)}) collective-permute-start(bf16[4,288,128]{2,1,0:T(8,128)(2,1)S(1)} %pad_maximum_fusion.1.refs_0_), channel_id=1, source_target_pairs={{0,192},{64,128},{128,64},{192,0},{1,193},{65,129},{129,65},{193,1... | collective-permute-start | bytes 884744 | tf_op jit(solution)/shard_map/ppermute | solution.py:14
  47.2 6.8 %collective-permute-start.9 = (bf16[4,288,128]{2,1,0:T(8,128)(2,1)S(1)}, bf16[4,288,128]{2,1,0:T(8,128)(2,1)S(1)}, u32[]{:S(2)}, u32[]{:S(2)}) collective-permute-start(bf16[4,288,128]{2,1,0:T(8,128)(2,1)S(1)} %slice.115.refs_4_), channel_id=1, source_target_pairs={{0,48},{16,32},{32,16},{48,0},{1,49},{17,33},{33,17},{49,1},{2,50}... | collective-permute-start | bytes 884744 | tf_op jit(solution)/shard_map/ppermute | solution.py:14
  61.9 3.1 %collective-permute-start.12 = (f32[512,512]{1,0:T(8,128)}, f32[512,512]{1,0:T(8,128)S(1)}, u32[]{:S(2)}, u32[]{:S(2)}) collective-permute-start(f32[512,512]{1,0:T(8,128)} %get-tuple-element.76), channel_id=1, source_target_pairs={{0,1},{1,0},{2,3},{3,2},{4,5},{5,4},{6,7},{7,6},{8,9},{9,8},{10,11... | collective-permute-start | bytes 3145736 | tf_op jit(solution)/shard_map/ppermute | solution.py:14
  65.5 12.2 %collective-permute-start.13 = (bf16[4,576,512]{2,1,0:T(8,128)(2,1)}, bf16[4,576,512]{2,1,0:T(8,128)(2,1)}, u32[]{:S(2)}, u32[]{:S(2)}) collective-permute-start(bf16[4,576,512]{2,1,0:T(8,128)(2,1)} %get-tuple-element.81.here_ref), channel_id=1, source_target_pairs={{0,1},{1,0},{2,3},{3,2},{4,5},{5,4},{6,7},{7,6},{8,9},{9,8},{10,11... | collective-permute-start | bytes 7077896 | tf_op jit(solution)/shard_map/ppermute | solution.py:14
  66.4 11.3 %all-to-all-start.1 = ((f32[16,2,4,128]{3,2,1,0:T(4,128)}), f32[16,2,4,128]{3,2,1,0:T(4,128)S(1)}, u32[]{:S(2)}, u32[]{:S(2)}) async-start(f32[16,2,4,128]{3,2,1,0:T(4,128)} %broadcast_in_dim.31), calls=%async_computation.1 | async-start | bytes 131072 | tf_op jit(solution)/shard_map/all_to_all | solution.py:27
  77.7 14.9 %collective-permute-start.14 = (f32[512,512]{1,0:T(8,128)S(1)}, f32[512,512]{1,0:T(8,128)S(1)}, u32[]{:S(2)}, u32[]{:S(2)}) collective-permute-start(f32[512,512]{1,0:T(8,128)S(1)} %subtract_multiply_fusion.grown_ref), channel_id=1, source_target_pairs={{0,1},{1,0},{2,3},{3,2},{4,5},{5,4},{6,7},{7,6},{8,9},{9,8},{10,11... | collective-permute-start | bytes 3145736 | tf_op jit(solution)/shard_map/ppermute | solution.py:14
  78.8 13.8 %all-to-all-start.2 = ((f32[16,2,4,128]{3,2,1,0:T(4,128)}), f32[16,2,4,128]{3,2,1,0:T(4,128)S(1)}, u32[]{:S(2)}, u32[]{:S(2)}) async-start(f32[16,2,4,128]{3,2,1,0:T(4,128)} %broadcast_in_dim.32), calls=%async_computation.2 | async-start | bytes 131072 | tf_op jit(solution)/shard_map/all_to_all | solution.py:27
  96.2 7.8 %collective-permute-start.15 = (bf16[4,288,128]{2,1,0:T(8,128)(2,1)S(1)}, bf16[4,288,128]{2,1,0:T(8,128)(2,1)S(1)}, u32[]{:S(2)}, u32[]{:S(2)}) collective-permute-start(bf16[4,288,128]{2,1,0:T(8,128)(2,1)S(1)} %get-tuple-element.92), channel_id=1, source_target_pairs={{0,64},{64,0},{128,192},{192,128},{1,65},{65,1},{129,193},{193,129... | collective-permute-start | bytes 884744 | tf_op jit(solution)/shard_map/ppermute | solution.py:14
  96.8 7.4 %collective-permute-start.16 = (bf16[288,512]{1,0:T(8,128)(2,1)S(1)}, bf16[288,512]{1,0:T(8,128)(2,1)S(1)}, u32[]{:S(2)}, u32[]{:S(2)}) collective-permute-start(bf16[288,512]{1,0:T(8,128)(2,1)S(1)} %get-tuple-element.93), channel_id=1, source_target_pairs={{0,16},{16,0},{32,48},{48,32},{1,17},{17,1},{33,49},{49,33},{2,18}... | collective-permute-start | bytes 884744 | tf_op jit(solution)/shard_map/ppermute | solution.py:14
  104.3 6.8 %collective-permute-start.17 = (bf16[4,288,128]{2,1,0:T(8,128)(2,1)S(1)}, bf16[4,288,128]{2,1,0:T(8,128)(2,1)S(1)}, u32[]{:S(2)}, u32[]{:S(2)}) collective-permute-start(bf16[4,288,128]{2,1,0:T(8,128)(2,1)S(1)} %convert_element_type.73), channel_id=1, source_target_pairs={{0,64},{64,0},{128,192},{192,128},{1,65},{65,1},{129,193},{193,129... | collective-permute-start | bytes 884744 | tf_op jit(solution)/shard_map/ppermute | solution.py:14
  106.0 6.7 %collective-permute-start.18 = (bf16[288,512]{1,0:T(8,128)(2,1)S(1)}, bf16[288,512]{1,0:T(8,128)(2,1)S(1)}, u32[]{:S(2)}, u32[]{:S(2)}) collective-permute-start(bf16[288,512]{1,0:T(8,128)(2,1)S(1)} %convert_element_type.74), channel_id=1, source_target_pairs={{0,16},{16,0},{32,48},{48,32},{1,17},{17,1},{33,49},{49,33},{2,18}... | collective-permute-start | bytes 884744 | tf_op jit(solution)/shard_map/ppermute | solution.py:14
  107.4 7.9 %collective-permute-start.19 = (bf16[4,288,128]{2,1,0:T(8,128)(2,1)S(1)}, bf16[4,288,128]{2,1,0:T(8,128)(2,1)S(1)}, u32[]{:S(2)}, u32[]{:S(2)}) collective-permute-start(bf16[4,288,128]{2,1,0:T(8,128)(2,1)S(1)} %add_convert_fusion.1), channel_id=1, source_target_pairs={{0,192},{64,128},{128,64},{192,0},{1,193},{65,129},{129,65},{193,1... | collective-permute-start | bytes 884744 | tf_op jit(solution)/shard_map/ppermute | solution.py:14
  108.5 6.8 %collective-permute-start.20 = (bf16[288,512]{1,0:T(8,128)(2,1)S(1)}, bf16[288,512]{1,0:T(8,128)(2,1)S(1)}, u32[]{:S(2)}, u32[]{:S(2)}) collective-permute-start(bf16[288,512]{1,0:T(8,128)(2,1)S(1)} %add_convert_fusion), channel_id=1, source_target_pairs={{0,48},{16,32},{32,16},{48,0},{1,49},{17,33},{33,17},{49,1},{2,50}... | collective-permute-start | bytes 884744 | tf_op jit(solution)/shard_map/ppermute | solution.py:14
  115.6 5.2 %collective-permute-start.21 = (bf16[2,288,128]{2,1,0:T(8,128)(2,1)S(1)}, bf16[2,288,128]{2,1,0:T(8,128)(2,1)S(1)}, u32[]{:S(2)}, u32[]{:S(2)}) collective-permute-start(bf16[2,288,128]{2,1,0:T(8,128)(2,1)S(1)} %slice.158), channel_id=1, source_target_pairs={{0,16},{16,0},{32,48},{48,32},{1,17},{17,1},{33,49},{49,33},{2,18}... | collective-permute-start | bytes 442376 | tf_op jit(solution)/shard_map/ppermute | solution.py:14
  117.3 5.1 %collective-permute-start.22 = (bf16[288,256]{1,0:T(8,128)(2,1)S(1)}, bf16[288,256]{1,0:T(8,128)(2,1)S(1)}, u32[]{:S(2)}, u32[]{:S(2)}) collective-permute-start(bf16[288,256]{1,0:T(8,128)(2,1)S(1)} %slice.157), channel_id=1, source_target_pairs={{0,64},{64,0},{128,192},{192,128},{1,65},{65,1},{129,193},{193,129... | collective-permute-start | bytes 442376 | tf_op jit(solution)/shard_map/ppermute | solution.py:14
  122.5 4.4 %collective-permute-start.23 = (bf16[288,128]{1,0:T(8,128)(2,1)S(1)}, bf16[288,128]{1,0:T(8,128)(2,1)S(1)}, u32[]{:S(2)}, u32[]{:S(2)}) collective-permute-start(bf16[288,128]{1,0:T(8,128)(2,1)S(1)} %fusion.6), channel_id=1, source_target_pairs={{0,48},{16,32},{32,16},{48,0},{1,49},{17,33},{33,17},{49,1},{2,50}... | collective-permute-start | bytes 221192 | tf_op jit(solution)/shard_map/ppermute | solution.py:14
  123.7 5.6 %collective-permute-start.24 = (bf16[288,128]{1,0:T(8,128)(2,1)S(1)}, bf16[288,128]{1,0:T(8,128)(2,1)S(1)}, u32[]{:S(2)}, u32[]{:S(2)}) collective-permute-start(bf16[288,128]{1,0:T(8,128)(2,1)S(1)} %fusion.1), channel_id=1, source_target_pairs={{0,192},{64,128},{128,64},{192,0},{1,193},{65,129},{129,65},{193,1... | collective-permute-start | bytes 221192 | tf_op jit(solution)/shard_map/ppermute | solution.py:14
  129.4 1.5 collective-permute-start.25
  131.6 16.5 %all-to-all-start.3 = ((f32[8,72,128]{2,1,0:T(8,128)}), f32[8,72,128]{2,1,0:T(8,128)S(1)}, u32[]{:S(2)}, u32[]{:S(2)}) async-start(f32[8,72,128]{2,1,0:T(8,128)} %pad_maximum_fusion.3), calls=%async_computation.3 | async-start | bytes 589824 | tf_op jit(solution)/shard_map/all_to_all | solution.py:388

commit v5 on v4

--- a/solution.py
+++ b/solution.py
@@ -267,7 +267,8 @@
     )(*in_hbm([wt]), dls)
 
 
-def weight_kernel(places_ref, dl_ref, here_ref, there_ref, out_ref, both):
+def weight_kernel(places_ref, dl_ref, here_ref, there_ref, *refs):
+    out_ref, both = refs[-2:]
     half = here_ref.shape[1]
     core = places_ref[Y]
     both[pl.ds(pl.multiple_of(core * half, 64), half)] = here_ref[0]
@@ -276,25 +277,26 @@
     out_ref[...] = lax.dot_general(dl_ref[...], both[...], over_last, preferred_element_type=F32).astype(BF16)
 
 
-def weight_of(places, dls, here, there):
+def weight_of(places, dls, here, there, first, count, into=()):
     voc, all_rows = dls.shape[0] // 2, dls.shape[1]
     half = here.shape[1]
-    one = pl.BlockSpec((1, half, all_rows), lambda i, places: (i, 0, 0))
+    one = pl.BlockSpec((1, half, all_rows), lambda i, places: (i + first, 0, 0))
     return pl.pallas_call(
         weight_kernel,
         out_shape=jax.ShapeDtypeStruct((voc, Y * 2 * half), BF16),
         grid_spec=pltpu.PrefetchScalarGridSpec(
             num_scalar_prefetch=1,
-            grid=(Y,),
-            in_specs=[pl.BlockSpec((voc, all_rows), lambda i, places: (0, 0)), one, one],
-            out_specs=pl.BlockSpec((voc, 2 * half), lambda i, places: (0, places[i])),
+            grid=(count,),
+            in_specs=[pl.BlockSpec((voc, all_rows), lambda i, places: (0, 0)), one, one] + [pl.BlockSpec(memory_space=pl.ANY)] * len(into),
+            out_specs=pl.BlockSpec((voc, 2 * half), lambda i, places: (0, places[i + first])),
             scratch_shapes=[pltpu.VMEM((2 * half, all_rows), BF16)],
         ),
+        input_output_aliases={4: 0} if into else {},
         compiler_params=pltpu.CompilerParams(vmem_limit_bytes=VMEM_LIMIT),
         cost_estimate=pl.CostEstimate(
-            flops=4 * Y * voc * half * all_rows, bytes_accessed=8 * Y * half * all_rows, transcendentals=0
-        ),
-    )(places, dls, *in_hbm([here, there]))
+            flops=4 * count * voc * half * all_rows, bytes_accessed=8 * count * half * all_rows, transcendentals=0
+        ),
+    )(places, dls, *in_hbm([here, there]), *into)
 
 
 def per_device(hidden, weight, targets):
@@ -367,7 +369,8 @@
     a0, a1, a3, b0, b1, b3 = rest_call([a_kind] * 3 + [b_kind] * 3, wt, dls)
     a1, a3 = a1.astype(BF16), (a3 + a_far.astype(F32)).astype(BF16)
     b1, b3 = b1.astype(BF16), (b3 + b_far.astype(F32)).astype(BF16)
-    a1, b1, a3, b3 = at_once(a1, b1, a3, b3)
+    begun = weight_of(jnp.append(places, c), dls, ht, other, 0, 1)
+    a1, b1, a3, b3, begun = at_once(a1, b1, a3, b3, begun)
     a1, b1, a3, b3 = at_once(flip(a1, "x", X, 1), flip(b1, "y", Y, 1), flip(a3, "x", X, 3), flip(b3, "y", Y, 3))
     a_own = a0 + a1.astype(F32) + a3.astype(F32)
     b_own = b0 + b1.astype(F32) + b3.astype(F32)
@@ -383,8 +386,8 @@
     mine = lax.dynamic_index_in_dim(total, c, 1, keepdims=False)
     theirs = flip(lax.dynamic_index_in_dim(total, 1 - c, 1, keepdims=False), "c", C, 1)
     by_z = jnp.concatenate([jnp.where(c == 0, mine, theirs), jnp.where(c == 0, theirs, mine)])
-    by_z, dls = at_once(by_z, dls)
-    grad_weight = weight_of(jnp.append(places, c), dls, ht, other)
+    by_z, dls, begun = at_once(by_z, dls, begun)
+    grad_weight = weight_of(jnp.append(places, c), dls, ht, other, 1, Y - 1, (begun,))
     grad_hidden = lax.all_to_all(by_z, "z", 0, 0, tiled=True).sum(0).astype(BF16).T
     return loss, grad_hidden, grad_weight
 

time: 151 us -> 154 us (1.020)
  Pallas kernels: 28.5 us -> 31.9 us
  starting transfers between devices: 51.6 us -> 49.2 us
  other arithmetic: 4.67 us -> 6.63 us
    pallas_call x1 -> x2, Pallas kernels: 7.52 us -> 10.2 us  [weight_of(): pl.pallas_call(weight_kernel, out_shape=jax.ShapeDtypeStruct((voc, Y * 2...]
  transfers between devices with their start and end apart: 30 -> 30, of which waited for: 21 -> 20; matrix products, arithmetic and copies ran while one was open for 3% -> 3% of each run, Pallas kernels for 12% -> 13%
where the time goes in v5:
time: 154 us; the launch traced here: 152 us
  waiting for transfers between devices  60.3 us (39%)
  starting transfers between devices  49.2 us (32%)
  Pallas kernels  31.9 us (21%)
  other arithmetic  6.63 us (4%)
  local copies, waits for them, and re-layouts  2.99 us (2%)
    ppermute x26, waiting for transfers between devices, flip(): return lax.ppermute(array, axis, [(i, i ^ change) for i in range(size)])  36.1 us
    ppermute x26, starting transfers between devices, flip(): return lax.ppermute(array, axis, [(i, i ^ change) for i in range(size)])  27.5 us
    all_to_all x3, starting transfers between devices, spread(): return lax.all_to_all(copies, axes, 0, 0, tiled=True)  18.3 us
    all_to_all x3, waiting for transfers between devices, spread(): return lax.all_to_all(copies, axes, 0, 0, tiled=True)  18.1 us
    pallas_call x2, Pallas kernels, weight_of(): pl.pallas_call(weight_kernel, out_shape=jax.ShapeDtypeStruct((voc, Y * 2...  10.2 us
    pallas_call x1, Pallas kernels, logits_of(): pl.pallas_call(logits_kernel, out_shape=(square, square, pltpu.HBM((Y, 2...  7.94 us
    all_to_all x1, waiting for transfers between devices, per_device(): lax.all_to_all(by_z, 'z', 0, 0, tiled=True).sum(0).astype(BF16)  6.14 us
    pallas_call x1, Pallas kernels, turned_weights(): pl.pallas_call(turn_kernel, out_shape=pltpu.HBM((Y, 2, part, 2 * voc), BF...  5.44 us
  transfers between devices with their start and end apart: 30, of which 20 were waited for; matrix products, arithmetic and copies ran while one was open for 3% of the time, Pallas kernels for 13%

profile of v5, /device:TPU:8, one launch (start us, length us, event | category | flops | bytes accessed | tf_op | source)
XLA Modules:
  0.0 152.0 jit_solution(3440560604356165019)
XLA Ops:
  0.7 1.4 broadcast_in_dim.14
  2.1 8.5 %all-to-all-start = ((bf16[8,72,128]{2,1,0:T(8,128)(2,1)}), bf16[8,72,128]{2,1,0:T(8,128)(2,1)S(1)}, u32[]{:S(2)}, u32[]{:S(2)}) async-start(bf16[8,72,128]{2,1,0:T(8,128)(2,1)} %broadcast_in_dim.14), calls=%async_computation | async-start | bytes 294912 | tf_op jit(solution)/shard_map/all_to_all | solution.py:27
  10.8 5.4 %shard_map.58.wt_ref = bf16[4,2,288,1024]{3,2,1,0:T(8,128)(2,1)} custom-call(s32[10]{0:T(128)S(1)} %pad_add_fusion.1.meta_ref, bf16[512,4608]{1,0:T(8,128)(2,1)} %own_ref.3, bf16[512,4608]{1,0:T(8,128)(2,1)} %collective-permute-done.other_ref), custom_call_target="tpu_custom_call" | custom-call | bytes 9437184 | tf_op jit(solution)/shard_map/pallas_call | solution.py:158
  16.2 4.5 %all-to-all-done = bf16[8,72,128]{2,1,0:T(8,128)(2,1)S(1)} async-done(((bf16[8,72,128]{2,1,0:T(8,128)(2,1)}), bf16[8,72,128]{2,1,0:T(8,128)(2,1)S(1)}, u32[]{:S(2)}, u32[]{:S(2)}) %all-to-all-start) | async-done | bytes 147488 | tf_op jit(solution)/shard_map/all_to_all | solution.py:27
  20.7 1.2 collective-permute-done.1
  22.1 1.6 %collective-permute-start.3 = (bf16[296,128]{1,0:T(8,128)(2,1)S(1)}, bf16[296,128]{1,0:T(8,128)(2,1)S(1)}, u32[]{:S(2)}, u32[]{:S(2)}) collective-permute-start(bf16[296,128]{1,0:T(8,128)(2,1)S(1)} %concatenate.33), channel_id=1, source_target_pairs={{0,64},{64,0},{128,192},{192,128},{1,65},{65,1},{129,193},{193,129... | collective-permute-start | bytes 227336 | tf_op jit(solution)/shard_map/ppermute | solution.py:14
  24.1 3.9 %collective-permute-done.2 = bf16[288,128]{1,0:T(8,128)(2,1)S(1)} collective-permute-done((bf16[288,128]{1,0:T(8,128)(2,1)S(1)}, bf16[288,128]{1,0:T(8,128)(2,1)S(1)}, u32[]{:S(2)}, u32[]{:S(2)}) %collective-permute-start.2) | collective-permute-done | bytes 73760 | tf_op jit(solution)/shard_map/ppermute | solution.py:14
  28.0 2.2 %collective-permute-start.5 = (bf16[2,296,128]{2,1,0:T(8,128)(2,1)S(1)}, bf16[2,296,128]{2,1,0:T(8,128)(2,1)S(1)}, u32[]{:S(2)}, u32[]{:S(2)}) collective-permute-start(bf16[2,296,128]{2,1,0:T(8,128)(2,1)S(1)} %pad_maximum_fusion.4), channel_id=1, source_target_pairs={{0,192},{64,128},{128,64},{192,0},{1,193},{65,129},{129,65},{193,1... | collective-permute-start | bytes 454664 | tf_op jit(solution)/shard_map/ppermute | solution.py:14
  30.2 1.7 %collective-permute-start.4 = (bf16[2,288,128]{2,1,0:T(8,128)(2,1)S(1)}, bf16[2,288,128]{2,1,0:T(8,128)(2,1)S(1)}, u32[]{:S(2)}, u32[]{:S(2)}) collective-permute-start(bf16[2,288,128]{2,1,0:T(8,128)(2,1)S(1)} %pad_maximum_fusion.5), channel_id=1, source_target_pairs={{0,48},{16,32},{32,16},{48,0},{1,49},{17,33},{33,17},{49,1},{2,50}... | collective-permute-start | bytes 442376 | tf_op jit(solution)/shard_map/ppermute | solution.py:14
  31.9 3.6 %collective-permute-done.4 = bf16[2,288,128]{2,1,0:T(8,128)(2,1)S(1)} collective-permute-done((bf16[2,288,128]{2,1,0:T(8,128)(2,1)S(1)}, bf16[2,288,128]{2,1,0:T(8,128)(2,1)S(1)}, u32[]{:S(2)}, u32[]{:S(2)}) %collective-permute-start.4) | collective-permute-done | bytes 147488 | tf_op jit(solution)/shard_map/ppermute | solution.py:14
  35.6 0.7 collective-permute-start.10
  36.4 2.6 %collective-permute-start.8 = (bf16[4,288,128]{2,1,0:T(8,128)(2,1)S(1)}, bf16[4,288,128]{2,1,0:T(8,128)(2,1)S(1)}, u32[]{:S(2)}, u32[]{:S(2)}) collective-permute-start(bf16[4,288,128]{2,1,0:T(8,128)(2,1)S(1)} %pad_maximum_fusion.1.refs_0_), channel_id=1, source_target_pairs={{0,192},{64,128},{128,64},{192,0},{1,193},{65,129},{129,65},{193,1... | collective-permute-start | bytes 884744 | tf_op jit(solution)/shard_map/ppermute | solution.py:14
  39.2 3.5 %collective-permute-start.11 = (bf16[4,288,128]{2,1,0:T(8,128)(2,1)S(1)}, bf16[4,288,128]{2,1,0:T(8,128)(2,1)S(1)}, u32[]{:S(2)}, u32[]{:S(2)}) collective-permute-start(bf16[4,288,128]{2,1,0:T(8,128)(2,1)S(1)} %slice.115.refs_4_), channel_id=1, source_target_pairs={{0,32},{16,48},{32,0},{48,16},{1,33},{17,49},{33,1},{49,17},{2,34}... | collective-permute-start | bytes 884744 | tf_op jit(solution)/shard_map/ppermute | solution.py:14
  42.7 4.5 %collective-permute-done.10.refs_2_ = bf16[4,288,128]{2,1,0:T(8,128)(2,1)S(1)} collective-permute-done((bf16[4,288,128]{2,1,0:T(8,128)(2,1)S(1)}, bf16[4,288,128]{2,1,0:T(8,128)(2,1)S(1)}, u32[]{:S(2)}, u32[]{:S(2)}) %collective-permute-start.10) | collective-permute-done | bytes 294944 | tf_op jit(solution)/shard_map/ppermute | solution.py:14
  47.2 1.7 %collective-permute-start.7 = (bf16[4,288,128]{2,1,0:T(8,128)(2,1)S(1)}, bf16[4,288,128]{2,1,0:T(8,128)(2,1)S(1)}, u32[]{:S(2)}, u32[]{:S(2)}) collective-permute-start(bf16[4,288,128]{2,1,0:T(8,128)(2,1)S(1)} %slice.115.refs_4_), channel_id=1, source_target_pairs={{0,16},{16,0},{32,48},{48,32},{1,17},{17,1},{33,49},{49,33},{2,18}... | collective-permute-start | bytes 884744 | tf_op jit(solution)/shard_map/ppermute | solution.py:14
  49.0 1.3 collective-permute-done.8.refs_3_
  50.3 2.9 %collective-permute-done.9.refs_7_ = bf16[4,288,128]{2,1,0:T(8,128)(2,1)S(1)} collective-permute-done((bf16[4,288,128]{2,1,0:T(8,128)(2,1)S(1)}, bf16[4,288,128]{2,1,0:T(8,128)(2,1)S(1)}, u32[]{:S(2)}, u32[]{:S(2)}) %collective-permute-start.9) | collective-permute-done | bytes 294944 | tf_op jit(solution)/shard_map/ppermute | solution.py:14
  53.3 0.7 collective-permute-done.7.refs_5_
  54.0 7.9 %shard_map.59 = (f32[512,512]{1,0:T(8,128)S(1)}, f32[512,512]{1,0:T(8,128)}, bf16[4,576,512]{2,1,0:T(8,128)(2,1)}) custom-call(s32[5]{0:T(128)S(1)} %pad_add_fusion.meta_ref, bf16[512,4608]{1,0:T(8,128)(2,1)} %own_ref.3, bf16[512,4608]{1,0:T(8,128)(2,1)} %collective-permute-done.other_ref, bf16[4,288,128]{2,1,0:T(8,128)(2,1)S(1)} %pad_maximum_fusion.1.refs_0_, ...), custom_call_target="tpu_custom_call" | custom-call | flops 2684354560 | bytes 5242880 | tf_op jit(solution)/shard_map/pallas_call | solution.py:109
  62.3 0.8 fusion.10
  63.1 2.0 %collective-permute-done.12 = f32[512,512]{1,0:T(8,128)S(1)} collective-permute-done((f32[512,512]{1,0:T(8,128)}, f32[512,512]{1,0:T(8,128)S(1)}, u32[]{:S(2)}, u32[]{:S(2)}) %collective-permute-start.12) | collective-permute-done | bytes 1048608 | tf_op jit(solution)/shard_map/ppermute | solution.py:14
  66.4 3.5 %all-to-all-start.1 = ((f32[16,2,4,128]{3,2,1,0:T(4,128)}), f32[16,2,4,128]{3,2,1,0:T(4,128)S(1)}, u32[]{:S(2)}, u32[]{:S(2)}) async-start(f32[16,2,4,128]{3,2,1,0:T(4,128)} %broadcast_in_dim.31), calls=%async_computation.1 | async-start | bytes 131072 | tf_op jit(solution)/shard_map/all_to_all | solution.py:27
  70.3 7.4 %all-to-all-done.1 = f32[16,2,4,128]{3,2,1,0:T(4,128)S(1)} async-done(((f32[16,2,4,128]{3,2,1,0:T(4,128)}), f32[16,2,4,128]{3,2,1,0:T(4,128)S(1)}, u32[]{:S(2)}, u32[]{:S(2)}) %all-to-all-start.1) | async-done | bytes 65568 | tf_op jit(solution)/shard_map/all_to_all | solution.py:27
  78.8 6.3 %all-to-all-start.2 = ((f32[16,2,4,128]{3,2,1,0:T(4,128)}), f32[16,2,4,128]{3,2,1,0:T(4,128)S(1)}, u32[]{:S(2)}, u32[]{:S(2)}) async-start(f32[16,2,4,128]{3,2,1,0:T(4,128)} %broadcast_in_dim.32), calls=%async_computation.2 | async-start | bytes 131072 | tf_op jit(solution)/shard_map/all_to_all | solution.py:27
  85.2 6.2 %all-to-all-done.2 = f32[16,2,4,128]{3,2,1,0:T(4,128)S(1)} async-done(((f32[16,2,4,128]{3,2,1,0:T(4,128)}), f32[16,2,4,128]{3,2,1,0:T(4,128)S(1)}, u32[]{:S(2)}, u32[]{:S(2)}) %all-to-all-start.2) | async-done | bytes 65568 | tf_op jit(solution)/shard_map/all_to_all | solution.py:27
  91.5 4.2 %shard_map.60 = (bf16[1024,512]{1,0:T(8,128)(2,1)S(1)}, bf16[4,288,128]{2,1,0:T(8,128)(2,1)}, bf16[288,512]{1,0:T(8,128)(2,1)S(1)}) custom-call(s32[2]{0:T(128)S(1)} %pad_add_fusion.2.base_ref, bf16[4,2,288,1024]{3,2,1,0:T(8,128)(2,1)} %shard_map.58.wt_ref, f32[512,512]{1,0:T(8,128)S(1)} %subtract_multiply_fusion.grown_ref, ...), custom_call_target="tpu_custom_call" | custom-call | flops 603979776 | bytes 4456448 | tf_op jit(solution)/shard_map/pallas_call | solution.py:219
  96.3 1.5 collective-permute-start.16
  97.9 4.2 %shard_map.61 = (f32[4,288,128]{2,1,0:T(8,128)S(1)}, f32[4,288,128]{2,1,0:T(8,128)S(1)}, f32[4,288,128]{2,1,0:T(8,128)S(1)}, f32[288,512]{1,0:T(8,128)S(1)}, f32...) custom-call(bf16[4,2,288,1024]{3,2,1,0:T(8,128)(2,1)} %shard_map.58.wt_ref, ...), custom_call_target="tpu_custom_call" | custom-call | flops 2113929216 | bytes 4128768 | tf_op jit(solution)/shard_map/pallas_call | solution.py:257
  102.1 3.8 %shard_map.62.refs_0_ = bf16[512,4608]{1,0:T(8,128)(2,1)} custom-call(s32[5]{0:T(128)S(1)} %concatenate.36.places_ref, bf16[1024,512]{1,0:T(8,128)(2,1)S(1)} %get-tuple-element.119.dls_ref.dl_ref, bf16[4,576,512]{2,1,0:T(8,128)(2,1)} %get-tuple-element.83.here_ref, bf16[4,576,512]{2,1,0:T(8,128)(2,1)} %collective-permute-done.13.there_ref), custom_call_target="tpu_custom_call" | custom-call | flops 603979776 | bytes 2359296 | tf_op jit(solution)/shard_map/pallas_call | solution.py:284
  105.9 1.1 add_convert_fusion
  107.0 1.0 add_convert_fusion.1
  108.0 1.6 %collective-permute-start.17 = (bf16[4,288,128]{2,1,0:T(8,128)(2,1)S(1)}, bf16[4,288,128]{2,1,0:T(8,128)(2,1)S(1)}, u32[]{:S(2)}, u32[]{:S(2)}) collective-permute-start(bf16[4,288,128]{2,1,0:T(8,128)(2,1)S(1)} %convert_element_type.73), channel_id=1, source_target_pairs={{0,64},{64,0},{128,192},{192,128},{1,65},{65,1},{129,193},{193,129... | collective-permute-start | bytes 884744 | tf_op jit(solution)/shard_map/ppermute | solution.py:14
  110.2 1.1 collective-permute-start.19
  111.3 0.8 collective-permute-start.20
  112.1 3.3 %collective-permute-done.17 = bf16[4,288,128]{2,1,0:T(8,128)(2,1)S(1)} collective-permute-done((bf16[4,288,128]{2,1,0:T(8,128)(2,1)S(1)}, bf16[4,288,128]{2,1,0:T(8,128)(2,1)S(1)}, u32[]{:S(2)}, u32[]{:S(2)}) %collective-permute-start.17) | collective-permute-done | bytes 294944 | tf_op jit(solution)/shard_map/ppermute | solution.py:14
  115.3 1.0 collective-permute-done.18
  116.4 1.7 %collective-permute-done.19 = bf16[4,288,128]{2,1,0:T(8,128)(2,1)S(1)} collective-permute-done((bf16[4,288,128]{2,1,0:T(8,128)(2,1)S(1)}, bf16[4,288,128]{2,1,0:T(8,128)(2,1)S(1)}, u32[]{:S(2)}, u32[]{:S(2)}) %collective-permute-start.19) | collective-permute-done | bytes 294944 | tf_op jit(solution)/shard_map/ppermute | solution.py:14
  118.4 2.7 %collective-permute-start.21 = (bf16[2,288,128]{2,1,0:T(8,128)(2,1)S(1)}, bf16[2,288,128]{2,1,0:T(8,128)(2,1)S(1)}, u32[]{:S(2)}, u32[]{:S(2)}) collective-permute-start(bf16[2,288,128]{2,1,0:T(8,128)(2,1)S(1)} %slice.158), channel_id=1, source_target_pairs={{0,16},{16,0},{32,48},{48,32},{1,17},{17,1},{33,49},{49,33},{2,18}... | collective-permute-start | bytes 442376 | tf_op jit(solution)/shard_map/ppermute | solution.py:14
  121.1 3.1 %collective-permute-done.21 = bf16[2,288,128]{2,1,0:T(8,128)(2,1)S(1)} collective-permute-done((bf16[2,288,128]{2,1,0:T(8,128)(2,1)S(1)}, bf16[2,288,128]{2,1,0:T(8,128)(2,1)S(1)}, u32[]{:S(2)}, u32[]{:S(2)}) %collective-permute-start.21) | collective-permute-done | bytes 147488 | tf_op jit(solution)/shard_map/ppermute | solution.py:14
  124.2 2.0 %collective-permute-done.22 = bf16[288,256]{1,0:T(8,128)(2,1)S(1)} collective-permute-done((bf16[288,256]{1,0:T(8,128)(2,1)S(1)}, bf16[288,256]{1,0:T(8,128)(2,1)S(1)}, u32[]{:S(2)}, u32[]{:S(2)}) %collective-permute-start.22) | collective-permute-done | bytes 147488 | tf_op jit(solution)/shard_map/ppermute | solution.py:14
  127.0 2.2 %collective-permute-start.24 = (bf16[288,128]{1,0:T(8,128)(2,1)S(1)}, bf16[288,128]{1,0:T(8,128)(2,1)S(1)}, u32[]{:S(2)}, u32[]{:S(2)}) collective-permute-start(bf16[288,128]{1,0:T(8,128)(2,1)S(1)} %fusion.1), channel_id=1, source_target_pairs={{0,192},{64,128},{128,64},{192,0},{1,193},{65,129},{129,65},{193,1... | collective-permute-start | bytes 221192 | tf_op jit(solution)/shard_map/ppermute | solution.py:14
  129.1 1.6 %collective-permute-done.23 = bf16[288,128]{1,0:T(8,128)(2,1)S(1)} collective-permute-done((bf16[288,128]{1,0:T(8,128)(2,1)S(1)}, bf16[288,128]{1,0:T(8,128)(2,1)S(1)}, u32[]{:S(2)}, u32[]{:S(2)}) %collective-permute-start.23) | collective-permute-done | bytes 73760 | tf_op jit(solution)/shard_map/ppermute | solution.py:14
  130.7 1.8 %collective-permute-done.24 = bf16[288,128]{1,0:T(8,128)(2,1)S(1)} collective-permute-done((bf16[288,128]{1,0:T(8,128)(2,1)S(1)}, bf16[288,128]{1,0:T(8,128)(2,1)S(1)}, u32[]{:S(2)}, u32[]{:S(2)}) %collective-permute-start.24) | collective-permute-done | bytes 73760 | tf_op jit(solution)/shard_map/ppermute | solution.py:14
  132.7 1.4 collective-permute-done.25
  134.1 0.8 pad_maximum_fusion.3
  134.9 3.4 %all-to-all-start.3 = ((f32[8,72,128]{2,1,0:T(8,128)}), f32[8,72,128]{2,1,0:T(8,128)S(1)}, u32[]{:S(2)}, u32[]{:S(2)}) async-start(f32[8,72,128]{2,1,0:T(8,128)} %pad_maximum_fusion.3), calls=%async_computation.3 | async-start | bytes 589824 | tf_op jit(solution)/shard_map/all_to_all | solution.py:391
  138.8 6.4 %shard_map.63 = bf16[512,4608]{1,0:T(8,128)(2,1)} custom-call(s32[5]{0:T(128)S(1)} %concatenate.36.places_ref, bf16[1024,512]{1,0:T(8,128)(2,1)S(1)} %get-tuple-element.119.dls_ref.dl_ref, bf16[4,576,512]{2,1,0:T(8,128)(2,1)} %get-tuple-element.83.here_ref, bf16[4,576,512]{2,1,0:T(8,128)(2,1)} %collective-permute-done.13.there_ref, ...), custom_call_target="tpu_custom_call", output_to_operand_aliasing={{}: (4, {})} | custom-call | flops 1811939328 | bytes 7077888 | tf_op jit(solution)/shard_map/pallas_call | solution.py:284
  145.2 6.1 %all-to-all-done.3 = f32[8,72,128]{2,1,0:T(8,128)S(1)} async-done(((f32[8,72,128]{2,1,0:T(8,128)}), f32[8,72,128]{2,1,0:T(8,128)S(1)}, u32[]{:S(2)}, u32[]{:S(2)}) %all-to-all-start.3) | async-done | bytes 294944 | tf_op jit(solution)/shard_map/all_to_all | solution.py:391
  (79 shorter events, 8.3 us)
Async XLA Ops:
  0.6 10.2 %collective-permute-start = (bf16[512,4608]{1,0:T(8,128)(2,1)}, bf16[512,4608]{1,0:T(8,128)(2,1)}, u32[]{:S(2)}, u32[]{:S(2)}) collective-permute-start(bf16[512,4608]{1,0:T(8,128)(2,1)} %own_ref.3), channel_id=1, source_target_pairs={{0,1},{1,0},{2,3},{3,2},{4,5},{5,4},{6,7},{7,6},{8,9},{9,8},{10,11... | collective-permute-start | bytes 14155784 | tf_op jit(solution)/shard_map/ppermute | solution.py:14
  2.1 18.5 %all-to-all-start = ((bf16[8,72,128]{2,1,0:T(8,128)(2,1)}), bf16[8,72,128]{2,1,0:T(8,128)(2,1)S(1)}, u32[]{:S(2)}, u32[]{:S(2)}) async-start(bf16[8,72,128]{2,1,0:T(8,128)(2,1)} %broadcast_in_dim.14), calls=%async_computation | async-start | bytes 294912 | tf_op jit(solution)/shard_map/all_to_all | solution.py:27
  10.8 9.9 %copy-start.3 = (s32[128]{0:T(128)S(1)}, s32[128]{0:T(128)}, u32[]{:S(2)}) copy-start(s32[128]{0:T(128)} %param.5) | copy-start | bytes 1540
  20.7 1.3 collective-permute-start.1
  22.1 5.9 %collective-permute-start.3 = (bf16[296,128]{1,0:T(8,128)(2,1)S(1)}, bf16[296,128]{1,0:T(8,128)(2,1)S(1)}, u32[]{:S(2)}, u32[]{:S(2)}) collective-permute-start(bf16[296,128]{1,0:T(8,128)(2,1)S(1)} %concatenate.33), channel_id=1, source_target_pairs={{0,64},{64,0},{128,192},{192,128},{1,65},{65,1},{129,193},{193,129... | collective-permute-start | bytes 227336 | tf_op jit(solution)/shard_map/ppermute | solution.py:14
  23.6 4.4 %collective-permute-start.2 = (bf16[288,128]{1,0:T(8,128)(2,1)S(1)}, bf16[288,128]{1,0:T(8,128)(2,1)S(1)}, u32[]{:S(2)}, u32[]{:S(2)}) collective-permute-start(bf16[288,128]{1,0:T(8,128)(2,1)S(1)} %bitcast.72), channel_id=1, source_target_pairs={{0,16},{16,0},{32,48},{48,32},{1,17},{17,1},{33,49},{49,33},{2,18}... | collective-permute-start | bytes 221192 | tf_op jit(solution)/shard_map/ppermute | solution.py:14
  28.0 19.2 %copy-start = (bf16[296,128]{1,0:T(8,128)(2,1)}, bf16[296,128]{1,0:T(8,128)(2,1)S(1)}, u32[]{:S(2)}) copy-start(bf16[296,128]{1,0:T(8,128)(2,1)S(1)} %collective-permute-done.3) | copy-start | bytes 227332
  28.0 7.4 %collective-permute-start.5 = (bf16[2,296,128]{2,1,0:T(8,128)(2,1)S(1)}, bf16[2,296,128]{2,1,0:T(8,128)(2,1)S(1)}, u32[]{:S(2)}, u32[]{:S(2)}) collective-permute-start(bf16[2,296,128]{2,1,0:T(8,128)(2,1)S(1)} %pad_maximum_fusion.4), channel_id=1, source_target_pairs={{0,192},{64,128},{128,64},{192,0},{1,193},{65,129},{129,65},{193,1... | collective-permute-start | bytes 454664 | tf_op jit(solution)/shard_map/ppermute | solution.py:14
  30.2 5.2 %collective-permute-start.4 = (bf16[2,288,128]{2,1,0:T(8,128)(2,1)S(1)}, bf16[2,288,128]{2,1,0:T(8,128)(2,1)S(1)}, u32[]{:S(2)}, u32[]{:S(2)}) collective-permute-start(bf16[2,288,128]{2,1,0:T(8,128)(2,1)S(1)} %pad_maximum_fusion.5), channel_id=1, source_target_pairs={{0,48},{16,32},{32,16},{48,0},{1,49},{17,33},{33,17},{49,1},{2,50}... | collective-permute-start | bytes 442376 | tf_op jit(solution)/shard_map/ppermute | solution.py:14
  35.5 11.7 %copy-start.1 = (bf16[1,296,128]{2,1,0:T(8,128)(2,1)}, bf16[1,296,128]{2,1,0:T(8,128)(2,1)S(1)}, u32[]{:S(2)}) copy-start(bf16[1,296,128]{2,1,0:T(8,128)(2,1)S(1)} %get-tuple-element.129) | copy-start | bytes 227332
  35.5 11.7 %copy-start.2 = (bf16[1,296,128]{2,1,0:T(8,128)(2,1)}, bf16[1,296,128]{2,1,0:T(8,128)(2,1)S(1)}, u32[]{:S(2)}) copy-start(bf16[1,296,128]{2,1,0:T(8,128)(2,1)S(1)} %get-tuple-element.130) | copy-start | bytes 227332
  35.6 11.5 %collective-permute-start.10 = (bf16[4,288,128]{2,1,0:T(8,128)(2,1)S(1)}, bf16[4,288,128]{2,1,0:T(8,128)(2,1)S(1)}, u32[]{:S(2)}, u32[]{:S(2)}) collective-permute-start(bf16[4,288,128]{2,1,0:T(8,128)(2,1)S(1)} %pad_maximum_fusion.1.refs_0_), channel_id=1, source_target_pairs={{0,128},{64,192},{128,0},{192,64},{1,129},{65,193},{129,1},{193,65... | collective-permute-start | bytes 884744 | tf_op jit(solution)/shard_map/ppermute | solution.py:14
  36.4 14.0 %collective-permute-start.8 = (bf16[4,288,128]{2,1,0:T(8,128)(2,1)S(1)}, bf16[4,288,128]{2,1,0:T(8,128)(2,1)S(1)}, u32[]{:S(2)}, u32[]{:S(2)}) collective-permute-start(bf16[4,288,128]{2,1,0:T(8,128)(2,1)S(1)} %pad_maximum_fusion.1.refs_0_), channel_id=1, source_target_pairs={{0,192},{64,128},{128,64},{192,0},{1,193},{65,129},{129,65},{193,1... | collective-permute-start | bytes 884744 | tf_op jit(solution)/shard_map/ppermute | solution.py:14
  39.0 11.3 %collective-permute-start.6 = (bf16[4,288,128]{2,1,0:T(8,128)(2,1)S(1)}, bf16[4,288,128]{2,1,0:T(8,128)(2,1)S(1)}, u32[]{:S(2)}, u32[]{:S(2)}) collective-permute-start(bf16[4,288,128]{2,1,0:T(8,128)(2,1)S(1)} %pad_maximum_fusion.1.refs_0_), channel_id=1, source_target_pairs={{0,64},{64,0},{128,192},{192,128},{1,65},{65,1},{129,193},{193,129... | collective-permute-start | bytes 884744 | tf_op jit(solution)/shard_map/ppermute | solution.py:14
  39.2 11.1 %collective-permute-start.11 = (bf16[4,288,128]{2,1,0:T(8,128)(2,1)S(1)}, bf16[4,288,128]{2,1,0:T(8,128)(2,1)S(1)}, u32[]{:S(2)}, u32[]{:S(2)}) collective-permute-start(bf16[4,288,128]{2,1,0:T(8,128)(2,1)S(1)} %slice.115.refs_4_), channel_id=1, source_target_pairs={{0,32},{16,48},{32,0},{48,16},{1,33},{17,49},{33,1},{49,17},{2,34}... | collective-permute-start | bytes 884744 | tf_op jit(solution)/shard_map/ppermute | solution.py:14
  42.7 10.5 %collective-permute-start.9 = (bf16[4,288,128]{2,1,0:T(8,128)(2,1)S(1)}, bf16[4,288,128]{2,1,0:T(8,128)(2,1)S(1)}, u32[]{:S(2)}, u32[]{:S(2)}) collective-permute-start(bf16[4,288,128]{2,1,0:T(8,128)(2,1)S(1)} %slice.115.refs_4_), channel_id=1, source_target_pairs={{0,48},{16,32},{32,16},{48,0},{1,49},{17,33},{33,17},{49,1},{2,50}... | collective-permute-start | bytes 884744 | tf_op jit(solution)/shard_map/ppermute | solution.py:14
  47.2 6.8 %collective-permute-start.7 = (bf16[4,288,128]{2,1,0:T(8,128)(2,1)S(1)}, bf16[4,288,128]{2,1,0:T(8,128)(2,1)S(1)}, u32[]{:S(2)}, u32[]{:S(2)}) collective-permute-start(bf16[4,288,128]{2,1,0:T(8,128)(2,1)S(1)} %slice.115.refs_4_), channel_id=1, source_target_pairs={{0,16},{16,0},{32,48},{48,32},{1,17},{17,1},{33,49},{49,33},{2,18}... | collective-permute-start | bytes 884744 | tf_op jit(solution)/shard_map/ppermute | solution.py:14
  61.9 3.1 %collective-permute-start.12 = (f32[512,512]{1,0:T(8,128)}, f32[512,512]{1,0:T(8,128)S(1)}, u32[]{:S(2)}, u32[]{:S(2)}) collective-permute-start(f32[512,512]{1,0:T(8,128)} %get-tuple-element.78), channel_id=1, source_target_pairs={{0,1},{1,0},{2,3},{3,2},{4,5},{5,4},{6,7},{7,6},{8,9},{9,8},{10,11... | collective-permute-start | bytes 3145736 | tf_op jit(solution)/shard_map/ppermute | solution.py:14
  65.5 12.2 %collective-permute-start.13 = (bf16[4,576,512]{2,1,0:T(8,128)(2,1)}, bf16[4,576,512]{2,1,0:T(8,128)(2,1)}, u32[]{:S(2)}, u32[]{:S(2)}) collective-permute-start(bf16[4,576,512]{2,1,0:T(8,128)(2,1)} %get-tuple-element.83.here_ref), channel_id=1, source_target_pairs={{0,1},{1,0},{2,3},{3,2},{4,5},{5,4},{6,7},{7,6},{8,9},{9,8},{10,11... | collective-permute-start | bytes 7077896 | tf_op jit(solution)/shard_map/ppermute | solution.py:14
  66.4 11.3 %all-to-all-start.1 = ((f32[16,2,4,128]{3,2,1,0:T(4,128)}), f32[16,2,4,128]{3,2,1,0:T(4,128)S(1)}, u32[]{:S(2)}, u32[]{:S(2)}) async-start(f32[16,2,4,128]{3,2,1,0:T(4,128)} %broadcast_in_dim.31), calls=%async_computation.1 | async-start | bytes 131072 | tf_op jit(solution)/shard_map/all_to_all | solution.py:27
  77.7 13.8 %collective-permute-start.14 = (f32[512,512]{1,0:T(8,128)S(1)}, f32[512,512]{1,0:T(8,128)S(1)}, u32[]{:S(2)}, u32[]{:S(2)}) collective-permute-start(f32[512,512]{1,0:T(8,128)S(1)} %subtract_multiply_fusion.grown_ref), channel_id=1, source_target_pairs={{0,1},{1,0},{2,3},{3,2},{4,5},{5,4},{6,7},{7,6},{8,9},{9,8},{10,11... | collective-permute-start | bytes 3145736 | tf_op jit(solution)/shard_map/ppermute | solution.py:14
  78.8 12.6 %all-to-all-start.2 = ((f32[16,2,4,128]{3,2,1,0:T(4,128)}), f32[16,2,4,128]{3,2,1,0:T(4,128)S(1)}, u32[]{:S(2)}, u32[]{:S(2)}) async-start(f32[16,2,4,128]{3,2,1,0:T(4,128)} %broadcast_in_dim.32), calls=%async_computation.2 | async-start | bytes 131072 | tf_op jit(solution)/shard_map/all_to_all | solution.py:27
  95.7 10.2 %collective-permute-start.15 = (bf16[4,288,128]{2,1,0:T(8,128)(2,1)}, bf16[4,288,128]{2,1,0:T(8,128)(2,1)}, u32[]{:S(2)}, u32[]{:S(2)}) collective-permute-start(bf16[4,288,128]{2,1,0:T(8,128)(2,1)} %get-tuple-element.94), channel_id=1, source_target_pairs={{0,64},{64,0},{128,192},{192,128},{1,65},{65,1},{129,193},{193,129... | collective-permute-start | bytes 884744 | tf_op jit(solution)/shard_map/ppermute | solution.py:14
  96.3 9.6 %collective-permute-start.16 = (bf16[288,512]{1,0:T(8,128)(2,1)S(1)}, bf16[288,512]{1,0:T(8,128)(2,1)}, u32[]{:S(2)}, u32[]{:S(2)}) collective-permute-start(bf16[288,512]{1,0:T(8,128)(2,1)S(1)} %get-tuple-element.95), channel_id=1, source_target_pairs={{0,16},{16,0},{32,48},{48,32},{1,17},{17,1},{33,49},{49,33},{2,18}... | collective-permute-start | bytes 884744 | tf_op jit(solution)/shard_map/ppermute | solution.py:14
  108.0 7.3 %collective-permute-start.17 = (bf16[4,288,128]{2,1,0:T(8,128)(2,1)S(1)}, bf16[4,288,128]{2,1,0:T(8,128)(2,1)S(1)}, u32[]{:S(2)}, u32[]{:S(2)}) collective-permute-start(bf16[4,288,128]{2,1,0:T(8,128)(2,1)S(1)} %convert_element_type.73), channel_id=1, source_target_pairs={{0,64},{64,0},{128,192},{192,128},{1,65},{65,1},{129,193},{193,129... | collective-permute-start | bytes 884744 | tf_op jit(solution)/shard_map/ppermute | solution.py:14
  109.6 6.8 %collective-permute-start.18 = (bf16[288,512]{1,0:T(8,128)(2,1)S(1)}, bf16[288,512]{1,0:T(8,128)(2,1)S(1)}, u32[]{:S(2)}, u32[]{:S(2)}) collective-permute-start(bf16[288,512]{1,0:T(8,128)(2,1)S(1)} %convert_element_type.74), channel_id=1, source_target_pairs={{0,16},{16,0},{32,48},{48,32},{1,17},{17,1},{33,49},{49,33},{2,18}... | collective-permute-start | bytes 884744 | tf_op jit(solution)/shard_map/ppermute | solution.py:14
  110.2 7.9 %collective-permute-start.19 = (bf16[4,288,128]{2,1,0:T(8,128)(2,1)S(1)}, bf16[4,288,128]{2,1,0:T(8,128)(2,1)S(1)}, u32[]{:S(2)}, u32[]{:S(2)}) collective-permute-start(bf16[4,288,128]{2,1,0:T(8,128)(2,1)S(1)} %add_convert_fusion.1), channel_id=1, source_target_pairs={{0,192},{64,128},{128,64},{192,0},{1,193},{65,129},{129,65},{193,1... | collective-permute-start | bytes 884744 | tf_op jit(solution)/shard_map/ppermute | solution.py:14
  111.3 6.8 %collective-permute-start.20 = (bf16[288,512]{1,0:T(8,128)(2,1)S(1)}, bf16[288,512]{1,0:T(8,128)(2,1)S(1)}, u32[]{:S(2)}, u32[]{:S(2)}) collective-permute-start(bf16[288,512]{1,0:T(8,128)(2,1)S(1)} %add_convert_fusion), channel_id=1, source_target_pairs={{0,48},{16,32},{32,16},{48,0},{1,49},{17,33},{33,17},{49,1},{2,50}... | collective-permute-start | bytes 884744 | tf_op jit(solution)/shard_map/ppermute | solution.py:14
  118.4 5.8 %collective-permute-start.21 = (bf16[2,288,128]{2,1,0:T(8,128)(2,1)S(1)}, bf16[2,288,128]{2,1,0:T(8,128)(2,1)S(1)}, u32[]{:S(2)}, u32[]{:S(2)}) collective-permute-start(bf16[2,288,128]{2,1,0:T(8,128)(2,1)S(1)} %slice.158), channel_id=1, source_target_pairs={{0,16},{16,0},{32,48},{48,32},{1,17},{17,1},{33,49},{49,33},{2,18}... | collective-permute-start | bytes 442376 | tf_op jit(solution)/shard_map/ppermute | solution.py:14
  121.1 5.1 %collective-permute-start.22 = (bf16[288,256]{1,0:T(8,128)(2,1)S(1)}, bf16[288,256]{1,0:T(8,128)(2,1)S(1)}, u32[]{:S(2)}, u32[]{:S(2)}) collective-permute-start(bf16[288,256]{1,0:T(8,128)(2,1)S(1)} %slice.157), channel_id=1, source_target_pairs={{0,64},{64,0},{128,192},{192,128},{1,65},{65,1},{129,193},{193,129... | collective-permute-start | bytes 442376 | tf_op jit(solution)/shard_map/ppermute | solution.py:14
  126.3 4.4 %collective-permute-start.23 = (bf16[288,128]{1,0:T(8,128)(2,1)S(1)}, bf16[288,128]{1,0:T(8,128)(2,1)S(1)}, u32[]{:S(2)}, u32[]{:S(2)}) collective-permute-start(bf16[288,128]{1,0:T(8,128)(2,1)S(1)} %fusion.6), channel_id=1, source_target_pairs={{0,48},{16,32},{32,16},{48,0},{1,49},{17,33},{33,17},{49,1},{2,50}... | collective-permute-start | bytes 221192 | tf_op jit(solution)/shard_map/ppermute | solution.py:14
  127.0 5.6 %collective-permute-start.24 = (bf16[288,128]{1,0:T(8,128)(2,1)S(1)}, bf16[288,128]{1,0:T(8,128)(2,1)S(1)}, u32[]{:S(2)}, u32[]{:S(2)}) collective-permute-start(bf16[288,128]{1,0:T(8,128)(2,1)S(1)} %fusion.1), channel_id=1, source_target_pairs={{0,192},{64,128},{128,64},{192,0},{1,193},{65,129},{129,65},{193,1... | collective-permute-start | bytes 221192 | tf_op jit(solution)/shard_map/ppermute | solution.py:14
  132.6 1.5 collective-permute-start.25
  134.9 16.5 %all-to-all-start.3 = ((f32[8,72,128]{2,1,0:T(8,128)}), f32[8,72,128]{2,1,0:T(8,128)S(1)}, u32[]{:S(2)}, u32[]{:S(2)}) async-start(f32[8,72,128]{2,1,0:T(8,128)} %pad_maximum_fusion.3), calls=%async_computation.3 | async-start | bytes 589824 | tf_op jit(solution)/shard_map/all_to_all | solution.py:391
